TPU v7x, 128 devices: a whole 4x4x4 slice. The times are simulated.
128 devices in a mesh: band: 4 (over y_hi, core), ga: 32 (over z, x, y_lo).
Axes of the slice: x: 4, y: 4 (y_hi: 2, y_lo: 2; y = y_hi * 2 + y_lo), z: 4, core: 2. Of those that a mesh axis runs over, the one named last changes fastest.
Arguments:
- orbitals: bfloat16 [2, 2048, 24576], P(None, 'band', 'ga'), may hold values from -0.078125 to 0.078125
- h_orbitals: bfloat16 [2, 2048, 24576], P(None, 'band', 'ga'), may hold values from -4.1875 to 4.1875
- rotation: bfloat16 [2, 2048, 2048], P(None, 'ga', 'band'), may hold values from -0.09375 to 0.09375
Outputs:
- rotated_psi: float32 [2, 2048, 24576], P(None, 'band', 'ga')
- rotated_hpsi: float32 [2, 2048, 24576], P(None, 'band', 'ga')
- subspace_h: float32 [2, 2048, 2048], P(None, 'ga', 'band')
- correlation_s: float32 [2, 2048, 2048], P(None, 'ga', 'band')
All inputs are finite; a program needn't handle non-finite values.
Results may differ from a plain program's by a relative error of at most 0.0003.
Values may be sent and summed in bfloat16 or wider, within the bound.
No kernel may reach another device: no remote copies, remote signals or barrier semaphores. Data moves between devices by JAX's collectives and lax.ppermute only.
A program may use at most 128 MiB of HBM per device.

v0:
```python
import jax
import jax.numpy as jnp
from jax import lax
from jax.sharding import PartitionSpec as P

NBLK = 32


def gram_terms(left_rows, right_rows):
    contract = (((1,), (1,)), ((), ()))

    def product(first_op, second_op):
        return lax.dot_general(first_op, second_op, contract, preferred_element_type=jnp.float32)

    real_part = product(left_rows[0], right_rows[0]) + product(left_rows[1], right_rows[1])
    imag_part = product(left_rows[0], right_rows[1]) - product(left_rows[1], right_rows[0])
    return jnp.concatenate([real_part, imag_part], axis=1)


def rotate(coefficient, operand):
    contract = (((0,), (0,)), ((), ()))

    def product(first_op, second_op):
        return lax.dot_general(first_op, second_op, contract, preferred_element_type=jnp.float32)

    real_part = product(coefficient[0], operand[0]) - product(coefficient[1], operand[1])
    imag_part = product(coefficient[0], operand[1]) + product(coefficient[1], operand[0])
    return (real_part, imag_part)


def to_storage(values, procs, blocksize):
    total_rows = values.shape[1]
    columns = values.shape[2]
    shaped = values.reshape(2, total_rows // (blocksize * procs), procs, blocksize, columns)
    return jnp.transpose(shaped, (0, 2, 1, 3, 4)).reshape(2, total_rows, columns)


def shards(orbitals, h_orbitals, rotation):
    band_count = lax.axis_size("band")
    ga_count = lax.axis_size("ga")
    local_bands = orbitals.shape[1]
    local_coeffs = orbitals.shape[2]
    local_rows = rotation.shape[1]
    blocksize = NBLK
    psi_all, hpsi_all = (
        lax.all_gather(orbitals, "band", axis=1, tiled=True),
        lax.all_gather(h_orbitals, "band", axis=1, tiled=True),
    )
    stacked = jnp.concatenate([psi_all, hpsi_all], axis=2)
    stored = to_storage(stacked, ga_count, blocksize)
    left_all = stored[:, :, :local_coeffs]
    left_rows = left_all
    h_part = lax.psum_scatter(
        gram_terms(left_rows, h_orbitals), "ga", scatter_dimension=0, tiled=True
    )
    left_rows = left_all
    s_part = lax.psum_scatter(
        gram_terms(left_rows, orbitals), "ga", scatter_dimension=0, tiled=True
    )
    partial_sums = jnp.concatenate([h_part, s_part], axis=1)
    partial_sums = partial_sums.reshape(local_rows, 4, local_bands)
    groups = local_bands // (blocksize * band_count)
    shaped = partial_sums.reshape(local_rows, 4, groups, band_count, blocksize)
    shaped = lax.all_to_all(shaped, "band", split_axis=3, concat_axis=2, tiled=True)
    partial_sums = shaped.reshape(local_rows, 4, local_bands)
    matrices = jnp.moveaxis(partial_sums, 1, 0)
    subspace_h = matrices[0:2]
    correlation_s = matrices[2:4]
    coefficient = rotation.reshape(2, local_rows, band_count, groups, 1, blocksize)
    coefficient = lax.all_to_all(coefficient, "band", split_axis=2, concat_axis=4, tiled=True)
    coefficient = coefficient.reshape(2, local_rows, local_bands)
    coeff_all = lax.all_gather(coefficient, "ga", axis=1, tiled=True)
    real_part, imag_part = rotate(coeff_all, stored)
    rotated = jnp.stack([real_part, imag_part])
    return (rotated[:, :, :local_coeffs], rotated[:, :, local_coeffs:], subspace_h, correlation_s)


def solution(mesh):
    placed = (P(None, "band", "ga"), P(None, "band", "ga"), P(None, "ga", "band"))
    return jax.shard_map(
        shards,
        mesh=mesh,
        in_specs=placed,
        out_specs=(
            P(None, "band", "ga"),
            P(None, "band", "ga"),
            P(None, "ga", "band"),
            P(None, "ga", "band"),
        ),
        check_vma=False,
    )
```

profile of v0, /device:TPU:0, one launch (start us, length us, event | category | flops | bytes accessed | tf_op | source)
XLA Modules:
  0.0 692.3 jit_solution(15522695721894609690)
XLA Ops:
  7.2 0.0 all-gather.4.cloned.1.call-start
  7.2 0.7 all-gather.4.cloned.1.call-update
  7.9 0.0 all-gather.6.cloned.1.call-start
  7.9 0.7 all-gather.6.cloned.1.call-update
  8.6 0.0 all-gather.8.cloned.1.call-start
  8.7 1.1 copy.41
  9.8 0.2 reshape.38
  10.0 10.5 %all_to_all.30 = bf16[4,2,8192]{2,1,0:T(2,128)(2,1)S(1)} all-to-all(bf16[4,2,8192]{2,1,0:T(2,128)(2,1)S(1)} %reshape.38), channel_id=1, replica_groups=mesh['band'=4,'ga'=32] {'band'}, dimensions={0} | all-to-all | bytes 262144 | tf_op jit(solution)/shard_map/all_to_all | solution.py:70
  20.5 0.2 reshape.39
  20.8 0.8 copy.44
  21.6 0.0 all-gather.8.cloned.1.call-update
  21.6 0.0 reduce-scatter.7.cloned.1.call-start
  21.7 40.9 %all-gather.4.cloned.1.call-done = bf16[2,2048,768]{2,1,0:T(8,128)(2,1)} async-done(((bf16[2,512,768]{2,1,0:T(8,128)(2,1)}), bf16[2,2048,768]{2,1,0:T(8,128)(2,1)}) %all-gather.4.cloned.1.call-update) | async-done | bytes 6291472 | tf_op jit(solution)/shard_map/all_gather | solution.py:46
  62.6 51.5 %all-gather.6.cloned.1.call-done = bf16[2,2048,768]{2,1,0:T(8,128)(2,1)} async-done(((bf16[2,512,768]{2,1,0:T(8,128)(2,1)}), bf16[2,2048,768]{2,1,0:T(8,128)(2,1)}) %all-gather.6.cloned.1.call-update) | async-done | bytes 6291472 | tf_op jit(solution)/shard_map/all_gather | solution.py:47
  114.1 6.0 pad_maximum_fusion
  120.2 0.0 copy-start.2
  120.2 2.0 copy.48
  122.2 2.7 copy-done
  125.0 1.8 fusion.6
  126.8 1.8 fusion.5
  128.6 1.8 convolution_add_fusion.2
  130.4 1.8 convolution_subtract_fusion.2
  132.3 3.8 pad_maximum_fusion.1
  136.1 9.3 %copy.55 = f32[2048,1024]{1,0:T(8,128)} copy(f32[2048,1024]{0,1:T(8,128)} %pad_maximum_fusion.1) | data formatting | bytes 16777216
  145.4 0.0 reduce-scatter.7.cloned.1.call-update
  145.4 0.2 reduce-scatter.9.cloned.1.call-start
  145.7 1.2 copy-done.3
  146.8 3.9 fusion.4
  150.7 3.9 fusion.3
  154.6 1.8 convolution_add_fusion.1
  156.4 1.8 convolution_subtract_fusion.1
  158.3 3.8 pad_maximum_fusion.2
  162.1 9.2 %copy.57 = f32[2048,1024]{1,0:T(8,128)} copy(f32[2048,1024]{0,1:T(8,128)} %pad_maximum_fusion.2) | data formatting | bytes 16777216
  171.3 0.0 reduce-scatter.9.cloned.1.call-update
  171.4 102.8 %all-gather.8.cloned.1.call-done = bf16[2,2048,512]{2,0,1:T(2,128)(2,1)} async-done(((bf16[2,64,512]{2,0,1:T(2,128)(2,1)}), bf16[2,2048,512]{2,0,1:T(2,128)(2,1)}) %all-gather.8.cloned.1.call-update) | async-done | bytes 4194320 | tf_op jit(solution)/shard_map/all_gather | solution.py:72
  274.2 10.2 %fusion.26 = (bf16[1,2048,512]{2,0,1:T(2,128)(2,1)}, bf16[1,2048,512]{2,0,1:T(2,128)(2,1)}) fusion(bf16[2,2048,512]{2,0,1:T(2,128)(2,1)} %all-gather.8.cloned.1.call-done), kind=kLoop, calls=%fused_computation.43 | loop fusion | bytes 8388608 | tf_op jit(solution)/shard_map/slice | solution.py:26
  284.4 5.6 fusion.25
  290.0 0.7 copy.40
  290.8 0.7 copy.46
  291.5 2.0 copy-done.4
  293.5 7.1 %fusion.8 = f32[1536,512]{1,0:T(8,128)S(1)} fusion(bf16[2048,1536]{1,0:T(8,128)(2,1)S(1)} %bitcast.96, bf16[1,2048,512]{2,0,1:T(2,128)(2,1)} %get-tuple-element.29), kind=kOutput, calls=%fused_computation.25 | convolution fusion | flops 3221225472 | bytes 11534336 | tf_op jit(solution)/shard_map/dot_general | solution.py:24
  300.7 5.1 fusion.7
  305.8 5.3 fusion.1
  311.0 154.8 %reduce-scatter.7.cloned.1.call-done = f32[64,1024]{1,0:T(8,128)} async-done(((f32[2048,1024]{1,0:T(8,128)}), f32[64,1024]{1,0:T(8,128)}) %reduce-scatter.7.cloned.1.call-update) | async-done | bytes 262160
  465.9 1.1 copy.56
  467.0 187.9 %reduce-scatter.9.cloned.1.call-done = f32[64,1024]{1,0:T(8,128)} async-done(((f32[2048,1024]{1,0:T(8,128)}), f32[64,1024]{1,0:T(8,128)}) %reduce-scatter.9.cloned.1.call-update) | async-done | bytes 262160
  654.9 1.1 copy.58
  656.0 0.1 pad_maximum_fusion.4
  656.1 0.1 copy.69
  656.2 1.4 reshape.40
  657.7 5.0 all-to-all-start.1
  662.7 8.6 %fusion = f32[1,512,1536]{1,2,0:T(8,128)S(1)} fusion(f32[1536,512]{1,0:T(8,128)} %fusion.7, bf16[2048,1536]{1,0:T(8,128)(2,1)} %bitcast.97, bf16[1,2048,512]{2,0,1:T(2,128)(2,1)} %get-tuple-element.28), kind=kOutput, calls=%fused_computation.6 | convolution fusion | flops 3222011904 | bytes 14680064 | tf_op jit(solution)/shard_map/dot_general | solution.py:24
  671.3 2.4 pad_maximum_fusion.3
  673.7 3.5 copy.51
  677.2 2.4 copy.52
  679.6 0.0 all-to-all-done.1
  679.6 0.5 broadcast
  680.1 3.1 reduce
  683.2 0.5 reshape.41
  683.7 0.1 bitcast_bitcast_fusion
  683.8 0.1 copy.50
  683.9 0.1 fusion.27
  684.0 0.9 copy.53
  684.9 0.9 copy.54
  (22 shorter events, 0.1 us)
Async XLA Ops:
  7.2 55.4 %all-gather.4.cloned.1.call-start = ((), (), s32[]{:S(2)}) async-start(), calls=%async_computation.4 | async-start | bytes 7864320 | tf_op jit(solution)/shard_map/all_gather | solution.py:46
  7.9 106.2 %all-gather.6.cloned.1.call-start = ((), (), s32[]{:S(2)}) async-start(), calls=%async_computation.5 | async-start | bytes 7864320 | tf_op jit(solution)/shard_map/all_gather | solution.py:47
  8.6 265.6 %all-gather.8.cloned.1.call-start = ((), (), s32[]{:S(2)}) async-start(), calls=%async_computation.6 | async-start | bytes 4325376 | tf_op jit(solution)/shard_map/all_gather | solution.py:72
  21.6 444.2 %reduce-scatter.7.cloned.1.call-start = ((), (), s32[]{:S(2)}) async-start(), calls=%async_computation.7 | async-start | bytes 8650752
  120.2 4.8 copy-start
  120.2 4.8 copy-start.2
  125.0 5.5 copy-start.1
  145.4 1.4 copy-start.3
  145.4 509.5 %reduce-scatter.9.cloned.1.call-start = ((), (), s32[]{:S(2)}) async-start(), calls=%async_computation.8 | async-start | bytes 8650752
  146.8 7.8 %slice-start = ((s8[12582912]{0:T(1024)(128)(4,1)}), s8[4194304]{0:T(1024)(128)(4,1)S(1)}, s32[]{:S(2)}) async-start(s8[12582912]{0:T(1024)(128)(4,1)} %bitcast.92), calls=%async_computation.9 | async-start | bytes 8388608
  146.8 7.8 %slice-start.1 = ((s8[12582912]{0:T(1024)(128)(4,1)}), s8[4194304]{0:T(1024)(128)(4,1)S(1)}, s32[]{:S(2)}) async-start(s8[12582912]{0:T(1024)(128)(4,1)} %bitcast.92), calls=%async_computation.10 | async-start | bytes 8388608
  150.7 3.9 slice-start.2
  290.8 2.7 copy-start.4
  293.5 7.2 %copy-start.6 = (bf16[1,2048,512]{2,0,1:T(2,128)(2,1)S(1)}, bf16[1,2048,512]{2,0,1:T(2,128)(2,1)}, u32[]{:S(2)}) copy-start(bf16[1,2048,512]{2,0,1:T(2,128)(2,1)} %get-tuple-element.29) | copy-start | bytes 6291460
  300.6 5.1 copy-start.5
  657.7 21.9 %all-to-all-start.1 = ((f32[4,1,32768]{2,1,0:T(1,128)}), f32[4,1,32768]{2,1,0:T(1,128)}, u32[]{:S(2)}, u32[]{:S(2)}) async-start(f32[4,1,32768]{2,1,0:T(1,128)} %reshape.40), calls=%async_computation.1 | async-start | bytes 1048576 | tf_op jit(solution)/shard_map/all_to_all | solution.py:64
  662.7 8.6 %copy-start.7 = (f32[1,512,1536]{1,2,0:T(8,128)S(1)}, f32[1,512,1536]{1,2,0:T(8,128)}, u32[]{:S(2)}) copy-start(f32[1,512,1536]{1,2,0:T(8,128)} %fusion.1) | copy-start | bytes 9437188
Sparse Core Ops, SparseCore 0:
  9.7 52.8 all-gather.3
  64.3 49.8 all-gather.5
  116.4 157.7 all-gather.7
  276.5 189.3 reduce-scatter.6
  468.1 186.7 reduce-scatter.8
where the time goes:
time: 694 us; the launch traced here: 692 us
  waiting for transfers between devices  539 us (78%)
  local copies, waits for them, and re-layouts  58.9 us (8%)
  matrix products  44.8 us (6%)
  other arithmetic  19.2 us (3%)
  between operations  14.1 us (2%)
  blocking collectives  10.5 us (2%)
    unnamed x7, waiting for transfers between devices  344 us
    all_gather x1, waiting for transfers between devices, shards(): coeff_all = lax.all_gather(coefficient, 'ga', axis=1, tiled=True)  103 us
    all_gather x1, waiting for transfers between devices, shards(): lax.all_gather(h_orbitals, 'band', axis=1, tiled=True)  51.5 us
    dot_general x12, matrix products, product(): lax.dot_general(first_op, second_op, contract, preferred_element_type=jnp...  44.8 us
    all_gather x1, waiting for transfers between devices, shards(): lax.all_gather(orbitals, 'band', axis=1, tiled=True)  40.9 us
    unnamed x35, local copies, waits for them, and re-layouts  37.9 us
  transfers between devices with their start and end apart: 6, of which 5 were waited for; matrix products, arithmetic and copies ran while one was open for 16% of the time, Pallas kernels for 0%

commit v1 on v0

v1 whole, which is shorter than its diff:
```python
import jax
import jax.numpy as jnp
from jax import lax
from jax.sharding import PartitionSpec as P

NBLK = 32
H_SCALE = 64.0
S_SCALE = 4096.0


def place(device):
    band, ga = divmod(device, 32)
    y_hi, core = divmod(band, 2)
    z, rest = divmod(ga, 8)
    x, y_lo = divmod(rest, 2)
    return [z, x, y_lo, y_hi, core]


def device_at(z, x, y_lo, y_hi, core):
    return (y_hi * 2 + core) * 32 + z * 8 + x * 2 + y_lo


def move(value, dz=0, dx=0, y_lo=0, y_hi=0, core=0):
    pairs = []
    for source in range(128):
        z, x, low, high, c = place(source)
        target = device_at((z + dz) % 4, (x + dx) % 4, low ^ y_lo, high ^ y_hi, c ^ core)
        pairs.append((source, target))
    return lax.ppermute(value, ("band", "ga"), pairs)


def pick(stacked, index):
    return lax.dynamic_index_in_dim(stacked, index, 0, keepdims=False)


def dot_rows(left, right):
    return lax.dot_general(left, right, (((1,), (1,)), ((), ())), preferred_element_type=jnp.float32)


def planes_side_by_side(block):
    return jnp.concatenate([block[0], block[1]], axis=1)


def shards(psi, hpsi, rot):
    band = lax.axis_index("band")
    ga = lax.axis_index("ga")
    y_hi, core = band // 2, band % 2
    mz, mx, y_lo = ga // 8, (ga // 2) % 4, ga % 2

    psi_mate = move(psi, core=1)
    psi_cross = move(psi, y_hi=1)
    hpsi_mate = move(hpsi, core=1)
    hpsi_cross = move(hpsi, y_hi=1)
    psi_cross_mate = move(psi_cross, core=1)
    hpsi_cross_mate = move(hpsi_cross, core=1)

    chunks = rot.reshape(2, 64, 4, 128)

    def chunk_for(k):
        return lax.dynamic_index_in_dim(chunks, band ^ k, 2, keepdims=False)

    arrived = jnp.stack([
        chunk_for(0),
        move(chunk_for(1), core=1),
        move(chunk_for(2), y_hi=1),
        move(chunk_for(3), core=1, y_hi=1),
    ])
    by_band = jnp.stack([pick(arrived, b ^ band) for b in range(4)])
    other = move(by_band, y_lo=1)
    pair = jnp.stack([by_band, other])
    pair = jnp.stack([pick(pair, y_lo), pick(pair, 1 - y_lo)])
    xs = jnp.stack([pair, move(pair, dx=-1), move(pair, dx=2), move(pair, dx=1)])
    xs = jnp.stack([pick(xs, (n - mx) % 4) for n in range(4)])
    xs = xs.reshape(4, 2, 4, 2, 2, 32, 128)
    mine = jnp.transpose(xs, (3, 4, 2, 6, 0, 1, 5)).reshape(2, 2, 512, 256)
    up = move(mine, dz=-1)
    down = move(mine, dz=1)
    far = jnp.stack([move(down[0], dz=1), move(up[1], dz=-1)])
    zs = jnp.stack([mine, up, far, down])

    def right_rows(block):
        rows = block.reshape(2, 4, 4, 32, 768).swapaxes(1, 2).reshape(2, 512, 768)
        return rows[0], rows[1]

    h_r, h_i = right_rows(hpsi * jnp.bfloat16(H_SCALE))
    p_r, p_i = right_rows(psi * jnp.bfloat16(S_SCALE))
    right_x = jnp.concatenate([
        jnp.concatenate([h_r, h_i], axis=1),
        jnp.concatenate([h_i, -h_r], axis=1),
        jnp.concatenate([p_r, p_i], axis=1),
    ], axis=0)
    right_z = jnp.concatenate([p_i, -p_r], axis=1)

    def z_slot(z):
        return ((z // 2) ^ core) * 2 + z % 2

    def reduced(first, second):
        left = jnp.concatenate([planes_side_by_side(first), planes_side_by_side(second)], axis=0)
        by_x = left.reshape(4, 4, 64, 1536)
        by_z = left.reshape(4, 256, 1536)

        def left_for_x(d):
            return lax.dynamic_index_in_dim(by_x, (mx + d) % 4, 1, keepdims=False).reshape(256, 1536)

        def left_for_z(d):
            return pick(by_z, z_slot((mz + d) % 4))

        def part_x(d):
            return dot_rows(left_for_x(d), right_x).astype(jnp.float16)

        def part_z(d):
            return dot_rows(left_for_z(d), right_z).astype(jnp.float16)

        got_x = [move(part_x(d), dx=d) for d in (1, 3, 2)]
        got_z = [move(part_z(d), dz=d) for d in (1, 3, 2)]
        sum_x = dot_rows(left_for_x(0), right_x)
        for g in got_x:
            sum_x = sum_x + g.astype(jnp.float32)
        sum_z = dot_rows(left_for_z(0), right_z)
        for g in got_z:
            sum_z = sum_z + g.astype(jnp.float32)
        sum_x = sum_x.reshape(4, 64, 1536)
        sum_z = sum_z.reshape(4, 64, 512)
        total_x = pick(sum_x, z_slot(mz))
        for d in (1, 3, 2):
            total_x = total_x + move(pick(sum_x, z_slot((mz + d) % 4)), dz=d)
        total_z = pick(sum_z, mx)
        for d in (1, 3, 2):
            total_z = total_z + move(pick(sum_z, (mx + d) % 4), dx=d)
        total = jnp.concatenate([total_x, total_z], axis=1).reshape(2, 32, 2048)
        return pick(total, y_lo) + move(pick(total, 1 - y_lo), y_lo=1)

    near = reduced(psi, psi_mate)
    away = reduced(psi_cross, psi_cross_mate)
    halves = jnp.stack([near, away])
    halves = jnp.stack([pick(halves, y_hi), pick(halves, 1 - y_hi)])
    halves = halves.reshape(2, 32, 4, 4, 128)

    def columns_for(k):
        return lax.dynamic_index_in_dim(halves, band ^ k, 3, keepdims=False)

    cols = jnp.stack([
        columns_for(0),
        move(columns_for(1), core=1),
        move(columns_for(2), y_hi=1),
        move(columns_for(3), core=1, y_hi=1),
    ])
    cols = jnp.stack([pick(cols, q ^ band) for q in range(4)])
    mats = jnp.transpose(cols, (3, 1, 2, 0, 4)).reshape(4, 64, 512)
    subspace_h = mats[0:2] * jnp.float32(1.0 / H_SCALE)
    correlation_s = mats[2:4] * jnp.float32(1.0 / S_SCALE)

    def weights(h, c):
        parts = [pick(pick(zs, (2 * c + n - mz) % 4).swapaxes(0, 1), h) for n in range(2)]
        a = jnp.concatenate(parts, axis=2)
        a = a.reshape(2, 4, 4, 32, 512).swapaxes(1, 2).reshape(2, 512, 512)
        return jnp.concatenate([
            jnp.concatenate([a[0], -a[1]], axis=1),
            jnp.concatenate([a[1], a[0]], axis=1),
        ], axis=0)

    w = [weights(y_hi, core), weights(y_hi, 1 - core), weights(1 - y_hi, core), weights(1 - y_hi, 1 - core)]

    def rotate(blocks):
        out = None
        for weight, block in zip(w, blocks):
            term = jnp.dot(weight, block.reshape(1024, 768), preferred_element_type=jnp.float32)
            out = term if out is None else out + term
        return out.reshape(2, 512, 768)

    rotated_psi = rotate([psi, psi_mate, psi_cross, psi_cross_mate])
    rotated_hpsi = rotate([hpsi, hpsi_mate, hpsi_cross, hpsi_cross_mate])
    return rotated_psi, rotated_hpsi, subspace_h, correlation_s


def solution(mesh):
    placed = (P(None, "band", "ga"), P(None, "band", "ga"), P(None, "ga", "band"))
    return jax.shard_map(
        shards,
        mesh=mesh,
        in_specs=placed,
        out_specs=(
            P(None, "band", "ga"),
            P(None, "band", "ga"),
            P(None, "ga", "band"),
            P(None, "ga", "band"),
        ),
        check_vma=False,
    )
```

time: 694 us -> 330 us (0.48)
  the two profiles are of different devices: /device:TPU:0 before, /device:TPU:1 now
where the time goes in v1:
time: 330 us; the launch traced here: 324 us
  waiting for transfers between devices  91.3 us (28%)
  starting transfers between devices  72.3 us (22%)
  matrix products  67.5 us (20%)
  other arithmetic  55.2 us (17%)
  local copies, waits for them, and re-layouts  35.6 us (11%)
    ppermute x46, waiting for transfers between devices, move(): return lax.ppermute(value, ('band', 'ga'), pairs)  91.3 us
    ppermute x46, starting transfers between devices, move(): return lax.ppermute(value, ('band', 'ga'), pairs)  72.3 us
    dot_general x8, matrix products, rotate(): jnp.dot(weight, block.reshape(1024, 768), preferred_element_type=jnp.floa...  46.1 us
    concatenate x2, other arithmetic, reduced(): jnp.concatenate([planes_side_by_side(first), planes_side_by_side(second)]...  26 us
    dot_general x16, matrix products, dot_rows(): lax.dot_general(left, right, (((1,), (1,)), ((), ())), preferred_element_...  21.4 us
    concatenate x1, other arithmetic, shards(): jnp.concatenate([jnp.concatenate([h_r, h_i], axis=1), jnp.concatenate([h_...  17.3 us
    another operation x9, local copies, waits for them, and re-layouts  11 us
    squeeze x4, local copies, waits for them, and re-layouts, planes_side_by_side(): return jnp.concatenate([block[0], block[1]], axis=1)  6.85 us
  transfers between devices with their start and end apart: 46, of which 15 were waited for; matrix products, arithmetic and copies ran while one was open for 44% of the time, Pallas kernels for 0%

profile of v1, /device:TPU:1, one launch (start us, length us, event | category | flops | bytes accessed | tf_op | source)
XLA Modules:
  0.0 324.0 jit_solution(16911926505197885894)
XLA Ops:
  0.6 3.8 %collective-permute-start.12 = (bf16[2,512,768]{2,1,0:T(8,128)(2,1)}, bf16[2,512,768]{2,1,0:T(8,128)(2,1)}, u32[]{:S(2)}, u32[]{:S(2)}) collective-permute-start(bf16[2,512,768]{2,1,0:T(8,128)(2,1)} %param.3), channel_id=1, source_target_pairs={{0,64},{1,65},{2,66},{3,67},{4,68},{5,69},{6,70},{7,71},{8,72},{9,... | collective-permute-start | bytes 4718600 | tf_op jit(solution)/shard_map/ppermute | solution.py:29
  6.8 2.8 collective-permute-start.1
  10.4 2.7 slice_bitcast_fusion.7
  13.4 1.5 broadcast_multiply_fusion.1
  16.0 24.4 %collective-permute-done.2 = bf16[2,64,128]{2,1,0:T(8,128)(2,1)S(1)} collective-permute-done((bf16[2,64,128]{2,1,0:T(8,128)(2,1)S(1)}, bf16[2,64,128]{2,1,0:T(8,128)(2,1)S(1)}, u32[]{:S(2)}, u32[]{:S(2)}) %collective-permute-start.2) | collective-permute-done | bytes 32800 | tf_op jit(solution)/shard_map/ppermute | solution.py:29
  40.5 1.4 collective-permute-start.3
  46.6 2.5 collective-permute-start.5
  51.2 1.8 collective-permute-done.6
  53.0 6.6 %collective-permute-done.5 = bf16[2,4,2,64,128]{4,3,2,1,0:T(8,128)(2,1)S(1)} collective-permute-done((bf16[2,4,2,64,128]{4,3,2,1,0:T(8,128)(2,1)S(1)}, bf16[2,4,2,64,128]{4,3,2,1,0:T(8,128)(2,1)S(1)}, u32[]{:S(2)}, u32[]{:S(2)}) %collective-permute-start.5) | collective-permute-done | bytes 262176 | tf_op jit(solution)/shard_map/ppermute | solution.py:29
  62.1 1.6 collective-permute-start.8
  63.7 2.6 collective-permute-start.7
  66.3 17.3 %maximum_maximum_fusion = bf16[1536,1536]{1,0:T(8,128)(2,1)} fusion(bf16[512,768]{1,0:T(8,128)(2,1)S(1)} %bitcast.293, bf16[512,768]{1,0:T(8,128)(2,1)S(1)} %bitcast.280, bf16[512,768]{1,0:T(8,128)(2,1)} %bitcast_negate_fusion.1, bf16[512,768]{1,0:T(8,128)(2,1)} %bitcast.302, bf16[512,768]{1,0:T(8,128)(2,1)S(1)} %bitcast.281), kind=kLoop, calls=%fused_computation | loop fusion | flops 28311552 | bytes 8650752 | tf_op jit(solution)/shard_map/concatenate | solution.py:87
  84.0 2.9 collective-permute-done.7
  88.0 3.5 %collective-permute-start.10 = (bf16[2,512,256]{1,2,0:T(8,128)(2,1)S(1)}, bf16[2,512,256]{1,2,0:T(8,128)(2,1)S(1)}, u32[]{:S(2)}, u32[]{:S(2)}) collective-permute-start(bf16[2,512,256]{1,2,0:T(8,128)(2,1)S(1)} %slice_bitcast_fusion.8), channel_id=1, source_target_pairs={{0,24},{1,25},{2,26},{3,27},{4,28},{5,29},{6,30},{7,31},{8,0},{9,1... | collective-permute-start | bytes 1572872 | tf_op jit(solution)/shard_map/ppermute | solution.py:29
  92.6 1.5 slice_bitcast_fusion.5
  94.1 13.0 %maximum_maximum_fusion.1 = bf16[1024,1536]{1,0:T(8,128)(2,1)S(1)} fusion(bf16[512,768]{1,0:T(8,128)(2,1)S(1)} %get-tuple-element.37, bf16[512,768]{1,0:T(8,128)(2,1)S(1)} %get-tuple-element.36, bf16[512,768]{1,0:T(8,128)(2,1)S(1)} %copy-done.3, bf16[512,768]{1,0:T(8,128)(2,1)S(1)} %copy-done.2), kind=kLoop, calls=%fused_computation.2 | loop fusion | flops 12582912 | bytes 6291456 | tf_op jit(solution)/shard_map/concatenate | solution.py:98
  112.0 2.4 convolution_convert_fusion.3
  114.4 2.4 convolution_convert_fusion.4
  116.7 2.3 convolution_convert_fusion.5
  121.0 2.0 collective-permute-start.28
  123.0 5.4 %collective-permute-start.27 = (f32[64,512]{1,0:T(8,128)S(1)}, f32[64,512]{1,0:T(8,128)S(1)}, u32[]{:S(2)}, u32[]{:S(2)}) collective-permute-start(f32[64,512]{1,0:T(8,128)S(1)} %get-tuple-element.67), channel_id=1, source_target_pairs={{0,6},{1,7},{2,0},{3,1},{4,2},{5,3},{6,4},{7,5},{8,14},{9,15},{10,... | collective-permute-start | bytes 393224 | tf_op jit(solution)/shard_map/ppermute | solution.py:29
  128.4 2.6 slice_bitcast_fusion.3
  131.0 2.6 collective-permute-start.15
  133.6 2.8 collective-permute-start.14
  137.6 2.7 collective-permute-start.18
  140.4 1.8 pad_maximum_fusion
  142.2 1.4 constant_dynamic-slice_fusion.17
  143.6 2.0 copy.42
  145.7 2.0 copy.41
  150.8 2.0 copy.34
  162.1 3.2 fusion.37
  166.2 3.8 %collective-permute-start.13 = (bf16[2,512,768]{2,1,0:T(8,128)(2,1)}, bf16[2,512,768]{2,1,0:T(8,128)(2,1)S(1)}, u32[]{:S(2)}, u32[]{:S(2)}) collective-permute-start(bf16[2,512,768]{2,1,0:T(8,128)(2,1)} %collective-permute-done.12), channel_id=1, source_target_pairs={{0,32},{1,33},{2,34},{3,35},{4,36},{5,37},{6,38},{7,39},{8,40},{9,... | collective-permute-start | bytes 4718600 | tf_op jit(solution)/shard_map/ppermute | solution.py:29
  170.0 5.0 %fusion.36 = f32[1024,768]{1,0:T(8,128)} fusion(bf16[1024,768]{1,0:T(8,128)(2,1)} %bitcast.45, bf16[512,512]{1,0:T(8,128)(2,1)S(1)} %bitcast.336, bf16[512,512]{1,0:T(8,128)(2,1)S(1)} %bitcast.310, bf16[512,512]{1,0:T(8,128)(2,1)S(1)} %bitcast_negate_fusion.3), kind=kOutput, calls=%fused_computation.71 | convolution fusion | flops 1619001344 | bytes 6291456 | tf_op jit(solution)/shard_map/dot_general | solution.py:167
  175.0 1.8 fusion.41
  176.8 4.9 %fusion.40 = f32[1024,768]{1,0:T(8,128)} fusion(bf16[1024,768]{1,0:T(8,128)(2,1)} %bitcast.43, bf16[512,512]{1,0:T(8,128)(2,1)S(1)} %bitcast.340, bf16[512,512]{1,0:T(8,128)(2,1)S(1)} %bitcast.312, bf16[512,512]{1,0:T(8,128)(2,1)S(1)} %bitcast_negate_fusion.5), kind=kOutput, calls=%fused_computation.75 | convolution fusion | flops 1619001344 | bytes 6291456 | tf_op jit(solution)/shard_map/dot_general | solution.py:167
  182.1 3.3 %fusion.39 = f32[1024,768]{1,0:T(8,128)S(1)} fusion(bf16[1024,768]{1,0:T(8,128)(2,1)} %bitcast.29, bf16[512,512]{1,0:T(8,128)(2,1)S(1)} %bitcast.337, bf16[512,512]{1,0:T(8,128)(2,1)S(1)} %bitcast.307, bf16[512,512]{1,0:T(8,128)(2,1)S(1)} %bitcast_negate_fusion.4), kind=kOutput, calls=%fused_computation.74 | convolution fusion | flops 1619001344 | bytes 6291456 | tf_op jit(solution)/shard_map/dot_general | solution.py:167
  185.5 3.3 %convert_add_fusion.1 = f32[256,1536]{1,0:T(8,128)S(1)} fusion(f16[256,1536]{1,0:T(8,128)(2,1)} %collective-permute-done.19, f16[256,1536]{1,0:T(8,128)(2,1)} %collective-permute-done.18, f16[256,1536]{1,0:T(8,128)(2,1)} %collective-permute-done.17, bf16[256,1536]{1,0:T(8,128)(2,1)S(1)} %bitcast.327, bf16[1536,1536]{1,0:T(8,128)(2,1)S(1)} %bitcast.291), kind=kOutput, calls=%fused_computation.18 | convolution fusion | flops 1210318848 | bytes 9437184 | tf_op jit(solution)/shard_map/dot_general | solution.py:37
  189.2 2.0 collective-permute-start.21
  191.4 4.8 %fusion.38 = f32[1024,768]{1,0:T(8,128)} fusion(bf16[1024,768]{1,0:T(8,128)(2,1)} %bitcast.44, bf16[512,512]{1,0:T(8,128)(2,1)S(1)} %bitcast.338, bf16[512,512]{1,0:T(8,128)(2,1)S(1)} %bitcast.308, bf16[512,512]{1,0:T(8,128)(2,1)S(1)} %bitcast_negate_fusion.4), kind=kOutput, calls=%fused_computation.73 | convolution fusion | flops 1619001344 | bytes 6291456 | tf_op jit(solution)/shard_map/dot_general | solution.py:167
  196.3 5.0 %collective-permute-done.22 = f32[64,1536]{1,0:T(8,128)S(1)} collective-permute-done((f32[64,1536]{1,0:T(8,128)S(1)}, f32[64,1536]{1,0:T(8,128)S(1)}, u32[]{:S(2)}, u32[]{:S(2)}) %collective-permute-start.22) | collective-permute-done | bytes 393248 | tf_op jit(solution)/shard_map/ppermute | solution.py:29
  201.3 6.5 %collective-permute-done.21 = f32[64,1536]{1,0:T(8,128)S(1)} collective-permute-done((f32[64,1536]{1,0:T(8,128)S(1)}, f32[64,1536]{1,0:T(8,128)S(1)}, u32[]{:S(2)}, u32[]{:S(2)}) %collective-permute-start.21) | collective-permute-done | bytes 393248 | tf_op jit(solution)/shard_map/ppermute | solution.py:29
  207.8 2.2 collective-permute-done.20
  210.2 13.0 %maximum_maximum_fusion.2 = bf16[1024,1536]{1,0:T(8,128)(2,1)S(1)} fusion(bf16[512,768]{1,0:T(8,128)(2,1)S(1)} %get-tuple-element.26, bf16[512,768]{1,0:T(8,128)(2,1)S(1)} %get-tuple-element.25, bf16[512,768]{1,0:T(8,128)(2,1)S(1)} %copy-done.5, bf16[512,768]{1,0:T(8,128)(2,1)S(1)} %copy-done.4), kind=kLoop, calls=%fused_computation.3 | loop fusion | flops 12582912 | bytes 6291456 | tf_op jit(solution)/shard_map/concatenate | solution.py:98
  225.4 1.8 collective-permute-start.37
  227.4 1.4 convolution_convert_fusion
  228.8 2.2 collective-permute-start.32
  230.9 1.4 convolution_convert_fusion.1
  232.4 2.1 collective-permute-start.31
  234.5 1.4 convolution_convert_fusion.2
  236.1 1.8 collective-permute-done.37
  238.4 2.2 collective-permute-done.36
  241.3 1.9 collective-permute-start.41
  243.1 5.2 %collective-permute-done.32 = f16[256,1536]{1,0:T(8,128)(2,1)S(1)} collective-permute-done((f16[256,1536]{1,0:T(8,128)(2,1)S(1)}, f16[256,1536]{1,0:T(8,128)(2,1)S(1)}, u32[]{:S(2)}, u32[]{:S(2)}) %collective-permute-start.32) | collective-permute-done | bytes 786464 | tf_op jit(solution)/shard_map/ppermute | solution.py:29
  248.3 2.6 collective-permute-start.40
  250.9 16.5 %collective-permute-done.31 = f16[256,1536]{1,0:T(8,128)(2,1)S(1)} collective-permute-done((f16[256,1536]{1,0:T(8,128)(2,1)S(1)}, f16[256,1536]{1,0:T(8,128)(2,1)S(1)}, u32[]{:S(2)}, u32[]{:S(2)}) %collective-permute-start.31) | collective-permute-done | bytes 786464 | tf_op jit(solution)/shard_map/ppermute | solution.py:29
  267.4 2.5 collective-permute-start.39
  269.8 1.7 convert_add_fusion
  271.7 2.5 collective-permute-start.35
  275.7 1.8 collective-permute-start.16
  277.6 5.5 %collective-permute-done.35 = f32[64,1536]{1,0:T(8,128)S(1)} collective-permute-done((f32[64,1536]{1,0:T(8,128)S(1)}, f32[64,1536]{1,0:T(8,128)S(1)}, u32[]{:S(2)}, u32[]{:S(2)}) %collective-permute-start.35) | collective-permute-done | bytes 393248 | tf_op jit(solution)/shard_map/ppermute | solution.py:29
  283.1 8.9 %collective-permute-done.34 = f32[64,1536]{1,0:T(8,128)S(1)} collective-permute-done((f32[64,1536]{1,0:T(8,128)S(1)}, f32[64,1536]{1,0:T(8,128)S(1)}, u32[]{:S(2)}, u32[]{:S(2)}) %collective-permute-start.34) | collective-permute-done | bytes 393248 | tf_op jit(solution)/shard_map/ppermute | solution.py:29
  293.2 9.7 %add_add_fusion.1 = f32[1024,768]{1,0:T(8,128)} fusion(f32[1024,768]{1,0:T(8,128)S(1)} %fusion.37, f32[1024,768]{1,0:T(8,128)S(1)} %fusion.41, f32[1024,768]{1,0:T(8,128)S(1)} %fusion.39, bf16[1024,768]{1,0:T(8,128)(2,1)S(1)} %bitcast.285, bf16[512,512]{1,0:T(8,128)(2,1)S(1)} %bitcast.286, bf16[512,512]{1,0:T(8,128)(2,1)S(1)} %bitcast.278, ...), kind=kOutput, calls=%fused_computation.5 | convolution fusion | flops 1621360640 | bytes 15728640 | tf_op jit(solution)/shard_map/dot_general | solution.py:167
  304.0 3.4 %collective-permute-start.45 = (f32[2,32,4,128]{3,1,2,0:T(8,128)S(1)}, f32[2,32,4,128]{3,1,2,0:T(8,128)S(1)}, u32[]{:S(2)}, u32[]{:S(2)}) collective-permute-start(f32[2,32,4,128]{3,1,2,0:T(8,128)S(1)} %bitcast.351), channel_id=1, source_target_pairs={{0,96},{1,97},{2,98},{3,99},{4,100},{5,101},{6,102},{7,103},{8,104... | collective-permute-start | bytes 393224 | tf_op jit(solution)/shard_map/ppermute | solution.py:29
  308.0 13.3 %add_add_fusion = f32[1024,768]{1,0:T(8,128)} fusion(f32[1024,768]{1,0:T(8,128)} %fusion.36, f32[1024,768]{1,0:T(8,128)} %fusion.40, f32[1024,768]{1,0:T(8,128)} %fusion.38, bf16[1024,768]{1,0:T(8,128)(2,1)} %bitcast.46, bf16[512,512]{1,0:T(8,128)(2,1)S(1)} %bitcast.287, bf16[512,512]{1,0:T(8,128)(2,1)S(1)} %bitcast.279, ...), kind=kOutput, calls=%fused_computation.4 | convolution fusion | flops 1621360640 | bytes 15728640 | tf_op jit(solution)/shard_map/dot_general | solution.py:167
  (187 shorter events, 48.8 us)
Async XLA Ops:
  0.6 12.5 %copy-start = (bf16[2,512,768]{2,1,0:T(8,128)(2,1)S(1)}, bf16[2,512,768]{2,1,0:T(8,128)(2,1)}, u32[]{:S(2)}) copy-start(bf16[2,512,768]{2,1,0:T(8,128)(2,1)} %param.3) | copy-start | bytes 4718596
  0.6 127.7 %collective-permute-start.12 = (bf16[2,512,768]{2,1,0:T(8,128)(2,1)}, bf16[2,512,768]{2,1,0:T(8,128)(2,1)}, u32[]{:S(2)}, u32[]{:S(2)}) collective-permute-start(bf16[2,512,768]{2,1,0:T(8,128)(2,1)} %param.3), channel_id=1, source_target_pairs={{0,64},{1,65},{2,66},{3,67},{4,68},{5,69},{6,70},{7,71},{8,72},{9,... | collective-permute-start | bytes 4718600 | tf_op jit(solution)/shard_map/ppermute | solution.py:29
  4.5 88.1 %collective-permute-start.11 = (bf16[2,512,768]{2,1,0:T(8,128)(2,1)}, bf16[2,512,768]{2,1,0:T(8,128)(2,1)}, u32[]{:S(2)}, u32[]{:S(2)}) collective-permute-start(bf16[2,512,768]{2,1,0:T(8,128)(2,1)} %param.3), channel_id=1, source_target_pairs={{0,32},{1,33},{2,34},{3,35},{4,36},{5,37},{6,38},{7,39},{8,40},{9,... | collective-permute-start | bytes 4718600 | tf_op jit(solution)/shard_map/ppermute | solution.py:29
  6.7 33.8 %collective-permute-start.2 = (bf16[2,64,128]{2,1,0:T(8,128)(2,1)S(1)}, bf16[2,64,128]{2,1,0:T(8,128)(2,1)S(1)}, u32[]{:S(2)}, u32[]{:S(2)}) collective-permute-start(bf16[2,64,128]{2,1,0:T(8,128)(2,1)S(1)} %bitcast.359), channel_id=1, source_target_pairs={{0,96},{1,97},{2,98},{3,99},{4,100},{5,101},{6,102},{7,103},{8,104... | collective-permute-start | bytes 98312 | tf_op jit(solution)/shard_map/ppermute | solution.py:29
  6.8 33.7 %collective-permute-start.1 = (bf16[2,64,128]{2,1,0:T(8,128)(2,1)S(1)}, bf16[2,64,128]{2,1,0:T(8,128)(2,1)S(1)}, u32[]{:S(2)}, u32[]{:S(2)}) collective-permute-start(bf16[2,64,128]{2,1,0:T(8,128)(2,1)S(1)} %bitcast.360), channel_id=1, source_target_pairs={{0,64},{1,65},{2,66},{3,67},{4,68},{5,69},{6,70},{7,71},{8,72},{9,... | collective-permute-start | bytes 98312 | tf_op jit(solution)/shard_map/ppermute | solution.py:29
  9.6 30.8 %collective-permute-start = (bf16[2,64,128]{2,1,0:T(8,128)(2,1)S(1)}, bf16[2,64,128]{2,1,0:T(8,128)(2,1)S(1)}, u32[]{:S(2)}, u32[]{:S(2)}) collective-permute-start(bf16[2,64,128]{2,1,0:T(8,128)(2,1)S(1)} %bitcast.361), channel_id=1, source_target_pairs={{0,32},{1,33},{2,34},{3,35},{4,36},{5,37},{6,38},{7,39},{8,40},{9,... | collective-permute-start | bytes 98312 | tf_op jit(solution)/shard_map/ppermute | solution.py:29
  40.5 4.7 %collective-permute-start.3 = (bf16[4,2,64,128]{3,2,1,0:T(8,128)(2,1)S(1)}, bf16[4,2,64,128]{3,2,1,0:T(8,128)(2,1)S(1)}, u32[]{:S(2)}, u32[]{:S(2)}) collective-permute-start(bf16[4,2,64,128]{3,2,1,0:T(8,128)(2,1)S(1)} %get-tuple-element.72), channel_id=1, source_target_pairs={{0,1},{1,0},{2,3},{3,2},{4,5},{5,4},{6,7},{7,6},{8,9},{9,8},{10,11... | collective-permute-start | bytes 393224 | tf_op jit(solution)/shard_map/ppermute | solution.py:29
  45.3 7.7 %collective-permute-start.6 = (bf16[2,4,2,64,128]{4,3,2,1,0:T(8,128)(2,1)S(1)}, bf16[2,4,2,64,128]{4,3,2,1,0:T(8,128)(2,1)S(1)}, u32[]{:S(2)}, u32[]{:S(2)}) collective-permute-start(bf16[2,4,2,64,128]{4,3,2,1,0:T(8,128)(2,1)S(1)} %get-tuple-element.69), channel_id=1, source_target_pairs={{0,2},{1,3},{2,4},{3,5},{4,6},{5,7},{6,0},{7,1},{8,10},{9,11},{10,... | collective-permute-start | bytes 786440 | tf_op jit(solution)/shard_map/ppermute | solution.py:29
  46.6 13.0 %collective-permute-start.5 = (bf16[2,4,2,64,128]{4,3,2,1,0:T(8,128)(2,1)S(1)}, bf16[2,4,2,64,128]{4,3,2,1,0:T(8,128)(2,1)S(1)}, u32[]{:S(2)}, u32[]{:S(2)}) collective-permute-start(bf16[2,4,2,64,128]{4,3,2,1,0:T(8,128)(2,1)S(1)} %get-tuple-element.69), channel_id=1, source_target_pairs={{0,4},{1,5},{2,6},{3,7},{4,0},{5,1},{6,2},{7,3},{8,12},{9,13},{10,... | collective-permute-start | bytes 786440 | tf_op jit(solution)/shard_map/ppermute | solution.py:29
  49.1 10.6 %collective-permute-start.4 = (bf16[2,4,2,64,128]{4,3,2,1,0:T(8,128)(2,1)S(1)}, bf16[2,4,2,64,128]{4,3,2,1,0:T(8,128)(2,1)S(1)}, u32[]{:S(2)}, u32[]{:S(2)}) collective-permute-start(bf16[2,4,2,64,128]{4,3,2,1,0:T(8,128)(2,1)S(1)} %get-tuple-element.69), channel_id=1, source_target_pairs={{0,6},{1,7},{2,0},{3,1},{4,2},{5,3},{6,4},{7,5},{8,14},{9,15},{10,... | collective-permute-start | bytes 786440 | tf_op jit(solution)/shard_map/ppermute | solution.py:29
  62.1 29.4 %collective-permute-start.8 = (bf16[2,2,512,256]{2,3,1,0:T(8,128)(2,1)}, bf16[2,2,512,256]{2,3,1,0:T(8,128)(2,1)}, u32[]{:S(2)}, u32[]{:S(2)}) collective-permute-start(bf16[2,2,512,256]{2,3,1,0:T(8,128)(2,1)} %reshape.211), channel_id=1, source_target_pairs={{0,8},{1,9},{2,10},{3,11},{4,12},{5,13},{6,14},{7,15},{8,16},{9,17... | collective-permute-start | bytes 3145736 | tf_op jit(solution)/shard_map/ppermute | solution.py:29
  63.7 23.2 %collective-permute-start.7 = (bf16[2,2,512,256]{2,3,1,0:T(8,128)(2,1)}, bf16[2,2,512,256]{2,3,1,0:T(8,128)(2,1)}, u32[]{:S(2)}, u32[]{:S(2)}) collective-permute-start(bf16[2,2,512,256]{2,3,1,0:T(8,128)(2,1)} %reshape.211), channel_id=1, source_target_pairs={{0,24},{1,25},{2,26},{3,27},{4,28},{5,29},{6,30},{7,31},{8,0},{9,1... | collective-permute-start | bytes 3145736 | tf_op jit(solution)/shard_map/ppermute | solution.py:29
  84.0 10.0 %copy-start.2 = (bf16[512,768]{1,0:T(8,128)(2,1)S(1)}, bf16[512,768]{1,0:T(8,128)(2,1)}, u32[]{:S(2)}) copy-start(bf16[512,768]{1,0:T(8,128)(2,1)} %get-tuple-element.34) | copy-start | bytes 2359300
  84.0 10.0 %copy-start.3 = (bf16[512,768]{1,0:T(8,128)(2,1)S(1)}, bf16[512,768]{1,0:T(8,128)(2,1)}, u32[]{:S(2)}) copy-start(bf16[512,768]{1,0:T(8,128)(2,1)} %get-tuple-element.35) | copy-start | bytes 2359300
  88.0 49.6 %collective-permute-start.10 = (bf16[2,512,256]{1,2,0:T(8,128)(2,1)S(1)}, bf16[2,512,256]{1,2,0:T(8,128)(2,1)S(1)}, u32[]{:S(2)}, u32[]{:S(2)}) collective-permute-start(bf16[2,512,256]{1,2,0:T(8,128)(2,1)S(1)} %slice_bitcast_fusion.8), channel_id=1, source_target_pairs={{0,24},{1,25},{2,26},{3,27},{4,28},{5,29},{6,30},{7,31},{8,0},{9,1... | collective-permute-start | bytes 1572872 | tf_op jit(solution)/shard_map/ppermute | solution.py:29
  94.1 13.0 %copy-start.8 = (bf16[512,768]{1,0:T(8,128)(2,1)S(1)}, bf16[512,768]{1,0:T(8,128)(2,1)}, u32[]{:S(2)}) copy-start(bf16[512,768]{1,0:T(8,128)(2,1)} %bitcast_negate_fusion) | copy-start | bytes 2359300
  107.7 11.4 %collective-permute-start.25 = (f16[256,512]{1,0:T(8,128)(2,1)S(1)}, f16[256,512]{1,0:T(8,128)(2,1)S(1)}, u32[]{:S(2)}, u32[]{:S(2)}) collective-permute-start(f16[256,512]{1,0:T(8,128)(2,1)S(1)} %convolution_convert_fusion.9), channel_id=1, source_target_pairs={{0,16},{1,17},{2,18},{3,19},{4,20},{5,21},{6,22},{7,23},{8,24},{9,... | collective-permute-start | bytes 786440 | tf_op jit(solution)/shard_map/ppermute | solution.py:29
  107.8 4.2 %slice-start = ((s8[4718592]{0:T(1024)(128)(4,1)}), s8[4194304]{0:T(1024)(128)(4,1)S(1)}, s32[]{:S(2)}) async-start(s8[4718592]{0:T(1024)(128)(4,1)} %bitcast.288), calls=%async_computation | async-start | bytes 8388608
  108.4 3.5 %slice-start.1 = ((s8[4718592]{0:T(1024)(128)(4,1)}), s8[524288]{0:T(1024)(128)(4,1)S(1)}, s32[]{:S(2)}) async-start(s8[4718592]{0:T(1024)(128)(4,1)} %bitcast.288), calls=%async_computation.1 | async-start | bytes 1048576
  108.4 11.8 %collective-permute-start.24 = (f16[256,512]{1,0:T(8,128)(2,1)S(1)}, f16[256,512]{1,0:T(8,128)(2,1)S(1)}, u32[]{:S(2)}, u32[]{:S(2)}) collective-permute-start(f16[256,512]{1,0:T(8,128)(2,1)S(1)} %convolution_convert_fusion.10), channel_id=1, source_target_pairs={{0,24},{1,25},{2,26},{3,27},{4,28},{5,29},{6,30},{7,31},{8,0},{9,1... | collective-permute-start | bytes 786440 | tf_op jit(solution)/shard_map/ppermute | solution.py:29
  109.7 10.6 %collective-permute-start.23 = (f16[256,512]{1,0:T(8,128)(2,1)S(1)}, f16[256,512]{1,0:T(8,128)(2,1)S(1)}, u32[]{:S(2)}, u32[]{:S(2)}) collective-permute-start(f16[256,512]{1,0:T(8,128)(2,1)S(1)} %convolution_convert_fusion.11), channel_id=1, source_target_pairs={{0,8},{1,9},{2,10},{3,11},{4,12},{5,13},{6,14},{7,15},{8,16},{9,17... | collective-permute-start | bytes 786440 | tf_op jit(solution)/shard_map/ppermute | solution.py:29
  119.1 21.2 %collective-permute-start.9 = (bf16[2,512,256]{1,2,0:T(8,128)(2,1)S(1)}, bf16[2,512,256]{1,2,0:T(8,128)(2,1)S(1)}, u32[]{:S(2)}, u32[]{:S(2)}) collective-permute-start(bf16[2,512,256]{1,2,0:T(8,128)(2,1)S(1)} %slice_bitcast_fusion.9), channel_id=1, source_target_pairs={{0,8},{1,9},{2,10},{3,11},{4,12},{5,13},{6,14},{7,15},{8,16},{9,17... | collective-permute-start | bytes 1572872 | tf_op jit(solution)/shard_map/ppermute | solution.py:29
  121.0 10.0 %collective-permute-start.28 = (f32[64,512]{1,0:T(8,128)S(1)}, f32[64,512]{1,0:T(8,128)S(1)}, u32[]{:S(2)}, u32[]{:S(2)}) collective-permute-start(f32[64,512]{1,0:T(8,128)S(1)} %get-tuple-element.66), channel_id=1, source_target_pairs={{0,4},{1,5},{2,6},{3,7},{4,0},{5,1},{6,2},{7,3},{8,12},{9,13},{10,... | collective-permute-start | bytes 393224 | tf_op jit(solution)/shard_map/ppermute | solution.py:29
  123.0 10.6 %collective-permute-start.27 = (f32[64,512]{1,0:T(8,128)S(1)}, f32[64,512]{1,0:T(8,128)S(1)}, u32[]{:S(2)}, u32[]{:S(2)}) collective-permute-start(f32[64,512]{1,0:T(8,128)S(1)} %get-tuple-element.67), channel_id=1, source_target_pairs={{0,6},{1,7},{2,0},{3,1},{4,2},{5,3},{6,4},{7,5},{8,14},{9,15},{10,... | collective-permute-start | bytes 393224 | tf_op jit(solution)/shard_map/ppermute | solution.py:29
  128.4 8.0 %collective-permute-start.26 = (f32[64,512]{1,0:T(8,128)S(1)}, f32[64,512]{1,0:T(8,128)S(1)}, u32[]{:S(2)}, u32[]{:S(2)}) collective-permute-start(f32[64,512]{1,0:T(8,128)S(1)} %get-tuple-element.65), channel_id=1, source_target_pairs={{0,2},{1,3},{2,4},{3,5},{4,6},{5,7},{6,0},{7,1},{8,10},{9,11},{10,... | collective-permute-start | bytes 393224 | tf_op jit(solution)/shard_map/ppermute | solution.py:29
  131.0 35.3 %collective-permute-start.15 = (bf16[2,512,768]{2,1,0:T(8,128)(2,1)}, bf16[2,512,768]{2,1,0:T(8,128)(2,1)}, u32[]{:S(2)}, u32[]{:S(2)}) collective-permute-start(bf16[2,512,768]{2,1,0:T(8,128)(2,1)} %param.4), channel_id=1, source_target_pairs={{0,64},{1,65},{2,66},{3,67},{4,68},{5,69},{6,70},{7,71},{8,72},{9,... | collective-permute-start | bytes 4718600 | tf_op jit(solution)/shard_map/ppermute | solution.py:29
  133.6 57.8 %collective-permute-start.14 = (bf16[2,512,768]{2,1,0:T(8,128)(2,1)}, bf16[2,512,768]{2,1,0:T(8,128)(2,1)}, u32[]{:S(2)}, u32[]{:S(2)}) collective-permute-start(bf16[2,512,768]{2,1,0:T(8,128)(2,1)} %param.4), channel_id=1, source_target_pairs={{0,32},{1,33},{2,34},{3,35},{4,36},{5,37},{6,38},{7,39},{8,40},{9,... | collective-permute-start | bytes 4718600 | tf_op jit(solution)/shard_map/ppermute | solution.py:29
  136.4 49.1 %collective-permute-start.19 = (f16[256,1536]{1,0:T(8,128)(2,1)}, f16[256,1536]{1,0:T(8,128)(2,1)}, u32[]{:S(2)}, u32[]{:S(2)}) collective-permute-start(f16[256,1536]{1,0:T(8,128)(2,1)} %convolution_convert_fusion.3), channel_id=1, source_target_pairs={{0,4},{1,5},{2,6},{3,7},{4,0},{5,1},{6,2},{7,3},{8,12},{9,13},{10,... | collective-permute-start | bytes 2359304 | tf_op jit(solution)/shard_map/ppermute | solution.py:29
  137.6 47.9 %collective-permute-start.18 = (f16[256,1536]{1,0:T(8,128)(2,1)}, f16[256,1536]{1,0:T(8,128)(2,1)}, u32[]{:S(2)}, u32[]{:S(2)}) collective-permute-start(f16[256,1536]{1,0:T(8,128)(2,1)} %convolution_convert_fusion.4), channel_id=1, source_target_pairs={{0,6},{1,7},{2,0},{3,1},{4,2},{5,3},{6,4},{7,5},{8,14},{9,15},{10,... | collective-permute-start | bytes 2359304 | tf_op jit(solution)/shard_map/ppermute | solution.py:29
  140.3 45.2 %collective-permute-start.17 = (f16[256,1536]{1,0:T(8,128)(2,1)}, f16[256,1536]{1,0:T(8,128)(2,1)}, u32[]{:S(2)}, u32[]{:S(2)}) collective-permute-start(f16[256,1536]{1,0:T(8,128)(2,1)} %convolution_convert_fusion.5), channel_id=1, source_target_pairs={{0,2},{1,3},{2,4},{3,5},{4,6},{5,7},{6,0},{7,1},{8,10},{9,11},{10,... | collective-permute-start | bytes 2359304 | tf_op jit(solution)/shard_map/ppermute | solution.py:29
  159.3 2.5 copy-start.6
  160.6 1.5 copy-start.11
  166.2 43.9 %collective-permute-start.13 = (bf16[2,512,768]{2,1,0:T(8,128)(2,1)}, bf16[2,512,768]{2,1,0:T(8,128)(2,1)S(1)}, u32[]{:S(2)}, u32[]{:S(2)}) collective-permute-start(bf16[2,512,768]{2,1,0:T(8,128)(2,1)} %collective-permute-done.12), channel_id=1, source_target_pairs={{0,32},{1,33},{2,34},{3,35},{4,36},{5,37},{6,38},{7,39},{8,40},{9,... | collective-permute-start | bytes 4718600 | tf_op jit(solution)/shard_map/ppermute | solution.py:29
  170.0 5.0 %copy-start.1 = (bf16[2,512,768]{2,1,0:T(8,128)(2,1)S(1)}, bf16[2,512,768]{2,1,0:T(8,128)(2,1)}, u32[]{:S(2)}) copy-start(bf16[2,512,768]{2,1,0:T(8,128)(2,1)} %param.3) | copy-start | bytes 4718596
  170.0 5.0 %copy-start.12 = (bf16[1,4,4,32,512]{4,3,2,1,0:T(8,128)(2,1)S(1)}, bf16[1,4,4,32,512]{4,3,2,1,0:T(8,128)(2,1)}, u32[]{:S(2)}) copy-start(bf16[1,4,4,32,512]{4,3,2,1,0:T(8,128)(2,1)} %copy.35) | copy-start | bytes 1572868
  176.8 5.0 %copy-start.7 = (bf16[1,4,4,32,512]{4,3,1,2,0:T(8,128)(2,1)S(1)}, bf16[1,4,4,32,512]{4,3,1,2,0:T(8,128)(2,1)}, u32[]{:S(2)}) copy-start(bf16[1,4,4,32,512]{4,3,1,2,0:T(8,128)(2,1)} %get-tuple-element.41) | copy-start | bytes 1572868
  181.9 3.6 %slice-start.2 = ((s8[4718592]{0:T(1024)(128)(4,1)}), s8[4194304]{0:T(1024)(128)(4,1)S(1)}, s32[]{:S(2)}) async-start(s8[4718592]{0:T(1024)(128)(4,1)} %bitcast.290), calls=%async_computation.2 | async-start | bytes 8388608
  182.1 3.4 %slice-start.3 = ((s8[4718592]{0:T(1024)(128)(4,1)}), s8[524288]{0:T(1024)(128)(4,1)S(1)}, s32[]{:S(2)}) async-start(s8[4718592]{0:T(1024)(128)(4,1)} %bitcast.290), calls=%async_computation.3 | async-start | bytes 1048576
  182.1 3.4 %copy-start.10 = (bf16[4,1,64,1536]{3,2,1,0:T(8,128)(2,1)S(1)}, bf16[4,1,64,1536]{3,2,1,0:T(8,128)(2,1)}, u32[]{:S(2)}) copy-start(bf16[4,1,64,1536]{3,2,1,0:T(8,128)(2,1)} %get-tuple-element.19) | copy-start | bytes 2359300
  189.0 12.3 %collective-permute-start.22 = (f32[64,1536]{1,0:T(8,128)S(1)}, f32[64,1536]{1,0:T(8,128)S(1)}, u32[]{:S(2)}, u32[]{:S(2)}) collective-permute-start(f32[64,1536]{1,0:T(8,128)S(1)} %get-tuple-element.28), channel_id=1, source_target_pairs={{0,16},{1,17},{2,18},{3,19},{4,20},{5,21},{6,22},{7,23},{8,24},{9,... | collective-permute-start | bytes 1179656 | tf_op jit(solution)/shard_map/ppermute | solution.py:29
  189.2 18.6 %collective-permute-start.21 = (f32[64,1536]{1,0:T(8,128)S(1)}, f32[64,1536]{1,0:T(8,128)S(1)}, u32[]{:S(2)}, u32[]{:S(2)}) collective-permute-start(f32[64,1536]{1,0:T(8,128)S(1)} %get-tuple-element.29), channel_id=1, source_target_pairs={{0,24},{1,25},{2,26},{3,27},{4,28},{5,29},{6,30},{7,31},{8,0},{9,1... | collective-permute-start | bytes 1179656 | tf_op jit(solution)/shard_map/ppermute | solution.py:29
  191.3 18.8 %collective-permute-start.20 = (f32[64,1536]{1,0:T(8,128)S(1)}, f32[64,1536]{1,0:T(8,128)S(1)}, u32[]{:S(2)}, u32[]{:S(2)}) collective-permute-start(f32[64,1536]{1,0:T(8,128)S(1)} %get-tuple-element.27), channel_id=1, source_target_pairs={{0,8},{1,9},{2,10},{3,11},{4,12},{5,13},{6,14},{7,15},{8,16},{9,17... | collective-permute-start | bytes 1179656 | tf_op jit(solution)/shard_map/ppermute | solution.py:29
  196.3 14.0 %copy-start.4 = (bf16[512,768]{1,0:T(8,128)(2,1)S(1)}, bf16[512,768]{1,0:T(8,128)(2,1)}, u32[]{:S(2)}) copy-start(bf16[512,768]{1,0:T(8,128)(2,1)} %get-tuple-element.23) | copy-start | bytes 2359300
  196.3 14.0 %copy-start.5 = (bf16[512,768]{1,0:T(8,128)(2,1)S(1)}, bf16[512,768]{1,0:T(8,128)(2,1)}, u32[]{:S(2)}) copy-start(bf16[512,768]{1,0:T(8,128)(2,1)} %get-tuple-element.24) | copy-start | bytes 2359300
  210.2 13.0 %copy-start.9 = (bf16[512,768]{1,0:T(8,128)(2,1)S(1)}, bf16[512,768]{1,0:T(8,128)(2,1)}, u32[]{:S(2)}) copy-start(bf16[512,768]{1,0:T(8,128)(2,1)} %bitcast_negate_fusion) | copy-start | bytes 2359300
  225.1 10.8 %collective-permute-start.38 = (f16[256,512]{1,0:T(8,128)(2,1)S(1)}, f16[256,512]{1,0:T(8,128)(2,1)S(1)}, u32[]{:S(2)}, u32[]{:S(2)}) collective-permute-start(f16[256,512]{1,0:T(8,128)(2,1)S(1)} %convolution_convert_fusion.6), channel_id=1, source_target_pairs={{0,16},{1,17},{2,18},{3,19},{4,20},{5,21},{6,22},{7,23},{8,24},{9,... | collective-permute-start | bytes 786440 | tf_op jit(solution)/shard_map/ppermute | solution.py:29
  225.4 12.5 %collective-permute-start.37 = (f16[256,512]{1,0:T(8,128)(2,1)S(1)}, f16[256,512]{1,0:T(8,128)(2,1)S(1)}, u32[]{:S(2)}, u32[]{:S(2)}) collective-permute-start(f16[256,512]{1,0:T(8,128)(2,1)S(1)} %convolution_convert_fusion.7), channel_id=1, source_target_pairs={{0,24},{1,25},{2,26},{3,27},{4,28},{5,29},{6,30},{7,31},{8,0},{9,1... | collective-permute-start | bytes 786440 | tf_op jit(solution)/shard_map/ppermute | solution.py:29
  227.1 13.4 %collective-permute-start.36 = (f16[256,512]{1,0:T(8,128)(2,1)S(1)}, f16[256,512]{1,0:T(8,128)(2,1)S(1)}, u32[]{:S(2)}, u32[]{:S(2)}) collective-permute-start(f16[256,512]{1,0:T(8,128)(2,1)S(1)} %convolution_convert_fusion.8), channel_id=1, source_target_pairs={{0,8},{1,9},{2,10},{3,11},{4,12},{5,13},{6,14},{7,15},{8,16},{9,17... | collective-permute-start | bytes 786440 | tf_op jit(solution)/shard_map/ppermute | solution.py:29
  228.8 19.5 %collective-permute-start.32 = (f16[256,1536]{1,0:T(8,128)(2,1)S(1)}, f16[256,1536]{1,0:T(8,128)(2,1)S(1)}, u32[]{:S(2)}, u32[]{:S(2)}) collective-permute-start(f16[256,1536]{1,0:T(8,128)(2,1)S(1)} %convolution_convert_fusion), channel_id=1, source_target_pairs={{0,4},{1,5},{2,6},{3,7},{4,0},{5,1},{6,2},{7,3},{8,12},{9,13},{10,... | collective-permute-start | bytes 2359304 | tf_op jit(solution)/shard_map/ppermute | solution.py:29
  232.4 35.0 %collective-permute-start.31 = (f16[256,1536]{1,0:T(8,128)(2,1)S(1)}, f16[256,1536]{1,0:T(8,128)(2,1)S(1)}, u32[]{:S(2)}, u32[]{:S(2)}) collective-permute-start(f16[256,1536]{1,0:T(8,128)(2,1)S(1)} %convolution_convert_fusion.1), channel_id=1, source_target_pairs={{0,6},{1,7},{2,0},{3,1},{4,2},{5,3},{6,4},{7,5},{8,14},{9,15},{10,... | collective-permute-start | bytes 2359304 | tf_op jit(solution)/shard_map/ppermute | solution.py:29
  236.0 33.9 %collective-permute-start.30 = (f16[256,1536]{1,0:T(8,128)(2,1)S(1)}, f16[256,1536]{1,0:T(8,128)(2,1)S(1)}, u32[]{:S(2)}, u32[]{:S(2)}) collective-permute-start(f16[256,1536]{1,0:T(8,128)(2,1)S(1)} %convolution_convert_fusion.2), channel_id=1, source_target_pairs={{0,2},{1,3},{2,4},{3,5},{4,6},{5,7},{6,0},{7,1},{8,10},{9,11},{10,... | collective-permute-start | bytes 2359304 | tf_op jit(solution)/shard_map/ppermute | solution.py:29
  237.9 36.3 %collective-permute-start.29 = (f32[32,2048]{1,0:T(8,128)S(1)}, f32[32,2048]{1,0:T(8,128)S(1)}, u32[]{:S(2)}, u32[]{:S(2)}) collective-permute-start(f32[32,2048]{1,0:T(8,128)S(1)} %dynamic-slice_bitcast_fusion.7), channel_id=1, source_target_pairs={{0,1},{1,0},{2,3},{3,2},{4,5},{5,4},{6,7},{7,6},{8,9},{9,8},{10,11... | collective-permute-start | bytes 786440 | tf_op jit(solution)/shard_map/ppermute | solution.py:29
  241.3 33.5 %collective-permute-start.41 = (f32[64,512]{1,0:T(8,128)S(1)}, f32[64,512]{1,0:T(8,128)S(1)}, u32[]{:S(2)}, u32[]{:S(2)}) collective-permute-start(f32[64,512]{1,0:T(8,128)S(1)} %get-tuple-element.63), channel_id=1, source_target_pairs={{0,4},{1,5},{2,6},{3,7},{4,0},{5,1},{6,2},{7,3},{8,12},{9,13},{10,... | collective-permute-start | bytes 393224 | tf_op jit(solution)/shard_map/ppermute | solution.py:29
  248.3 27.4 %collective-permute-start.40 = (f32[64,512]{1,0:T(8,128)S(1)}, f32[64,512]{1,0:T(8,128)S(1)}, u32[]{:S(2)}, u32[]{:S(2)}) collective-permute-start(f32[64,512]{1,0:T(8,128)S(1)} %get-tuple-element.64), channel_id=1, source_target_pairs={{0,6},{1,7},{2,0},{3,1},{4,2},{5,3},{6,4},{7,5},{8,14},{9,15},{10,... | collective-permute-start | bytes 393224 | tf_op jit(solution)/shard_map/ppermute | solution.py:29
  267.4 10.1 %collective-permute-start.39 = (f32[64,512]{1,0:T(8,128)S(1)}, f32[64,512]{1,0:T(8,128)S(1)}, u32[]{:S(2)}, u32[]{:S(2)}) collective-permute-start(f32[64,512]{1,0:T(8,128)S(1)} %get-tuple-element.62), channel_id=1, source_target_pairs={{0,2},{1,3},{2,4},{3,5},{4,6},{5,7},{6,0},{7,1},{8,10},{9,11},{10,... | collective-permute-start | bytes 393224 | tf_op jit(solution)/shard_map/ppermute | solution.py:29
  271.7 11.4 %collective-permute-start.35 = (f32[64,1536]{1,0:T(8,128)S(1)}, f32[64,1536]{1,0:T(8,128)S(1)}, u32[]{:S(2)}, u32[]{:S(2)}) collective-permute-start(f32[64,1536]{1,0:T(8,128)S(1)} %get-tuple-element.21), channel_id=1, source_target_pairs={{0,16},{1,17},{2,18},{3,19},{4,20},{5,21},{6,22},{7,23},{8,24},{9,... | collective-permute-start | bytes 1179656 | tf_op jit(solution)/shard_map/ppermute | solution.py:29
  274.2 17.8 %collective-permute-start.34 = (f32[64,1536]{1,0:T(8,128)S(1)}, f32[64,1536]{1,0:T(8,128)S(1)}, u32[]{:S(2)}, u32[]{:S(2)}) collective-permute-start(f32[64,1536]{1,0:T(8,128)S(1)} %get-tuple-element.22), channel_id=1, source_target_pairs={{0,24},{1,25},{2,26},{3,27},{4,28},{5,29},{6,30},{7,31},{8,0},{9,1... | collective-permute-start | bytes 1179656 | tf_op jit(solution)/shard_map/ppermute | solution.py:29
  274.8 17.9 %collective-permute-start.33 = (f32[64,1536]{1,0:T(8,128)S(1)}, f32[64,1536]{1,0:T(8,128)S(1)}, u32[]{:S(2)}, u32[]{:S(2)}) collective-permute-start(f32[64,1536]{1,0:T(8,128)S(1)} %get-tuple-element.20), channel_id=1, source_target_pairs={{0,8},{1,9},{2,10},{3,11},{4,12},{5,13},{6,14},{7,15},{8,16},{9,17... | collective-permute-start | bytes 1179656 | tf_op jit(solution)/shard_map/ppermute | solution.py:29
  275.7 32.3 %collective-permute-start.16 = (bf16[2,512,768]{2,1,0:T(8,128)(2,1)}, bf16[2,512,768]{2,1,0:T(8,128)(2,1)}, u32[]{:S(2)}, u32[]{:S(2)}) collective-permute-start(bf16[2,512,768]{2,1,0:T(8,128)(2,1)} %collective-permute-done.15), channel_id=1, source_target_pairs={{0,32},{1,33},{2,34},{3,35},{4,36},{5,37},{6,38},{7,39},{8,40},{9,... | collective-permute-start | bytes 4718600 | tf_op jit(solution)/shard_map/ppermute | solution.py:29
  292.9 10.0 %collective-permute-start.42 = (f32[32,2048]{1,0:T(8,128)S(1)}, f32[32,2048]{1,0:T(8,128)S(1)}, u32[]{:S(2)}, u32[]{:S(2)}) collective-permute-start(f32[32,2048]{1,0:T(8,128)S(1)} %dynamic-slice_bitcast_fusion.6), channel_id=1, source_target_pairs={{0,1},{1,0},{2,3},{3,2},{4,5},{5,4},{6,7},{7,6},{8,9},{9,8},{10,11... | collective-permute-start | bytes 786440 | tf_op jit(solution)/shard_map/ppermute | solution.py:29
  304.0 17.4 %collective-permute-start.45 = (f32[2,32,4,128]{3,1,2,0:T(8,128)S(1)}, f32[2,32,4,128]{3,1,2,0:T(8,128)S(1)}, u32[]{:S(2)}, u32[]{:S(2)}) collective-permute-start(f32[2,32,4,128]{3,1,2,0:T(8,128)S(1)} %bitcast.351), channel_id=1, source_target_pairs={{0,96},{1,97},{2,98},{3,99},{4,100},{5,101},{6,102},{7,103},{8,104... | collective-permute-start | bytes 393224 | tf_op jit(solution)/shard_map/ppermute | solution.py:29
  307.4 13.9 %collective-permute-start.44 = (f32[2,32,4,128]{3,1,2,0:T(8,128)S(1)}, f32[2,32,4,128]{3,1,2,0:T(8,128)S(1)}, u32[]{:S(2)}, u32[]{:S(2)}) collective-permute-start(f32[2,32,4,128]{3,1,2,0:T(8,128)S(1)} %bitcast.352), channel_id=1, source_target_pairs={{0,64},{1,65},{2,66},{3,67},{4,68},{5,69},{6,70},{7,71},{8,72},{9,... | collective-permute-start | bytes 393224 | tf_op jit(solution)/shard_map/ppermute | solution.py:29
  307.8 13.5 %collective-permute-start.43 = (f32[2,32,4,128]{3,1,2,0:T(8,128)S(1)}, f32[2,32,4,128]{3,1,2,0:T(8,128)S(1)}, u32[]{:S(2)}, u32[]{:S(2)}) collective-permute-start(f32[2,32,4,128]{3,1,2,0:T(8,128)S(1)} %bitcast.353), channel_id=1, source_target_pairs={{0,32},{1,33},{2,34},{3,35},{4,36},{5,37},{6,38},{7,39},{8,40},{9,... | collective-permute-start | bytes 393224 | tf_op jit(solution)/shard_map/ppermute | solution.py:29

commit v2 on v0

v2 whole, which is shorter than its diff:
```python
import functools

import jax
import jax.numpy as jnp
from jax import lax
from jax.experimental import pallas as pl
from jax.experimental.pallas import tpu as pltpu
from jax.sharding import PartitionSpec as P

H_SCALE = 64.0
S_SCALE = 4096.0
MIB = 1024 * 1024
VMEM = pl.BlockSpec(memory_space=pltpu.VMEM)
SMEM = pl.BlockSpec(memory_space=pltpu.SMEM)


def place(device):
    band, ga = divmod(device, 32)
    y_hi, core = divmod(band, 2)
    z, rest = divmod(ga, 8)
    x, y_lo = divmod(rest, 2)
    return [z, x, y_lo, y_hi, core]


def device_at(z, x, y_lo, y_hi, core):
    return (y_hi * 2 + core) * 32 + z * 8 + x * 2 + y_lo


def move(value, dz=0, dx=0, y_lo=0, y_hi=0, core=0):
    pairs = []
    for source in range(128):
        z, x, low, high, c = place(source)
        target = device_at((z + dz) % 4, (x + dx) % 4, low ^ y_lo, high ^ y_hi, c ^ core)
        pairs.append((source, target))
    return lax.ppermute(value, ("band", "ga"), pairs)


def dot_rows(left, right):
    return lax.dot_general(left, right, (((1,), (1,)), ((), ())), preferred_element_type=jnp.float32)


def where_am_i(at):
    return at[0], at[1], at[2], at[3], at[4]


def call(kernel, outs, *args, limit=24, flops=0, **kw):
    moved = sum(a.size * a.dtype.itemsize for a in args)
    moved += sum(o.size * o.dtype.itemsize for o in jax.tree.leaves(outs))
    return pl.pallas_call(
        kernel,
        out_shape=outs,
        compiler_params=pltpu.CompilerParams(vmem_limit_bytes=limit * MIB),
        cost_estimate=pl.CostEstimate(flops=flops, bytes_accessed=moved, transcendentals=0),
        **kw,
    )(*args)


def split_kernel(at, own, other, first, second, third, fourth):
    mz, mx, y_lo, y_hi, core = where_am_i(at)
    for k, out in enumerate((first, second, third, fourth)):
        band = (y_hi * 2 + core) ^ k
        cols = pl.ds(pl.multiple_of(band * 128, 128), 128)
        out[y_lo] = own[:, :, cols]
        out[1 - y_lo] = other[:, :, cols]


def turn_kernel(at, first, second, third, fourth, out):
    mz, mx, y_lo, y_hi, core = where_am_i(at)
    for k, src in enumerate((first, second, third, fourth)):
        band = (y_hi * 2 + core) ^ k
        rows = jnp.concatenate(
            [src[low, c, h * 32:h * 32 + 32, :] for h in range(2) for c in range(2) for low in range(2)], axis=0)
        turned = rows.astype(jnp.float32).T.astype(jnp.bfloat16)
        for g in range(4):
            out[pl.ds(pl.multiple_of(g * 128 + band * 32, 32), 32), :] = turned[g * 32:g * 32 + 32, :]


def right_kernel(at, psi, psi_mate, hpsi, hpsi_mate, out):
    mz, mx, y_lo, y_hi, core = where_am_i(at)
    for half in range(2):
        band = (y_hi ^ half) * 2 + core
        for m, pair in enumerate(((hpsi, hpsi_mate), (psi, psi_mate))):
            for c, src in enumerate(pair):
                for g in range(4):
                    rows = pl.ds(pl.multiple_of(g * 128 + band * 32, 32), 32)
                    re, im = src[0, rows, :], src[1, rows, :]
                    base = half * 1024 + m * 512 + c * 128 + g * 32
                    out[base:base + 32, 0:768] = re
                    out[base:base + 32, 768:1536] = im
                    out[base + 256:base + 288, 0:768] = im
                    out[base + 256:base + 288, 768:1536] = -re


def left_kernel(x_first, at, near, other, *outs):
    mz, mx, y_lo, y_hi, core = where_am_i(at)
    for dz in range(4):
        z = (mz + dz) & 3
        is_near = (z >> 1) == core
        for dx in range(4):
            x = (mx + dx) & 3
            out = outs[dx] if x_first else outs[dz]
            for dy in range(2):
                base = (dz if x_first else dx) * 64 + dy * 32
                rows = pl.ds(pl.multiple_of((z & 1) * 256 + x * 64 + (y_lo ^ dy) * 32, 32), 32)
                for c in range(2):
                    value = jnp.where(is_near, near[c, rows, :], other[c, rows, :])
                    out[base:base + 32, c * 768:c * 768 + 768] = value


def rotate_kernel(pairs, has_acc, at, coef, *refs):
    mz, mx, y_lo, y_hi, core = where_am_i(at)
    blocks = refs[:2 * pairs]
    acc = refs[2 * pairs] if has_acc else None
    out, left, right_re, right_im = refs[-4:]

    @pl.when(pl.program_id(0) == 0)
    def _():
        for n in range(pairs):
            h = y_hi if (n == 0 and not has_acc) else 1 - y_hi
            for zx in range(16):
                left[:, n * 2048 + zx * 128:n * 2048 + zx * 128 + 128] = coef[
                    zx * 512:zx * 512 + 512, pl.ds(pl.multiple_of(h * 128, 128), 128)]

    for n in range(pairs):
        near, other = blocks[2 * n], blocks[2 * n + 1]
        for z in range(4):
            is_near = (z >> 1) == core
            for x in range(4):
                src = (z & 1) * 256 + x * 64
                base = n * 2048 + (z * 4 + x) * 128
                re = jnp.where(is_near, near[0, src:src + 64, :], other[0, src:src + 64, :])
                im = jnp.where(is_near, near[1, src:src + 64, :], other[1, src:src + 64, :])
                right_re[base:base + 64, :] = re
                right_re[base + 64:base + 128, :] = -im
                right_im[base:base + 64, :] = im
                right_im[base + 64:base + 128, :] = re
    for part, right in enumerate((right_re, right_im)):
        value = jnp.dot(left[...], right[...], preferred_element_type=jnp.float32)
        if has_acc:
            value = value + acc[part]
        out[part] = value


def rotate(at, coef, blocks, acc=None):
    pairs = len(blocks) // 2
    depth = 2048 * pairs
    tile = pl.BlockSpec((2, 512, 256), lambda n: (0, 0, n))
    whole = pl.BlockSpec((8192, 256), lambda n: (0, 0))
    args = [at, coef, *blocks] + ([acc] if acc is not None else [])
    return call(
        functools.partial(rotate_kernel, pairs, acc is not None),
        jax.ShapeDtypeStruct((2, 512, 768), jnp.float32),
        *args,
        limit=44,
        flops=2 * 1024 * depth * 768,
        grid=(3,),
        in_specs=[SMEM, whole] + [tile] * (len(args) - 2),
        out_specs=tile,
        scratch_shapes=[
            pltpu.VMEM((512, depth), jnp.bfloat16),
            pltpu.VMEM((depth, 256), jnp.bfloat16),
            pltpu.VMEM((depth, 256), jnp.bfloat16),
        ],
    )


def final_kernel(at, near, away, near_got, away_got, h_out, s_out):
    mz, mx, y_lo, y_hi, core = where_am_i(at)
    pieces = ((near, y_hi, y_hi), (away, 1 - y_hi, y_hi), (near_got, 1 - y_hi, 1 - y_hi), (away_got, y_hi, 1 - y_hi))
    for src, h, col_half in pieces:
        rows = pl.ds(pl.multiple_of(h * 32, 32), 32)
        for m in range(4):
            out, scale = (h_out, 1.0 / H_SCALE) if m < 2 else (s_out, 1.0 / S_SCALE)
            for c in range(2):
                cols = pl.ds(pl.multiple_of((col_half * 2 + (core ^ c)) * 128, 128), 128)
                out[m % 2, rows, cols] = src[:, m * 256 + c * 128:m * 256 + c * 128 + 128] * scale


def shards(psi, hpsi, rot):
    band = lax.axis_index("band")
    ga = lax.axis_index("ga")
    y_hi, core = band >> 1, band & 1
    mz, mx, y_lo = ga >> 3, (ga >> 1) & 3, ga & 1
    at = jnp.stack([mz, mx, y_lo, y_hi, core]).astype(jnp.int32)

    rot_other = move(rot, y_lo=1)
    psi_cross = move(psi, y_hi=1)
    psi_mate = move(psi, core=1)
    hpsi_mate = move(hpsi, core=1)
    hpsi_cross = move(hpsi, y_hi=1)

    sent = call(split_kernel, [jax.ShapeDtypeStruct((2, 2, 64, 128), jnp.bfloat16)] * 4, at, rot, rot_other,
                in_specs=[SMEM, VMEM, VMEM], out_specs=[VMEM] * 4)
    got = [sent[0], move(sent[1], core=1), move(sent[2], y_hi=1), move(sent[3], core=1, y_hi=1)]
    turned = call(turn_kernel, jax.ShapeDtypeStruct((512, 256), jnp.bfloat16), at, *got,
                  in_specs=[SMEM] + [VMEM] * 4, out_specs=VMEM)
    groups = [[z * 8 + x * 2 + low for z in range(4) for x in range(4)] for low in range(2)]
    coef = lax.all_gather(turned, "ga", axis=0, tiled=True, axis_index_groups=groups)

    right = call(right_kernel, jax.ShapeDtypeStruct((2048, 1536), jnp.bfloat16), at, psi, psi_mate, hpsi, hpsi_mate,
                 limit=32, in_specs=[SMEM] + [VMEM] * 4, out_specs=VMEM)
    column = lax.broadcasted_iota(jnp.int32, (1, 2048), 1)
    scale = jnp.where((column & 1023) < 512, H_SCALE, S_SCALE).astype(jnp.float32)

    def reduced(x_first, first, second):
        left = call(functools.partial(left_kernel, x_first), [jax.ShapeDtypeStruct((256, 1536), jnp.bfloat16)] * 4,
                    at, first, second, in_specs=[SMEM, VMEM, VMEM], out_specs=[VMEM] * 4)
        one, two = ("dx", "dz") if x_first else ("dz", "dx")
        got = [move((dot_rows(left[d], right) * scale).astype(jnp.float16), **{one: d}) for d in (1, 3, 2)]
        total = dot_rows(left[0], right) * scale
        for g in got:
            total = total + g.astype(jnp.float32)
        mine = total[0:64]
        for d in (1, 3, 2):
            mine = mine + move(total[d * 64:d * 64 + 64], **{two: d})
        return mine[0:32] + move(mine[32:64], y_lo=1)

    near = reduced(True, psi, psi_mate)
    psi_cross_mate = move(psi_cross, core=1)
    away = reduced(False, psi_cross, psi_cross_mate)
    hpsi_cross_mate = move(hpsi_cross, core=1)
    near_got = move(near[:, 1024:2048], y_hi=1)
    away_got = move(away[:, 1024:2048], y_hi=1)
    half = jax.ShapeDtypeStruct((2, 64, 512), jnp.float32)
    subspace_h, correlation_s = call(
        final_kernel, [half, half], at, near[:, 0:1024], away[:, 0:1024], near_got, away_got,
        in_specs=[SMEM] + [VMEM] * 4, out_specs=[VMEM] * 2)

    rotated_psi = rotate(at, coef, [psi, psi_mate, psi_cross, psi_cross_mate])
    hpsi_near = rotate(at, coef, [hpsi, hpsi_mate])
    rotated_hpsi = rotate(at, coef, [hpsi_cross, hpsi_cross_mate], hpsi_near)
    return rotated_psi, rotated_hpsi, subspace_h, correlation_s


def solution(mesh):
    placed = (P(None, "band", "ga"), P(None, "band", "ga"), P(None, "ga", "band"))
    return jax.shard_map(
        shards,
        mesh=mesh,
        in_specs=placed,
        out_specs=(
            P(None, "band", "ga"),
            P(None, "band", "ga"),
            P(None, "ga", "band"),
            P(None, "ga", "band"),
        ),
        check_vma=False,
    )
```

time: 694 us -> 242 us (0.35)
  waiting for transfers between devices: 539 us -> 132 us
  local copies, waits for them, and re-layouts: 58.9 us -> 5.08 us
  Pallas kernels: 0 us -> 35.7 us
  starting transfers between devices: 5.43 us -> 36.7 us
  matrix products: 44.8 us -> 15.6 us
  other arithmetic: 19.2 us -> 0.33 us
  blocking collectives: 10.5 us -> 0 us
    unnamed x7 -> x1, waiting for transfers between devices: 344 us -> 0.02 us
    all_gather x3 -> x1, waiting for transfers between devices: 195 us -> 0.01 us  [shards(): lax.all_gather(turned, 'ga', axis=0, tiled=True, axis_index_groups=groups)]
    ppermute x0 -> x26, waiting for transfers between devices: none -> 132 us  [move(): return lax.ppermute(value, ('band', 'ga'), pairs)]
    ppermute x0 -> x26, starting transfers between devices: none -> 36.7 us  [move(): return lax.ppermute(value, ('band', 'ga'), pairs)]
    pallas_call x0 -> x9, Pallas kernels: none -> 35.7 us  [call(): pl.pallas_call(kernel, out_shape=outs, compiler_params=pltpu.CompilerPara...]
    unnamed x35 -> x14, local copies, waits for them, and re-layouts: 37.9 us -> 4.71 us
    dot_general x12 -> x8, matrix products: 44.8 us -> 15.6 us  [dot_rows(): lax.dot_general(left, right, (((1,), (1,)), ((), ())), preferred_element_...]
    slice x5 -> x6, local copies, waits for them, and re-layouts: 17.3 us -> 0.28 us  [the longest x2 0.21 us: reduced(): mine = mine + move(total[d * 64:d * 64 + 64], **{two: d})]
  transfers between devices with their start and end apart: 6 -> 27, of which waited for: 5 -> 12; matrix products, arithmetic and copies ran while one was open for 16% -> 7% of each run, Pallas kernels for 0% -> 11%
where the time goes in v2:
time: 242 us; the launch traced here: 240 us
  waiting for transfers between devices  132 us (55%)
  starting transfers between devices  36.7 us (15%)
  Pallas kernels  35.7 us (15%)
  matrix products  15.6 us (6%)
  between operations  14.3 us (6%)
  local copies, waits for them, and re-layouts  5.08 us (2%)
    ppermute x26, waiting for transfers between devices, move(): return lax.ppermute(value, ('band', 'ga'), pairs)  132 us
    ppermute x26, starting transfers between devices, move(): return lax.ppermute(value, ('band', 'ga'), pairs)  36.7 us
    pallas_call x9, Pallas kernels, call(): pl.pallas_call(kernel, out_shape=outs, compiler_params=pltpu.CompilerPara...  35.7 us
    dot_general x8, matrix products, dot_rows(): lax.dot_general(left, right, (((1,), (1,)), ((), ())), preferred_element_...  15.6 us
  transfers between devices with their start and end apart: 27, of which 12 were waited for; matrix products, arithmetic and copies ran while one was open for 7% of the time, Pallas kernels for 11%

profile of v2, /device:TPU:0, one launch (start us, length us, event | category | flops | bytes accessed | tf_op | source)
XLA Modules:
  0.0 239.8 jit_solution(9300496443320369147)
XLA Ops:
  7.2 0.0 all-gather.2.cloned.1.call-start
  7.2 0.1 collective-permute-start.4
  7.3 0.5 collective-permute-start.9
  7.8 3.3 %collective-permute-start.5 = (bf16[2,512,768]{2,1,0:T(8,128)(2,1)}, bf16[2,512,768]{2,1,0:T(8,128)(2,1)}, u32[]{:S(2)}, u32[]{:S(2)}) collective-permute-start(bf16[2,512,768]{2,1,0:T(8,128)(2,1)} %psi.1), channel_id=1, source_target_pairs={{0,64},{1,65},{2,66},{3,67},{4,68},{5,69},{6,70},{7,71},{8,72},{9,... | collective-permute-start | bytes 4718600 | tf_op jit(solution)/shard_map/ppermute | solution.py:35
  11.1 0.7 collective-permute-start
  11.8 0.1 stack.23.at
  11.8 37.3 %collective-permute-done.other = bf16[2,64,512]{2,1,0:T(8,128)(2,1)S(1)} collective-permute-done((bf16[2,64,512]{2,1,0:T(8,128)(2,1)}, bf16[2,64,512]{2,1,0:T(8,128)(2,1)S(1)}, u32[]{:S(2)}, u32[]{:S(2)}) %collective-permute-start) | collective-permute-done | bytes 131104 | tf_op jit(solution)/shard_map/ppermute | solution.py:35
  49.1 0.9 copy-done.6
  50.0 0.6 shard_map.66
  50.6 0.1 collective-permute-start.1
  50.7 1.9 collective-permute-start.2
  52.7 1.4 collective-permute-start.3
  54.1 2.6 %collective-permute-done.2.third = bf16[2,2,64,128]{3,2,1,0:T(8,128)(2,1)S(1)} collective-permute-done((bf16[2,2,64,128]{3,2,1,0:T(8,128)(2,1)S(1)}, bf16[2,2,64,128]{3,2,1,0:T(8,128)(2,1)S(1)}, u32[]{:S(2)}, u32[]{:S(2)}) %collective-permute-start.2) | collective-permute-done | bytes 65568 | tf_op jit(solution)/shard_map/ppermute | solution.py:35
  56.8 1.8 collective-permute-start.7
  58.6 1.4 shard_map.67
  60.0 1.4 copy-done
  61.4 0.9 shard_map.71
  62.3 0.5 copy-done.1
  62.8 0.5 copy-done.2
  63.3 1.8 shard_map.72
  65.2 0.1 collective-permute-start.6
  65.3 1.8 fusion.6
  67.1 1.6 collective-permute-start.10
  68.6 1.8 fusion.7
  70.5 1.8 collective-permute-start.11
  72.3 1.9 fusion.8
  74.2 1.9 collective-permute-start.12
  76.1 2.4 %shard_map.73 = (bf16[256,1536]{1,0:T(8,128)(2,1)S(1)}, bf16[256,1536]{1,0:T(8,128)(2,1)S(1)}, bf16[256,1536]{1,0:T(8,128)(2,1)S(1)}, bf16[256,1536]{1,0:T(8,128)(2,1)S(1)}) custom-call(s32[5]{0:T(128)S(1)} %stack.23.at, bf16[2,512,768]{2,1,0:T(8,128)(2,1)} %collective-permute-done.5.refs_2_.near, bf16[2,512,768]{2,1,0:T(8,128)(2,1)S(1)} %collective-permute-done.6.refs_3_.other), custom_call_target="tpu_custom_call" | custom-call | bytes 6291476 | tf_op jit(solution)/shard_map/pallas_call | solution.py:49
  78.5 1.9 fusion.9
  80.4 2.2 collective-permute-start.17
  82.5 1.9 fusion.10
  84.4 1.9 fusion.11
  86.3 11.8 %collective-permute-done.10 = f16[256,2048]{1,0:T(8,128)(2,1)S(1)} collective-permute-done((f16[256,2048]{1,0:T(8,128)(2,1)S(1)}, f16[256,2048]{1,0:T(8,128)(2,1)S(1)}, u32[]{:S(2)}, u32[]{:S(2)}) %collective-permute-start.10) | collective-permute-done | bytes 1048608 | tf_op jit(solution)/shard_map/ppermute | solution.py:35
  98.1 5.2 %collective-permute-start.18 = (f16[256,2048]{1,0:T(8,128)(2,1)S(1)}, f16[256,2048]{1,0:T(8,128)(2,1)S(1)}, u32[]{:S(2)}, u32[]{:S(2)}) collective-permute-start(f16[256,2048]{1,0:T(8,128)(2,1)S(1)} %fusion.10), channel_id=1, source_target_pairs={{0,24},{1,25},{2,26},{3,27},{4,28},{5,29},{6,30},{7,31},{8,0},{9,1... | collective-permute-start | bytes 3145736 | tf_op jit(solution)/shard_map/ppermute | solution.py:35
  103.3 0.9 collective-permute-done.11
  104.2 3.9 %collective-permute-start.19 = (f16[256,2048]{1,0:T(8,128)(2,1)S(1)}, f16[256,2048]{1,0:T(8,128)(2,1)S(1)}, u32[]{:S(2)}, u32[]{:S(2)}) collective-permute-start(f16[256,2048]{1,0:T(8,128)(2,1)S(1)} %fusion.11), channel_id=1, source_target_pairs={{0,16},{1,17},{2,18},{3,19},{4,20},{5,21},{6,22},{7,23},{8,24},{9,... | collective-permute-start | bytes 3145736 | tf_op jit(solution)/shard_map/ppermute | solution.py:35
  108.1 30.3 %collective-permute-done.12 = f16[256,2048]{1,0:T(8,128)(2,1)S(1)} collective-permute-done((f16[256,2048]{1,0:T(8,128)(2,1)S(1)}, f16[256,2048]{1,0:T(8,128)(2,1)S(1)}, u32[]{:S(2)}, u32[]{:S(2)}) %collective-permute-start.12) | collective-permute-done | bytes 1048608 | tf_op jit(solution)/shard_map/ppermute | solution.py:35
  138.4 2.2 fusion.5
  140.7 0.1 fusion.18
  140.8 2.0 collective-permute-start.13
  142.8 2.2 collective-permute-start.14
  145.0 13.8 %collective-permute-done.18 = f16[256,2048]{1,0:T(8,128)(2,1)S(1)} collective-permute-done((f16[256,2048]{1,0:T(8,128)(2,1)S(1)}, f16[256,2048]{1,0:T(8,128)(2,1)S(1)}, u32[]{:S(2)}, u32[]{:S(2)}) %collective-permute-start.18) | collective-permute-done | bytes 1048608 | tf_op jit(solution)/shard_map/ppermute | solution.py:35
  158.8 2.2 fusion.3
  161.1 0.1 fusion.17
  161.2 0.6 collective-permute-start.20
  161.8 2.7 %collective-permute-start.21 = (f32[64,2048]{1,0:T(8,128)S(1)}, f32[64,2048]{1,0:T(8,128)S(1)}, u32[]{:S(2)}, u32[]{:S(2)}) collective-permute-start(f32[64,2048]{1,0:T(8,128)S(1)} %get-tuple-element.34), channel_id=1, source_target_pairs={{0,6},{1,7},{2,0},{3,1},{4,2},{5,3},{6,4},{7,5},{8,14},{9,15},{10,... | collective-permute-start | bytes 1572872 | tf_op jit(solution)/shard_map/ppermute | solution.py:35
  164.5 1.1 collective-permute-start.22
  165.6 15.5 %collective-permute-done.14 = f32[64,2048]{1,0:T(8,128)S(1)} collective-permute-done((f32[64,2048]{1,0:T(8,128)S(1)}, f32[64,2048]{1,0:T(8,128)S(1)}, u32[]{:S(2)}, u32[]{:S(2)}) %collective-permute-start.14) | collective-permute-done | bytes 524320 | tf_op jit(solution)/shard_map/ppermute | solution.py:35
  181.1 0.1 fusion.15
  181.2 0.1 collective-permute-start.16
  181.3 0.8 collective-permute-done.20
  182.2 0.1 fusion.13
  182.3 1.2 collective-permute-start.23
  183.6 6.8 %collective-permute-done.16 = f32[32,2048]{1,0:T(8,128)S(1)} collective-permute-done((f32[32,2048]{1,0:T(8,128)S(1)}, f32[32,2048]{1,0:T(8,128)S(1)}, u32[]{:S(2)}, u32[]{:S(2)}) %collective-permute-start.16) | collective-permute-done | bytes 262176 | tf_op jit(solution)/shard_map/ppermute | solution.py:35
  190.5 0.1 collective-permute-start.24
  190.6 5.5 %collective-permute-done.23 = f32[32,2048]{1,0:T(8,128)S(1)} collective-permute-done((f32[32,2048]{1,0:T(8,128)S(1)}, f32[32,2048]{1,0:T(8,128)S(1)}, u32[]{:S(2)}, u32[]{:S(2)}) %collective-permute-start.23) | collective-permute-done | bytes 262176 | tf_op jit(solution)/shard_map/ppermute | solution.py:35
  196.1 0.3 collective-permute-start.25
  196.4 0.6 collective-permute-done.24.near_got
  197.0 5.8 %collective-permute-done.25.away_got = f32[32,1024]{1,0:T(8,128)S(1)} collective-permute-done((f32[32,1024]{1,0:T(8,128)S(1)}, f32[32,1024]{1,0:T(8,128)S(1)}, u32[]{:S(2)}, u32[]{:S(2)}) %collective-permute-start.25) | collective-permute-done | bytes 131104 | tf_op jit(solution)/shard_map/ppermute | solution.py:35
  202.9 1.4 shard_map.74
  204.2 1.4 copy-done.3
  205.6 7.1 %shard_map.69.refs_2_ = f32[2,512,768]{2,1,0:T(8,128)S(1)} custom-call(s32[5]{0:T(128)S(1)} %stack.23.at, bf16[8192,256]{1,0:T(8,128)(2,1)} %all-gather.2.cloned.1.call-done.coef, bf16[2,512,768]{2,1,0:T(8,128)(2,1)S(1)} %copy-done.3, bf16[2,512,768]{2,1,0:T(8,128)(2,1)} %collective-permute-done.9.refs_1_.hpsi_mate), custom_call_target="tpu_custom_call" | custom-call | flops 3221225472 | bytes 10485780 | tf_op jit(solution)/shard_map/pallas_call | solution.py:49
  212.8 11.8 %shard_map.68 = f32[2,512,768]{2,1,0:T(8,128)} custom-call(s32[5]{0:T(128)S(1)} %stack.23.at, bf16[8192,256]{1,0:T(8,128)(2,1)} %all-gather.2.cloned.1.call-done.coef, bf16[2,512,768]{2,1,0:T(8,128)(2,1)S(1)} %copy-done.1, bf16[2,512,768]{2,1,0:T(8,128)(2,1)S(1)} %collective-permute-done.4.refs_1_.other.psi_mate, ...), custom_call_target="tpu_custom_call" | custom-call | flops 6442450944 | bytes 13631508 | tf_op jit(solution)/shard_map/pallas_call | solution.py:49
  224.6 8.3 %shard_map.70 = f32[2,512,768]{2,1,0:T(8,128)} custom-call(s32[5]{0:T(128)S(1)} %stack.23.at, bf16[8192,256]{1,0:T(8,128)(2,1)} %all-gather.2.cloned.1.call-done.coef, bf16[2,512,768]{2,1,0:T(8,128)(2,1)} %collective-permute-done.7.refs_0_, bf16[2,512,768]{2,1,0:T(8,128)(2,1)} %collective-permute-done.8.refs_1_, f32[2,512,768]{2,1,0:T(8,128)S(1)} %shard_map.69.refs_2_), custom_call_target="tpu_custom_call" | custom-call | flops 3221225472 | bytes 13631508 | tf_op jit(solution)/shard_map/pallas_call | solution.py:49
  (34 shorter events, 0.2 us)
Async XLA Ops:
  7.2 197.1 %all-gather.2.cloned.1.call-start = ((), (), s32[]{:S(2)}) async-start(), calls=%async_computation | async-start | bytes 4456448 | tf_op jit(solution)/shard_map/all_gather | solution.py:198
  7.2 52.8 %collective-permute-start.4 = (bf16[2,512,768]{2,1,0:T(8,128)(2,1)}, bf16[2,512,768]{2,1,0:T(8,128)(2,1)S(1)}, u32[]{:S(2)}, u32[]{:S(2)}) collective-permute-start(bf16[2,512,768]{2,1,0:T(8,128)(2,1)} %psi.1), channel_id=1, source_target_pairs={{0,32},{1,33},{2,34},{3,35},{4,36},{5,37},{6,38},{7,39},{8,40},{9,... | collective-permute-start | bytes 4718600 | tf_op jit(solution)/shard_map/ppermute | solution.py:35
  7.3 55.0 %collective-permute-start.9 = (bf16[2,512,768]{2,1,0:T(8,128)(2,1)}, bf16[2,512,768]{2,1,0:T(8,128)(2,1)}, u32[]{:S(2)}, u32[]{:S(2)}) collective-permute-start(bf16[2,512,768]{2,1,0:T(8,128)(2,1)} %hpsi.1), channel_id=1, source_target_pairs={{0,32},{1,33},{2,34},{3,35},{4,36},{5,37},{6,38},{7,39},{8,40},{9,... | collective-permute-start | bytes 4718600 | tf_op jit(solution)/shard_map/ppermute | solution.py:35
  7.8 57.4 %collective-permute-start.5 = (bf16[2,512,768]{2,1,0:T(8,128)(2,1)}, bf16[2,512,768]{2,1,0:T(8,128)(2,1)}, u32[]{:S(2)}, u32[]{:S(2)}) collective-permute-start(bf16[2,512,768]{2,1,0:T(8,128)(2,1)} %psi.1), channel_id=1, source_target_pairs={{0,64},{1,65},{2,66},{3,67},{4,68},{5,69},{6,70},{7,71},{8,72},{9,... | collective-permute-start | bytes 4718600 | tf_op jit(solution)/shard_map/ppermute | solution.py:35
  11.1 38.1 %collective-permute-start = (bf16[2,64,512]{2,1,0:T(8,128)(2,1)}, bf16[2,64,512]{2,1,0:T(8,128)(2,1)S(1)}, u32[]{:S(2)}, u32[]{:S(2)}) collective-permute-start(bf16[2,64,512]{2,1,0:T(8,128)(2,1)} %own.1), channel_id=1, source_target_pairs={{0,1},{1,0},{2,3},{3,2},{4,5},{5,4},{6,7},{7,6},{8,9},{9,8},{10,11... | collective-permute-start | bytes 393224 | tf_op jit(solution)/shard_map/ppermute | solution.py:35
  49.1 0.9 copy-start.6
  50.6 2.0 collective-permute-start.1
  50.7 6.0 %collective-permute-start.2 = (bf16[2,2,64,128]{3,2,1,0:T(8,128)(2,1)S(1)}, bf16[2,2,64,128]{3,2,1,0:T(8,128)(2,1)S(1)}, u32[]{:S(2)}, u32[]{:S(2)}) collective-permute-start(bf16[2,2,64,128]{3,2,1,0:T(8,128)(2,1)S(1)} %get-tuple-element.20), channel_id=1, source_target_pairs={{0,64},{1,65},{2,66},{3,67},{4,68},{5,69},{6,70},{7,71},{8,72},{9,... | collective-permute-start | bytes 196616 | tf_op jit(solution)/shard_map/ppermute | solution.py:35
  52.7 5.9 %collective-permute-start.3 = (bf16[2,2,64,128]{3,2,1,0:T(8,128)(2,1)S(1)}, bf16[2,2,64,128]{3,2,1,0:T(8,128)(2,1)S(1)}, u32[]{:S(2)}, u32[]{:S(2)}) collective-permute-start(bf16[2,2,64,128]{3,2,1,0:T(8,128)(2,1)S(1)} %get-tuple-element.21), channel_id=1, source_target_pairs={{0,96},{1,97},{2,98},{3,99},{4,100},{5,101},{6,102},{7,103},{8,104... | collective-permute-start | bytes 196616 | tf_op jit(solution)/shard_map/ppermute | solution.py:35
  56.8 105.1 %collective-permute-start.7 = (bf16[2,512,768]{2,1,0:T(8,128)(2,1)}, bf16[2,512,768]{2,1,0:T(8,128)(2,1)}, u32[]{:S(2)}, u32[]{:S(2)}) collective-permute-start(bf16[2,512,768]{2,1,0:T(8,128)(2,1)} %hpsi.1), channel_id=1, source_target_pairs={{0,64},{1,65},{2,66},{3,67},{4,68},{5,69},{6,70},{7,71},{8,72},{9,... | collective-permute-start | bytes 4718600 | tf_op jit(solution)/shard_map/ppermute | solution.py:35
  60.0 1.4 copy-start
  61.4 1.4 copy-start.1
  61.4 1.9 copy-start.2
  65.2 10.9 %collective-permute-start.6 = (bf16[2,512,768]{2,1,0:T(8,128)(2,1)}, bf16[2,512,768]{2,1,0:T(8,128)(2,1)S(1)}, u32[]{:S(2)}, u32[]{:S(2)}) collective-permute-start(bf16[2,512,768]{2,1,0:T(8,128)(2,1)} %collective-permute-done.5.refs_2_.near), channel_id=1, source_target_pairs={{0,32},{1,33},{2,34},{3,35},{4,36},{5,37},{6,38},{7,39},{8,40},{9,... | collective-permute-start | bytes 4718600 | tf_op jit(solution)/shard_map/ppermute | solution.py:35
  67.1 31.1 %collective-permute-start.10 = (f16[256,2048]{1,0:T(8,128)(2,1)S(1)}, f16[256,2048]{1,0:T(8,128)(2,1)S(1)}, u32[]{:S(2)}, u32[]{:S(2)}) collective-permute-start(f16[256,2048]{1,0:T(8,128)(2,1)S(1)} %fusion.6), channel_id=1, source_target_pairs={{0,2},{1,3},{2,4},{3,5},{4,6},{5,7},{6,0},{7,1},{8,10},{9,11},{10,... | collective-permute-start | bytes 3145736 | tf_op jit(solution)/shard_map/ppermute | solution.py:35
  70.5 33.7 %collective-permute-start.11 = (f16[256,2048]{1,0:T(8,128)(2,1)S(1)}, f16[256,2048]{1,0:T(8,128)(2,1)S(1)}, u32[]{:S(2)}, u32[]{:S(2)}) collective-permute-start(f16[256,2048]{1,0:T(8,128)(2,1)S(1)} %fusion.7), channel_id=1, source_target_pairs={{0,6},{1,7},{2,0},{3,1},{4,2},{5,3},{6,4},{7,5},{8,14},{9,15},{10,... | collective-permute-start | bytes 3145736 | tf_op jit(solution)/shard_map/ppermute | solution.py:35
  74.2 64.3 %collective-permute-start.12 = (f16[256,2048]{1,0:T(8,128)(2,1)S(1)}, f16[256,2048]{1,0:T(8,128)(2,1)S(1)}, u32[]{:S(2)}, u32[]{:S(2)}) collective-permute-start(f16[256,2048]{1,0:T(8,128)(2,1)S(1)} %fusion.8), channel_id=1, source_target_pairs={{0,4},{1,5},{2,6},{3,7},{4,0},{5,1},{6,2},{7,3},{8,12},{9,13},{10,... | collective-permute-start | bytes 3145736 | tf_op jit(solution)/shard_map/ppermute | solution.py:35
  76.1 4.3 %copy-start.4 = (bf16[2,512,768]{2,1,0:T(8,128)(2,1)}, bf16[2,512,768]{2,1,0:T(8,128)(2,1)S(1)}, u32[]{:S(2)}) copy-start(bf16[2,512,768]{2,1,0:T(8,128)(2,1)S(1)} %collective-permute-done.6.refs_3_.other) | copy-start | bytes 4718596
  80.4 62.4 %collective-permute-start.17 = (f16[256,2048]{1,0:T(8,128)(2,1)S(1)}, f16[256,2048]{1,0:T(8,128)(2,1)S(1)}, u32[]{:S(2)}, u32[]{:S(2)}) collective-permute-start(f16[256,2048]{1,0:T(8,128)(2,1)S(1)} %fusion.9), channel_id=1, source_target_pairs={{0,8},{1,9},{2,10},{3,11},{4,12},{5,13},{6,14},{7,15},{8,16},{9,17... | collective-permute-start | bytes 3145736 | tf_op jit(solution)/shard_map/ppermute | solution.py:35
  98.1 60.7 %collective-permute-start.18 = (f16[256,2048]{1,0:T(8,128)(2,1)S(1)}, f16[256,2048]{1,0:T(8,128)(2,1)S(1)}, u32[]{:S(2)}, u32[]{:S(2)}) collective-permute-start(f16[256,2048]{1,0:T(8,128)(2,1)S(1)} %fusion.10), channel_id=1, source_target_pairs={{0,24},{1,25},{2,26},{3,27},{4,28},{5,29},{6,30},{7,31},{8,0},{9,1... | collective-permute-start | bytes 3145736 | tf_op jit(solution)/shard_map/ppermute | solution.py:35
  104.2 54.6 %collective-permute-start.19 = (f16[256,2048]{1,0:T(8,128)(2,1)S(1)}, f16[256,2048]{1,0:T(8,128)(2,1)S(1)}, u32[]{:S(2)}, u32[]{:S(2)}) collective-permute-start(f16[256,2048]{1,0:T(8,128)(2,1)S(1)} %fusion.11), channel_id=1, source_target_pairs={{0,16},{1,17},{2,18},{3,19},{4,20},{5,21},{6,22},{7,23},{8,24},{9,... | collective-permute-start | bytes 3145736 | tf_op jit(solution)/shard_map/ppermute | solution.py:35
  140.8 23.7 %collective-permute-start.13 = (f32[64,2048]{1,0:T(8,128)S(1)}, f32[64,2048]{1,0:T(8,128)S(1)}, u32[]{:S(2)}, u32[]{:S(2)}) collective-permute-start(f32[64,2048]{1,0:T(8,128)S(1)} %get-tuple-element.35), channel_id=1, source_target_pairs={{0,8},{1,9},{2,10},{3,11},{4,12},{5,13},{6,14},{7,15},{8,16},{9,17... | collective-permute-start | bytes 1572872 | tf_op jit(solution)/shard_map/ppermute | solution.py:35
  142.8 38.3 %collective-permute-start.14 = (f32[64,2048]{1,0:T(8,128)S(1)}, f32[64,2048]{1,0:T(8,128)S(1)}, u32[]{:S(2)}, u32[]{:S(2)}) collective-permute-start(f32[64,2048]{1,0:T(8,128)S(1)} %get-tuple-element.37), channel_id=1, source_target_pairs={{0,24},{1,25},{2,26},{3,27},{4,28},{5,29},{6,30},{7,31},{8,0},{9,1... | collective-permute-start | bytes 1572872 | tf_op jit(solution)/shard_map/ppermute | solution.py:35
  158.8 22.2 %collective-permute-start.15 = (f32[64,2048]{1,0:T(8,128)S(1)}, f32[64,2048]{1,0:T(8,128)S(1)}, u32[]{:S(2)}, u32[]{:S(2)}) collective-permute-start(f32[64,2048]{1,0:T(8,128)S(1)} %get-tuple-element.36), channel_id=1, source_target_pairs={{0,16},{1,17},{2,18},{3,19},{4,20},{5,21},{6,22},{7,23},{8,24},{9,... | collective-permute-start | bytes 1572872 | tf_op jit(solution)/shard_map/ppermute | solution.py:35
  161.2 21.0 %collective-permute-start.20 = (f32[64,2048]{1,0:T(8,128)S(1)}, f32[64,2048]{1,0:T(8,128)S(1)}, u32[]{:S(2)}, u32[]{:S(2)}) collective-permute-start(f32[64,2048]{1,0:T(8,128)S(1)} %get-tuple-element.32), channel_id=1, source_target_pairs={{0,2},{1,3},{2,4},{3,5},{4,6},{5,7},{6,0},{7,1},{8,10},{9,11},{10,... | collective-permute-start | bytes 1572872 | tf_op jit(solution)/shard_map/ppermute | solution.py:35
  161.8 20.3 %collective-permute-start.21 = (f32[64,2048]{1,0:T(8,128)S(1)}, f32[64,2048]{1,0:T(8,128)S(1)}, u32[]{:S(2)}, u32[]{:S(2)}) collective-permute-start(f32[64,2048]{1,0:T(8,128)S(1)} %get-tuple-element.34), channel_id=1, source_target_pairs={{0,6},{1,7},{2,0},{3,1},{4,2},{5,3},{6,4},{7,5},{8,14},{9,15},{10,... | collective-permute-start | bytes 1572872 | tf_op jit(solution)/shard_map/ppermute | solution.py:35
  164.5 17.7 %collective-permute-start.22 = (f32[64,2048]{1,0:T(8,128)S(1)}, f32[64,2048]{1,0:T(8,128)S(1)}, u32[]{:S(2)}, u32[]{:S(2)}) collective-permute-start(f32[64,2048]{1,0:T(8,128)S(1)} %get-tuple-element.33), channel_id=1, source_target_pairs={{0,4},{1,5},{2,6},{3,7},{4,0},{5,1},{6,2},{7,3},{8,12},{9,13},{10,... | collective-permute-start | bytes 1572872 | tf_op jit(solution)/shard_map/ppermute | solution.py:35
  181.1 43.6 %collective-permute-start.8 = (bf16[2,512,768]{2,1,0:T(8,128)(2,1)}, bf16[2,512,768]{2,1,0:T(8,128)(2,1)}, u32[]{:S(2)}, u32[]{:S(2)}) collective-permute-start(bf16[2,512,768]{2,1,0:T(8,128)(2,1)} %collective-permute-done.7.refs_0_), channel_id=1, source_target_pairs={{0,32},{1,33},{2,34},{3,35},{4,36},{5,37},{6,38},{7,39},{8,40},{9,... | collective-permute-start | bytes 4718600 | tf_op jit(solution)/shard_map/ppermute | solution.py:35
  181.2 9.2 %collective-permute-start.16 = (f32[32,2048]{1,0:T(8,128)S(1)}, f32[32,2048]{1,0:T(8,128)S(1)}, u32[]{:S(2)}, u32[]{:S(2)}) collective-permute-start(f32[32,2048]{1,0:T(8,128)S(1)} %slice.69), channel_id=1, source_target_pairs={{0,1},{1,0},{2,3},{3,2},{4,5},{5,4},{6,7},{7,6},{8,9},{9,8},{10,11... | collective-permute-start | bytes 786440 | tf_op jit(solution)/shard_map/ppermute | solution.py:35
  182.3 13.7 %collective-permute-start.23 = (f32[32,2048]{1,0:T(8,128)S(1)}, f32[32,2048]{1,0:T(8,128)S(1)}, u32[]{:S(2)}, u32[]{:S(2)}) collective-permute-start(f32[32,2048]{1,0:T(8,128)S(1)} %slice.76), channel_id=1, source_target_pairs={{0,1},{1,0},{2,3},{3,2},{4,5},{5,4},{6,7},{7,6},{8,9},{9,8},{10,11... | collective-permute-start | bytes 786440 | tf_op jit(solution)/shard_map/ppermute | solution.py:35
  190.5 6.6 %collective-permute-start.24 = (f32[32,1024]{1,0:T(8,128)S(1)}, f32[32,1024]{1,0:T(8,128)S(1)}, u32[]{:S(2)}, u32[]{:S(2)}) collective-permute-start(f32[32,1024]{1,0:T(8,128)S(1)} %get-tuple-element.40), channel_id=1, source_target_pairs={{0,64},{1,65},{2,66},{3,67},{4,68},{5,69},{6,70},{7,71},{8,72},{9,... | collective-permute-start | bytes 393224 | tf_op jit(solution)/shard_map/ppermute | solution.py:35
  196.1 6.8 %collective-permute-start.25 = (f32[32,1024]{1,0:T(8,128)S(1)}, f32[32,1024]{1,0:T(8,128)S(1)}, u32[]{:S(2)}, u32[]{:S(2)}) collective-permute-start(f32[32,1024]{1,0:T(8,128)S(1)} %get-tuple-element.38), channel_id=1, source_target_pairs={{0,64},{1,65},{2,66},{3,67},{4,68},{5,69},{6,70},{7,71},{8,72},{9,... | collective-permute-start | bytes 393224 | tf_op jit(solution)/shard_map/ppermute | solution.py:35
  204.2 1.4 copy-start.3
  205.6 7.2 %copy-start.5 = (bf16[2,512,768]{2,1,0:T(8,128)(2,1)S(1)}, bf16[2,512,768]{2,1,0:T(8,128)(2,1)}, u32[]{:S(2)}) copy-start(bf16[2,512,768]{2,1,0:T(8,128)(2,1)} %copy-done.4) | copy-start | bytes 4718596
Sparse Core Ops, SparseCore 0:
  60.1 71.3 all-gather.1

commit v3 on v2

v3 whole, which is shorter than its diff:
```python
import functools

import jax
import jax.numpy as jnp
from jax import lax
from jax.experimental import pallas as pl
from jax.experimental.pallas import tpu as pltpu
from jax.sharding import PartitionSpec as P

H_SCALE = 16.0
S_SCALE = 1024.0
MIB = 1024 * 1024
VMEM = pl.BlockSpec(memory_space=pltpu.VMEM)
SMEM = pl.BlockSpec(memory_space=pltpu.SMEM)


def place(device):
    band, ga = divmod(device, 32)
    y_hi, core = divmod(band, 2)
    z, rest = divmod(ga, 8)
    x, y_lo = divmod(rest, 2)
    return [z, x, y_lo, y_hi, core]


def device_at(z, x, y_lo, y_hi, core):
    return (y_hi * 2 + core) * 32 + z * 8 + x * 2 + y_lo


def move(value, dz=0, dx=0, y_lo=0, y_hi=0, core=0):
    pairs = []
    for source in range(128):
        z, x, low, high, c = place(source)
        target = device_at((z + dz) % 4, (x + dx) % 4, low ^ y_lo, high ^ y_hi, c ^ core)
        pairs.append((source, target))
    return lax.ppermute(value, ("band", "ga"), pairs)


def dot_rows(left, right):
    return lax.dot_general(left, right, (((1,), (1,)), ((), ())), preferred_element_type=jnp.float32)


def where_am_i(at):
    return at[0], at[1], at[2], at[3], at[4]


def call(kernel, outs, *args, limit=24, **kw):
    return pl.pallas_call(
        kernel,
        out_shape=outs,
        compiler_params=pltpu.CompilerParams(vmem_limit_bytes=limit * MIB),
        cost_estimate=pl.CostEstimate(flops=1024, bytes_accessed=1024, transcendentals=0),
        **kw,
    )(*args)


def split_kernel(at, own, other, first, second, third, fourth):
    mz, mx, y_lo, y_hi, core = where_am_i(at)
    for k, out in enumerate((first, second, third, fourth)):
        band = (y_hi * 2 + core) ^ k
        cols = pl.ds(pl.multiple_of(band * 128, 128), 128)
        out[y_lo] = own[:, :, cols]
        out[1 - y_lo] = other[:, :, cols]


def turn_kernel(at, first, second, third, fourth, out):
    mz, mx, y_lo, y_hi, core = where_am_i(at)
    for k, src in enumerate((first, second, third, fourth)):
        band = (y_hi * 2 + core) ^ k
        rows = jnp.concatenate(
            [src[low, c, h * 32:h * 32 + 32, :] for h in range(2) for c in range(2) for low in range(2)], axis=0)
        turned = rows.astype(jnp.float32).T.astype(jnp.bfloat16)
        for g in range(4):
            out[pl.ds(pl.multiple_of(g * 128 + band * 32, 32), 32), :] = turned[g * 32:g * 32 + 32, :]


def merge_kernel(at, first, second, third, fourth, out, pieces):
    mz, mx, y_lo, y_hi, core = where_am_i(at)
    for d, src in enumerate((first, second, third, fourth)):
        pieces[d] = src[...]
    for part in range(4):
        blocks = [pieces[(x - mx) & 3, :, part * 64:part * 64 + 64] for x in range(4)]
        out[:, part * 256:part * 256 + 256] = jnp.concatenate(blocks, axis=1)


def right_kernel(at, psi, psi_mate, hpsi, hpsi_mate, out):
    mz, mx, y_lo, y_hi, core = where_am_i(at)
    for half in range(2):
        band = (y_hi ^ half) * 2 + core
        for m, pair in enumerate(((hpsi, hpsi_mate), (psi, psi_mate))):
            for c, src in enumerate(pair):
                for g in range(4):
                    rows = pl.ds(pl.multiple_of(g * 128 + band * 32, 32), 32)
                    re, im = src[0, rows, :], src[1, rows, :]
                    base = m * 1024 + half * 512 + c * 128 + g * 32
                    out[base:base + 32, 0:768] = re
                    out[base:base + 32, 768:1536] = im
                    out[base + 256:base + 288, 0:768] = im
                    out[base + 256:base + 288, 768:1536] = -re


def left_kernel(both, at, near_re, near_im, other_re, other_im, *outs):
    mz, mx, y_lo, y_hi, core = where_am_i(at)
    for dz in range(4):
        z = (mz + dz) & 3
        is_near = (z >> 1) == core
        for dx in range(4):
            x = (mx + dx) & 3
            for dy in range(2):
                rows = pl.ds(pl.multiple_of((z & 1) * 256 + x * 64 + (y_lo ^ dy) * 32, 32), 32)
                by_x, by_z = dz * 64 + dy * 32, dx * 64 + dy * 32
                for c, (near, other) in enumerate(((near_re, other_re), (near_im, other_im))):
                    value = jnp.where(is_near, near[rows, :], other[rows, :])
                    outs[dx][by_x:by_x + 32, c * 768:c * 768 + 768] = value
                    if both:
                        outs[4 + dz][by_z:by_z + 32, c * 768:c * 768 + 768] = value


def whole_left_kernel(both, at, near, other, *outs):
    left_kernel(both, at, near.at[0], near.at[1], other.at[0], other.at[1], *outs)


def rotate_kernel(early, at, z0, z1, z3, *refs):
    mz, mx, y_lo, y_hi, core = where_am_i(at)
    out = refs[-1]
    if early:
        pairs = ((y_hi, refs[0:2], refs[2:4], ((0, z0), (1, z1), (3, z3))),)
        total = None
    else:
        far0, far1, acc = refs[0], refs[1], refs[10]
        pairs = ((y_hi, refs[2:4], refs[4:6], ((2, None),)),
                 (1 - y_hi, refs[6:8], refs[8:10], ((0, z0), (1, z1), (2, None), (3, z3))))
        total = jnp.concatenate([acc[0], acc[1]], axis=0)
    for h, near, other, pieces in pairs:
        for dz, piece in pieces:
            z = (mz + dz) & 3
            is_near = (z >> 1) == core
            rows = pl.ds(pl.multiple_of((z & 1) * 256, 256), 256)
            if piece is None:
                coef = jnp.where(h == 0, far0[...], far1[...])
                re, im = coef[:, 0:256], coef[:, 256:512]
            else:
                re = piece[:, pl.ds(pl.multiple_of(h * 512, 512), 256)]
                im = piece[:, pl.ds(pl.multiple_of(h * 512 + 256, 256), 256)]
            left = jnp.concatenate([
                jnp.concatenate([re, -im], axis=1),
                jnp.concatenate([im, re], axis=1),
            ], axis=0)
            right = jnp.concatenate([
                jnp.where(is_near, near[0][rows, :], other[0][rows, :]),
                jnp.where(is_near, near[1][rows, :], other[1][rows, :]),
            ], axis=0)
            term = jnp.dot(left, right, preferred_element_type=jnp.float32)
            total = term if total is None else total + term
    size = total.shape[0] // 2
    for part in range(2):
        out[part] = total[part * size:part * size + size]


def rotate(at, pieces, blocks, acc=None, rows=None):
    step = 256
    first, steps = (0, 512 // step) if rows is None else (rows * 256 // step, 256 // step)
    tile = pl.BlockSpec((2, step, 768), lambda n: (0, n + first, 0))
    plane = [pl.BlockSpec((pl.squeezed, 512, 768), lambda n, c=c: (c, 0, 0)) for c in range(2)]
    args = [at, *pieces]
    specs = [SMEM] + [pl.BlockSpec((step, c.shape[1]), lambda n: (n + first, 0)) for c in pieces]
    for block in blocks:
        args += block if isinstance(block, list) else [block, block]
        specs += [VMEM, VMEM] if isinstance(block, list) else plane
    if acc is not None:
        args.append(acc)
        specs.append(tile)
    return call(
        functools.partial(rotate_kernel, acc is None),
        jax.ShapeDtypeStruct((2, 512, 768), jnp.float32),
        *args,
        limit=20 if acc is None else 32,
        grid=(steps,),
        in_specs=specs,
        out_specs=tile,
        input_output_aliases={} if rows is None else {len(args) - 1: 0},
    )


def fold_kernel(first, h0, h1, h2, h3, keep, low):
    h = h0[...] + h1[...] + h2[...] + h3[...]
    for rows, out in ((slice(0, 32), keep), (slice(32, 64), low)):
        out[:, 0:3072] = first[rows, :]
        out[:, 3072:4096] = h[rows, :]


def part_kernel(keep, got, own, over):
    for m in range(4):
        for half, out in enumerate((own, over)):
            cols = slice(m * 1024 + half * 512, m * 1024 + half * 512 + 512)
            out[:, m * 512:m * 512 + 512] = keep[:, cols] + got[:, cols]


def final_kernel(at, own, got, h_out, s_out):
    mz, mx, y_lo, y_hi, core = where_am_i(at)
    for src, col_half in ((own, y_hi), (got, 1 - y_hi)):
        for m, out, scale, h in ((0, h_out, H_SCALE, col_half), (1, s_out, S_SCALE, col_half),
                                 (2, s_out, S_SCALE, 1 - col_half), (3, h_out, H_SCALE, 1 - col_half)):
            rows = pl.ds(pl.multiple_of(h * 32, 32), 32)
            for n in range(2):
                for c in range(2):
                    cols = pl.ds(pl.multiple_of((col_half * 2 + (core ^ c)) * 128, 128), 128)
                    base = m * 512 + n * 256 + c * 128
                    out[n, rows, cols] = src[:, base:base + 128] * (1.0 / scale)


def after(value, *earlier):
    return lax.optimization_barrier((value, *earlier))[0]


def after_all(values, *earlier):
    return list(lax.optimization_barrier((*values, *earlier))[:len(values)])


def shards(psi, hpsi, rot):
    band = lax.axis_index("band")
    ga = lax.axis_index("ga")
    y_hi, core = band >> 1, band & 1
    mz, mx, y_lo = ga >> 3, (ga >> 1) & 3, ga & 1
    at = jnp.stack([mz, mx, y_lo, y_hi, core]).astype(jnp.int32)
    column = lax.broadcasted_iota(jnp.int32, (1, 2048), 1)
    scale = jnp.where(column < 1024, H_SCALE, S_SCALE).astype(jnp.float32)

    def lefts(first, second, both):
        sizes = [256] * (8 if both else 4)
        return call(functools.partial(left_kernel, both), [jax.ShapeDtypeStruct((n, 1536), jnp.bfloat16) for n in sizes],
                    at, *first, *second, in_specs=[SMEM] + [VMEM] * 4, out_specs=[VMEM] * len(sizes))

    def for_peer(left, operand, factor):
        return (dot_rows(left, operand) * factor).astype(jnp.float16)

    def gathered(mine, operand, factor, got):
        total = dot_rows(mine, operand) * factor
        for g in got:
            total = total + g.astype(jnp.float32)
        return total

    fence = lax.optimization_barrier

    rot_other = move(rot, y_lo=1)
    psi_mate = move(psi, core=1)
    hpsi_mate = move(hpsi, core=1)
    psi, hpsi, psi_mate, hpsi_mate, rot_other = fence((psi, hpsi, psi_mate, hpsi_mate, rot_other))

    sent = call(split_kernel, [jax.ShapeDtypeStruct((2, 2, 64, 128), jnp.bfloat16)] * 4, at, rot, rot_other,
                in_specs=[SMEM, VMEM, VMEM], out_specs=[VMEM] * 4)
    got = [sent[0], move(sent[1], core=1), move(sent[2], y_hi=1), move(sent[3], core=1, y_hi=1)]
    right = call(right_kernel, jax.ShapeDtypeStruct((2048, 1536), jnp.bfloat16), at, psi, psi_mate,
                 after(hpsi, sent[0]), hpsi_mate, limit=32, in_specs=[SMEM] + [VMEM] * 4, out_specs=VMEM)
    near_left = call(functools.partial(whole_left_kernel, False), [jax.ShapeDtypeStruct((256, 1536), jnp.bfloat16)] * 4,
                     at, after(psi, right), psi_mate, in_specs=[SMEM, VMEM, VMEM], out_specs=[VMEM] * 4)
    psi, hpsi, got, right, near_left = fence((psi, hpsi, got, right, near_left))

    turned = call(turn_kernel, jax.ShapeDtypeStruct((512, 256), jnp.bfloat16), at, *got,
                  in_specs=[SMEM] + [VMEM] * 4, out_specs=VMEM)
    cross_re = move(psi[0], y_hi=1)
    xs = [turned, move(turned, dx=-1), move(turned, dx=2), move(turned, dx=1)]
    near_1 = for_peer(after(near_left[1], turned), right, scale)
    near_3 = for_peer(after(near_left[3], near_1), right, scale)
    psi, hpsi, cross_re, xs, near_1, near_3, right = fence((psi, hpsi, cross_re, xs, near_1, near_3, right))

    mine = call(merge_kernel, jax.ShapeDtypeStruct((512, 1024), jnp.bfloat16), at, *xs,
                in_specs=[SMEM] + [VMEM] * 4, out_specs=VMEM,
                scratch_shapes=[pltpu.VMEM((4, 512, 256), jnp.bfloat16)])
    near_got = [move(near_1, dx=1), move(near_3, dx=3)]
    up, down = move(mine, dz=-1), move(mine, dz=1)
    cross_im = move(psi[1], y_hi=1)
    near_2 = for_peer(after(near_left[2], mine), right, scale)
    near_own = dot_rows(after(near_left[0], near_2), right) * scale
    hpsi, cross_re, cross_im, mine, up, down, near_got, near_2, near_own, right = fence(
        (hpsi, cross_re, cross_im, mine, up, down, near_got, near_2, near_own, right))

    mate_re, mate_im = move(cross_re, core=1), move(cross_im, core=1)
    near_got.append(move(near_2, dx=2))
    down_half, up_half = down[:, 0:512], up[:, 512:1024]
    far0, far1 = move(down_half, dz=1), move(up_half, dz=-1)
    hpsi_cross = move(hpsi, y_hi=1)
    psi_cross, psi_cross_mate = [cross_re, cross_im], [mate_re, mate_im]
    away_left = lefts(psi_cross, psi_cross_mate, True)
    right_h, right_s = right[0:1024], right[1024:2048]
    h_2 = for_peer(away_left[6], right_h, H_SCALE)
    got_h = [move(h_2, dz=2)]
    h_1 = for_peer(after(away_left[5], h_2), right_h, H_SCALE)
    h_3 = for_peer(after(away_left[7], h_1), right_h, H_SCALE)
    s_1 = for_peer(after(away_left[1], h_3), right_s, S_SCALE)
    s_3 = for_peer(after(away_left[3], s_1), right_s, S_SCALE)
    s_2 = for_peer(after(away_left[2], s_3), right_s, S_SCALE)
    psi_near = rotate(at, after_all([mine, up, down], s_2), [psi, psi_mate])
    hpsi_near = rotate(at, after_all([mine, up, down], psi_near), [hpsi, hpsi_mate])
    coef = [mine, up, down, far0, far1]
    near_got, coef, h_1, h_3, s_1, s_3, s_2, got_h, right, away_left, psi_near, hpsi_near = fence(
        (near_got, coef, h_1, h_3, s_1, s_3, s_2, got_h, right, away_left, psi_near, hpsi_near))

    right_h, right_s = right[0:1024], right[1024:2048]
    got_h += [move(h_1, dz=1), move(h_3, dz=3)]
    got_s = [move(s_1, dx=1), move(s_3, dx=3), move(s_2, dx=2)]
    rotated_psi = rotate(at, coef, [psi, psi_mate, psi_cross, psi_cross_mate], psi_near)
    near_total = after(near_own, rotated_psi)
    for g in near_got:
        near_total = near_total + g.astype(jnp.float32)
    away_h = gathered(after(away_left[4], near_total), right_h, H_SCALE, got_h)
    hpsi_cross, away_h, got_s, near_total, rotated_psi, right_s = fence(
        (hpsi_cross, away_h, got_s, near_total, rotated_psi, right_s))

    hpsi_cross_mate = move(hpsi_cross, core=1)
    by_x = [away_h[0:64]] + [move(away_h[d * 64:d * 64 + 64], dx=d) for d in (1, 3, 2)]
    away_s = gathered(away_left[0], right_s, S_SCALE, got_s)
    by_z = jnp.concatenate([near_total, away_s], axis=1)
    by_z = [by_z[0:64]] + [move(by_z[d * 64:d * 64 + 64].astype(jnp.float16), dz=d) for d in (1, 3, 2)]
    first = by_z[0]
    for p in by_z[1:]:
        first = first + p.astype(jnp.float32)
    keep, low = call(fold_kernel, [jax.ShapeDtypeStruct((32, 4096), jnp.float32)] * 2, first, *by_x,
                     in_specs=[VMEM] * 5, out_specs=[VMEM] * 2)
    low_got = move(low, y_lo=1)
    blocks = [hpsi, hpsi_mate, hpsi_cross, hpsi_cross_mate]
    part_1 = rotate(at, after_all(coef, low), blocks, hpsi_near, rows=0)
    own, over = call(part_kernel, [jax.ShapeDtypeStruct((32, 2048), jnp.float32)] * 2, after(keep, part_1),
                     low_got, in_specs=[VMEM] * 2, out_specs=[VMEM] * 2)
    rotated_hpsi = rotate(at, after_all(coef, over), blocks, part_1, rows=1)
    own = after(own, rotated_hpsi)
    half = jax.ShapeDtypeStruct((2, 64, 512), jnp.float32)
    subspace_h, correlation_s = call(
        final_kernel, [half, half], at, own, move(over, y_hi=1), in_specs=[SMEM] + [VMEM] * 2, out_specs=[VMEM] * 2)
    return rotated_psi, rotated_hpsi, subspace_h, correlation_s


def solution(mesh):
    placed = (P(None, "band", "ga"), P(None, "band", "ga"), P(None, "ga", "band"))
    return jax.shard_map(
        shards,
        mesh=mesh,
        in_specs=placed,
        out_specs=(
            P(None, "band", "ga"),
            P(None, "band", "ga"),
            P(None, "ga", "band"),
            P(None, "ga", "band"),
        ),
        check_vma=False,
    )
```

time: 242 us -> 191 us (0.79)
  waiting for transfers between devices: 132 us -> 83.8 us
  between operations: 14.3 us -> 0.95 us
  starting transfers between devices: 36.7 us -> 49.3 us
    ppermute x26 -> x36, waiting for transfers between devices: 132 us -> 83.8 us  [move(): return lax.ppermute(value, ('band', 'ga'), pairs)]
    ppermute x26 -> x36, starting transfers between devices: 36.7 us -> 49.3 us  [move(): return lax.ppermute(value, ('band', 'ga'), pairs)]
    pallas_call x9 -> x14, Pallas kernels: 35.7 us -> 33.8 us  [call(): pl.pallas_call(kernel, out_shape=outs, compiler_params=pltpu.CompilerPara...]
    dot_general x8 -> x12, matrix products: 15.6 us -> 17.3 us  [dot_rows(): lax.dot_general(left, right, (((1,), (1,)), ((), ())), preferred_element_...]
  transfers between devices with their start and end apart: 27 -> 36, of which waited for: 12 -> 19; matrix products, arithmetic and copies ran while one was open for 7% -> 9% of each run, Pallas kernels for 11% -> 16%
where the time goes in v3:
time: 191 us
  waiting for transfers between devices  83.8 us (44%)
  starting transfers between devices  49.3 us (26%)
  Pallas kernels  33.8 us (18%)
  matrix products  17.3 us (9%)
  local copies, waits for them, and re-layouts  4.27 us (2%)
    ppermute x36, waiting for transfers between devices, move(): return lax.ppermute(value, ('band', 'ga'), pairs)  83.8 us
    ppermute x36, starting transfers between devices, move(): return lax.ppermute(value, ('band', 'ga'), pairs)  49.3 us
    pallas_call x14, Pallas kernels, call(): pl.pallas_call(kernel, out_shape=outs, compiler_params=pltpu.CompilerPara...  33.8 us
    dot_general x12, matrix products, dot_rows(): lax.dot_general(left, right, (((1,), (1,)), ((), ())), preferred_element_...  17.3 us
  transfers between devices with their start and end apart: 36, of which 19 were waited for; matrix products, arithmetic and copies ran while one was open for 9% of the time, Pallas kernels for 16%

profile of v3, /device:TPU:0, one launch (start us, length us, event | category | flops | bytes accessed | tf_op | source)
XLA Modules:
  0.0 190.6 jit_solution(12463943149347995423)
XLA Ops:
  1.2 1.7 collective-permute-start.2
  3.0 4.0 %collective-permute-done.2.other = bf16[2,64,512]{2,1,0:T(8,128)(2,1)S(1)} collective-permute-done((bf16[2,64,512]{2,1,0:T(8,128)(2,1)}, bf16[2,64,512]{2,1,0:T(8,128)(2,1)S(1)}, u32[]{:S(2)}, u32[]{:S(2)}) %collective-permute-start.2) | collective-permute-done | bytes 131104 | tf_op jit(solution)/shard_map/ppermute | solution.py:35
  6.9 0.9 copy-done.2
  8.5 3.4 %collective-permute-start.4 = (bf16[2,2,64,128]{3,2,1,0:T(8,128)(2,1)S(1)}, bf16[2,2,64,128]{3,2,1,0:T(8,128)(2,1)S(1)}, u32[]{:S(2)}, u32[]{:S(2)}) collective-permute-start(bf16[2,2,64,128]{3,2,1,0:T(8,128)(2,1)S(1)} %get-tuple-element.126), channel_id=1, source_target_pairs={{0,64},{1,65},{2,66},{3,67},{4,68},{5,69},{6,70},{7,71},{8,72},{9,... | collective-permute-start | bytes 196616 | tf_op jit(solution)/shard_map/ppermute | solution.py:35
  12.0 1.4 copy-done
  13.4 1.8 shard_map.67
  15.2 0.9 shard_map.68
  16.1 1.4 collective-permute-done.5.fourth
  18.1 2.8 %collective-permute-start.7 = (bf16[512,256]{1,0:T(8,128)(2,1)S(1)}, bf16[512,256]{1,0:T(8,128)(2,1)S(1)}, u32[]{:S(2)}, u32[]{:S(2)}) collective-permute-start(bf16[512,256]{1,0:T(8,128)(2,1)S(1)} %shard_map.69.first), channel_id=1, source_target_pairs={{0,6},{1,7},{2,0},{3,1},{4,2},{5,3},{6,4},{7,5},{8,14},{9,15},{10,... | collective-permute-start | bytes 786440 | tf_op jit(solution)/shard_map/ppermute | solution.py:35
  21.8 0.9 collective-permute-start.9
  22.7 2.0 %collective-permute-start.6 = (bf16[512,768]{1,0:T(8,128)(2,1)S(1)}, bf16[512,768]{1,0:T(8,128)(2,1)S(1)}, u32[]{:S(2)}, u32[]{:S(2)}) collective-permute-start(bf16[512,768]{1,0:T(8,128)(2,1)S(1)} %slice_bitcast_fusion.1), channel_id=1, source_target_pairs={{0,64},{1,65},{2,66},{3,67},{4,68},{5,69},{6,70},{7,71},{8,72},{9,... | collective-permute-start | bytes 2359304 | tf_op jit(solution)/shard_map/ppermute | solution.py:35
  24.7 1.8 fusion.3
  26.5 1.8 fusion.4
  28.4 4.2 %collective-permute-done.7.second = bf16[512,256]{1,0:T(8,128)(2,1)S(1)} collective-permute-done((bf16[512,256]{1,0:T(8,128)(2,1)S(1)}, bf16[512,256]{1,0:T(8,128)(2,1)S(1)}, u32[]{:S(2)}, u32[]{:S(2)}) %collective-permute-start.7) | collective-permute-done | bytes 262176 | tf_op jit(solution)/shard_map/ppermute | solution.py:35
  32.5 3.7 %collective-permute-done.9.fourth = bf16[512,256]{1,0:T(8,128)(2,1)S(1)} collective-permute-done((bf16[512,256]{1,0:T(8,128)(2,1)S(1)}, bf16[512,256]{1,0:T(8,128)(2,1)S(1)}, u32[]{:S(2)}, u32[]{:S(2)}) %collective-permute-start.9) | collective-permute-done | bytes 262176 | tf_op jit(solution)/shard_map/ppermute | solution.py:35
  36.2 6.9 %collective-permute-done.6.near_re.refs_6_ = bf16[512,768]{1,0:T(8,128)(2,1)S(1)} collective-permute-done((bf16[512,768]{1,0:T(8,128)(2,1)S(1)}, bf16[512,768]{1,0:T(8,128)(2,1)S(1)}, u32[]{:S(2)}, u32[]{:S(2)}) %collective-permute-start.6) | collective-permute-done | bytes 786464 | tf_op jit(solution)/shard_map/ppermute | solution.py:35
  43.1 1.0 shard_map.70.z0
  44.1 4.1 %collective-permute-start.11 = (bf16[512,1024]{1,0:T(8,128)(2,1)S(1)}, bf16[512,1024]{1,0:T(8,128)(2,1)S(1)}, u32[]{:S(2)}, u32[]{:S(2)}) collective-permute-start(bf16[512,1024]{1,0:T(8,128)(2,1)S(1)} %shard_map.70.z0), channel_id=1, source_target_pairs={{0,24},{1,25},{2,26},{3,27},{4,28},{5,29},{6,30},{7,31},{8,0},{9,1... | collective-permute-start | bytes 3145736 | tf_op jit(solution)/shard_map/ppermute | solution.py:35
  48.2 2.2 %collective-permute-start.10 = (bf16[512,768]{1,0:T(8,128)(2,1)S(1)}, bf16[512,768]{1,0:T(8,128)(2,1)S(1)}, u32[]{:S(2)}, u32[]{:S(2)}) collective-permute-start(bf16[512,768]{1,0:T(8,128)(2,1)S(1)} %slice_bitcast_fusion), channel_id=1, source_target_pairs={{0,64},{1,65},{2,66},{3,67},{4,68},{5,69},{6,70},{7,71},{8,72},{9,... | collective-permute-start | bytes 2359304 | tf_op jit(solution)/shard_map/ppermute | solution.py:35
  50.4 1.8 collective-permute-start.13
  52.2 1.4 collective-permute-start.14
  53.6 1.8 fusion.5
  55.5 1.8 convolution_multiply_fusion
  57.3 10.1 %collective-permute-done.10.near_im.refs_7_ = bf16[512,768]{1,0:T(8,128)(2,1)S(1)} collective-permute-done((bf16[512,768]{1,0:T(8,128)(2,1)S(1)}, bf16[512,768]{1,0:T(8,128)(2,1)S(1)}, u32[]{:S(2)}, u32[]{:S(2)}) %collective-permute-start.10) | collective-permute-done | bytes 786464 | tf_op jit(solution)/shard_map/ppermute | solution.py:35
  67.4 1.8 collective-permute-done.11.z1
  69.2 3.4 %collective-permute-done.12.z3 = bf16[512,1024]{1,0:T(8,128)(2,1)S(1)} collective-permute-done((bf16[512,1024]{1,0:T(8,128)(2,1)S(1)}, bf16[512,1024]{1,0:T(8,128)(2,1)S(1)}, u32[]{:S(2)}, u32[]{:S(2)}) %collective-permute-start.12) | collective-permute-done | bytes 1048608 | tf_op jit(solution)/shard_map/ppermute | solution.py:35
  72.6 2.1 %collective-permute-done.13 = f16[256,2048]{1,0:T(8,128)(2,1)S(1)} collective-permute-done((f16[256,2048]{1,0:T(8,128)(2,1)S(1)}, f16[256,2048]{1,0:T(8,128)(2,1)S(1)}, u32[]{:S(2)}, u32[]{:S(2)}) %collective-permute-start.13) | collective-permute-done | bytes 1048608 | tf_op jit(solution)/shard_map/ppermute | solution.py:35
  75.5 2.0 %collective-permute-start.16 = (f16[256,2048]{1,0:T(8,128)(2,1)S(1)}, f16[256,2048]{1,0:T(8,128)(2,1)S(1)}, u32[]{:S(2)}, u32[]{:S(2)}) collective-permute-start(f16[256,2048]{1,0:T(8,128)(2,1)S(1)} %fusion.5), channel_id=1, source_target_pairs={{0,4},{1,5},{2,6},{3,7},{4,0},{5,1},{6,2},{7,3},{8,12},{9,13},{10,... | collective-permute-start | bytes 3145736 | tf_op jit(solution)/shard_map/ppermute | solution.py:35
  77.7 3.3 %collective-permute-start.18 = (bf16[512,512]{1,0:T(8,128)(2,1)S(1)}, bf16[512,512]{1,0:T(8,128)(2,1)S(1)}, u32[]{:S(2)}, u32[]{:S(2)}) collective-permute-start(bf16[512,512]{1,0:T(8,128)(2,1)S(1)} %slice.54), channel_id=1, source_target_pairs={{0,24},{1,25},{2,26},{3,27},{4,28},{5,29},{6,30},{7,31},{8,0},{9,1... | collective-permute-start | bytes 1572872 | tf_op jit(solution)/shard_map/ppermute | solution.py:35
  81.0 1.0 shard_map.71
  82.0 1.0 fusion.66
  83.0 1.3 collective-permute-start.21
  84.3 1.8 fusion.63
  86.1 1.8 fusion.60
  87.9 1.0 fusion.57
  88.9 1.0 fusion.54
  90.0 1.0 fusion.51
  91.4 3.7 %shard_map.72.refs_10_ = f32[2,512,768]{2,1,0:T(8,128)S(1)} custom-call(s32[5]{0:T(128)S(1)} %stack.23.at, bf16[512,1024]{1,0:T(8,128)(2,1)S(1)} %shard_map.70.z0, bf16[512,1024]{1,0:T(8,128)(2,1)S(1)} %collective-permute-done.11.z1, bf16[512,1024]{1,0:T(8,128)(2,1)S(1)} %collective-permute-done.12.z3, bf16[2,512,768]{2,1,0:T(8,128)(2,1)S(1)} %copy-done.1, ...), custom_call_target="tpu_custom_call" | custom-call | flops 1024 | bytes 1024 | tf_op jit(solution)/shard_map/pallas_call | solution.py:47
  95.1 5.4 %shard_map.73.refs_10_ = f32[2,512,768]{2,1,0:T(8,128)} custom-call(s32[5]{0:T(128)S(1)} %stack.23.at, bf16[512,1024]{1,0:T(8,128)(2,1)S(1)} %shard_map.70.z0, bf16[512,1024]{1,0:T(8,128)(2,1)S(1)} %collective-permute-done.11.z1, bf16[512,1024]{1,0:T(8,128)(2,1)S(1)} %collective-permute-done.12.z3, bf16[2,512,768]{2,1,0:T(8,128)(2,1)} %refs_3_.2, ...), custom_call_target="tpu_custom_call" | custom-call | flops 1024 | bytes 1024 | tf_op jit(solution)/shard_map/pallas_call | solution.py:47
  100.5 2.5 %collective-permute-done.18.refs_1_ = bf16[512,512]{1,0:T(8,128)(2,1)S(1)} collective-permute-done((bf16[512,512]{1,0:T(8,128)(2,1)S(1)}, bf16[512,512]{1,0:T(8,128)(2,1)S(1)}, u32[]{:S(2)}, u32[]{:S(2)}) %collective-permute-start.18) | collective-permute-done | bytes 524320 | tf_op jit(solution)/shard_map/ppermute | solution.py:35
  103.0 1.8 collective-permute-done.21
  105.6 1.2 collective-permute-start.22
  106.9 1.2 collective-permute-start.15
  108.1 6.5 %shard_map.74 = f32[2,512,768]{2,1,0:T(8,128)} custom-call(s32[5]{0:T(128)S(1)} %stack.23.at, bf16[512,1024]{1,0:T(8,128)(2,1)S(1)} %shard_map.70.z0, bf16[512,1024]{1,0:T(8,128)(2,1)S(1)} %collective-permute-done.11.z1, bf16[512,1024]{1,0:T(8,128)(2,1)S(1)} %collective-permute-done.12.z3, bf16[512,512]{1,0:T(8,128)(2,1)S(1)} %collective-permute-done.17.refs_0_, ...), custom_call_target="tpu_custom_call" | custom-call | flops 1024 | bytes 1024 | tf_op jit(solution)/shard_map/pallas_call | solution.py:47
  114.6 2.0 %collective-permute-start.23 = (f16[256,1024]{1,0:T(8,128)(2,1)S(1)}, f16[256,1024]{1,0:T(8,128)(2,1)S(1)}, u32[]{:S(2)}, u32[]{:S(2)}) collective-permute-start(f16[256,1024]{1,0:T(8,128)(2,1)S(1)} %copy-done.5), channel_id=1, source_target_pairs={{0,24},{1,25},{2,26},{3,27},{4,28},{5,29},{6,30},{7,31},{8,0},{9,1... | collective-permute-start | bytes 1572872 | tf_op jit(solution)/shard_map/ppermute | solution.py:35
  116.6 1.5 collective-permute-start.24
  118.1 1.7 collective-permute-start.25
  119.9 1.4 collective-permute-start.26
  122.2 4.2 %collective-permute-done.23 = f16[256,1024]{1,0:T(8,128)(2,1)S(1)} collective-permute-done((f16[256,1024]{1,0:T(8,128)(2,1)S(1)}, f16[256,1024]{1,0:T(8,128)(2,1)S(1)}, u32[]{:S(2)}, u32[]{:S(2)}) %collective-permute-start.23) | collective-permute-done | bytes 524320 | tf_op jit(solution)/shard_map/ppermute | solution.py:35
  126.4 1.2 fusion.48
  127.6 15.6 %collective-permute-done.15.refs_6_.refs_7_ = bf16[2,512,768]{2,1,0:T(8,128)(2,1)S(1)} collective-permute-done((bf16[2,512,768]{2,1,0:T(8,128)(2,1)}, bf16[2,512,768]{2,1,0:T(8,128)(2,1)S(1)}, u32[]{:S(2)}, u32[]{:S(2)}) %collective-permute-start.15) | collective-permute-done | bytes 1572896 | tf_op jit(solution)/shard_map/ppermute | solution.py:35
  143.2 1.2 fusion.47
  145.1 3.0 %collective-permute-start.28 = (f16[64,3072]{1,0:T(8,128)(2,1)S(1)}, f16[64,3072]{1,0:T(8,128)(2,1)S(1)}, u32[]{:S(2)}, u32[]{:S(2)}) collective-permute-start(f16[64,3072]{1,0:T(8,128)(2,1)S(1)} %get-tuple-element.240), channel_id=1, source_target_pairs={{0,24},{1,25},{2,26},{3,27},{4,28},{5,29},{6,30},{7,31},{8,0},{9,1... | collective-permute-start | bytes 1179656 | tf_op jit(solution)/shard_map/ppermute | solution.py:35
  148.7 1.6 collective-permute-start.30
  150.3 6.7 %collective-permute-done.27 = f16[64,3072]{1,0:T(8,128)(2,1)S(1)} collective-permute-done((f16[64,3072]{1,0:T(8,128)(2,1)S(1)}, f16[64,3072]{1,0:T(8,128)(2,1)S(1)}, u32[]{:S(2)}, u32[]{:S(2)}) %collective-permute-start.27) | collective-permute-done | bytes 393248 | tf_op jit(solution)/shard_map/ppermute | solution.py:35
  157.0 1.3 collective-permute-start.31
  158.2 3.9 %collective-permute-done.28 = f16[64,3072]{1,0:T(8,128)(2,1)S(1)} collective-permute-done((f16[64,3072]{1,0:T(8,128)(2,1)S(1)}, f16[64,3072]{1,0:T(8,128)(2,1)S(1)}, u32[]{:S(2)}, u32[]{:S(2)}) %collective-permute-start.28) | collective-permute-done | bytes 393248 | tf_op jit(solution)/shard_map/ppermute | solution.py:35
  162.1 1.5 collective-permute-start.32
  163.9 6.1 %collective-permute-done.32.h3 = f32[64,1024]{1,0:T(8,128)S(1)} collective-permute-done((f32[64,1024]{1,0:T(8,128)S(1)}, f32[64,1024]{1,0:T(8,128)S(1)}, u32[]{:S(2)}, u32[]{:S(2)}) %collective-permute-start.32) | collective-permute-done | bytes 262176 | tf_op jit(solution)/shard_map/ppermute | solution.py:35
  170.9 5.4 %shard_map.76.refs_10_ = f32[2,512,768]{2,1,0:T(8,128)} custom-call(s32[5]{0:T(128)S(1)} %stack.23.at, bf16[512,1024]{1,0:T(8,128)(2,1)S(1)} %shard_map.70.z0, bf16[512,1024]{1,0:T(8,128)(2,1)S(1)} %collective-permute-done.11.z1, bf16[512,1024]{1,0:T(8,128)(2,1)S(1)} %collective-permute-done.12.z3, ...), custom_call_target="tpu_custom_call", output_to_operand_aliasing={{}: (14, {})} | custom-call | flops 1024 | bytes 1024 | tf_op jit(solution)/shard_map/pallas_call | solution.py:47
  176.2 5.0 %collective-permute-done.34.got = f32[32,4096]{1,0:T(8,128)S(1)} collective-permute-done((f32[32,4096]{1,0:T(8,128)S(1)}, f32[32,4096]{1,0:T(8,128)S(1)}, u32[]{:S(2)}, u32[]{:S(2)}) %collective-permute-start.34) | collective-permute-done | bytes 524320 | tf_op jit(solution)/shard_map/ppermute | solution.py:35
  181.2 2.3 %collective-permute-start.35 = (f32[32,2048]{1,0:T(8,128)S(1)}, f32[32,2048]{1,0:T(8,128)S(1)}, u32[]{:S(2)}, u32[]{:S(2)}) collective-permute-start(f32[32,2048]{1,0:T(8,128)S(1)} %get-tuple-element.228), channel_id=1, source_target_pairs={{0,64},{1,65},{2,66},{3,67},{4,68},{5,69},{6,70},{7,71},{8,72},{9,... | collective-permute-start | bytes 786440 | tf_op jit(solution)/shard_map/ppermute | solution.py:35
  183.6 5.3 %shard_map.78 = f32[2,512,768]{2,1,0:T(8,128)} custom-call(s32[5]{0:T(128)S(1)} %stack.23.at, bf16[512,1024]{1,0:T(8,128)(2,1)S(1)} %shard_map.70.z0, bf16[512,1024]{1,0:T(8,128)(2,1)S(1)} %collective-permute-done.11.z1, bf16[512,1024]{1,0:T(8,128)(2,1)S(1)} %collective-permute-done.12.z3, ...), custom_call_target="tpu_custom_call", output_to_operand_aliasing={{}: (14, {})} | custom-call | flops 1024 | bytes 1024 | tf_op jit(solution)/shard_map/pallas_call | solution.py:47
  189.2 1.4 shard_map.79
  (58 shorter events, 8.9 us)
Async XLA Ops:
  0.6 6.3 %collective-permute-start = (bf16[2,512,768]{2,1,0:T(8,128)(2,1)}, bf16[2,512,768]{2,1,0:T(8,128)(2,1)S(1)}, u32[]{:S(2)}, u32[]{:S(2)}) collective-permute-start(bf16[2,512,768]{2,1,0:T(8,128)(2,1)} %refs_3_), channel_id=1, source_target_pairs={{0,32},{1,33},{2,34},{3,35},{4,36},{5,37},{6,38},{7,39},{8,40},{9,... | collective-permute-start | bytes 4718600 | tf_op jit(solution)/shard_map/ppermute | solution.py:35
  0.7 6.2 %collective-permute-start.1 = (bf16[2,512,768]{2,1,0:T(8,128)(2,1)}, bf16[2,512,768]{2,1,0:T(8,128)(2,1)S(1)}, u32[]{:S(2)}, u32[]{:S(2)}) collective-permute-start(bf16[2,512,768]{2,1,0:T(8,128)(2,1)} %refs_3_.2), channel_id=1, source_target_pairs={{0,32},{1,33},{2,34},{3,35},{4,36},{5,37},{6,38},{7,39},{8,40},{9,... | collective-permute-start | bytes 4718600 | tf_op jit(solution)/shard_map/ppermute | solution.py:35
  1.2 5.7 %collective-permute-start.2 = (bf16[2,64,512]{2,1,0:T(8,128)(2,1)}, bf16[2,64,512]{2,1,0:T(8,128)(2,1)S(1)}, u32[]{:S(2)}, u32[]{:S(2)}) collective-permute-start(bf16[2,64,512]{2,1,0:T(8,128)(2,1)} %own.1), channel_id=1, source_target_pairs={{0,1},{1,0},{2,3},{3,2},{4,5},{5,4},{6,7},{7,6},{8,9},{9,8},{10,11... | collective-permute-start | bytes 393224 | tf_op jit(solution)/shard_map/ppermute | solution.py:35
  6.9 0.9 copy-start.2
  8.4 7.6 %collective-permute-start.3 = (bf16[2,2,64,128]{3,2,1,0:T(8,128)(2,1)S(1)}, bf16[2,2,64,128]{3,2,1,0:T(8,128)(2,1)S(1)}, u32[]{:S(2)}, u32[]{:S(2)}) collective-permute-start(bf16[2,2,64,128]{3,2,1,0:T(8,128)(2,1)S(1)} %get-tuple-element.125), channel_id=1, source_target_pairs={{0,32},{1,33},{2,34},{3,35},{4,36},{5,37},{6,38},{7,39},{8,40},{9,... | collective-permute-start | bytes 196616 | tf_op jit(solution)/shard_map/ppermute | solution.py:35
  8.5 7.6 %collective-permute-start.4 = (bf16[2,2,64,128]{3,2,1,0:T(8,128)(2,1)S(1)}, bf16[2,2,64,128]{3,2,1,0:T(8,128)(2,1)S(1)}, u32[]{:S(2)}, u32[]{:S(2)}) collective-permute-start(bf16[2,2,64,128]{3,2,1,0:T(8,128)(2,1)S(1)} %get-tuple-element.126), channel_id=1, source_target_pairs={{0,64},{1,65},{2,66},{3,67},{4,68},{5,69},{6,70},{7,71},{8,72},{9,... | collective-permute-start | bytes 196616 | tf_op jit(solution)/shard_map/ppermute | solution.py:35
  11.9 5.6 %collective-permute-start.5 = (bf16[2,2,64,128]{3,2,1,0:T(8,128)(2,1)S(1)}, bf16[2,2,64,128]{3,2,1,0:T(8,128)(2,1)S(1)}, u32[]{:S(2)}, u32[]{:S(2)}) collective-permute-start(bf16[2,2,64,128]{3,2,1,0:T(8,128)(2,1)S(1)} %get-tuple-element.127), channel_id=1, source_target_pairs={{0,96},{1,97},{2,98},{3,99},{4,100},{5,101},{6,102},{7,103},{8,104... | collective-permute-start | bytes 196616 | tf_op jit(solution)/shard_map/ppermute | solution.py:35
  11.9 1.4 copy-start
  18.1 14.4 %collective-permute-start.7 = (bf16[512,256]{1,0:T(8,128)(2,1)S(1)}, bf16[512,256]{1,0:T(8,128)(2,1)S(1)}, u32[]{:S(2)}, u32[]{:S(2)}) collective-permute-start(bf16[512,256]{1,0:T(8,128)(2,1)S(1)} %shard_map.69.first), channel_id=1, source_target_pairs={{0,6},{1,7},{2,0},{3,1},{4,2},{5,3},{6,4},{7,5},{8,14},{9,15},{10,... | collective-permute-start | bytes 786440 | tf_op jit(solution)/shard_map/ppermute | solution.py:35
  21.0 11.5 %collective-permute-start.8 = (bf16[512,256]{1,0:T(8,128)(2,1)S(1)}, bf16[512,256]{1,0:T(8,128)(2,1)S(1)}, u32[]{:S(2)}, u32[]{:S(2)}) collective-permute-start(bf16[512,256]{1,0:T(8,128)(2,1)S(1)} %shard_map.69.first), channel_id=1, source_target_pairs={{0,4},{1,5},{2,6},{3,7},{4,0},{5,1},{6,2},{7,3},{8,12},{9,13},{10,... | collective-permute-start | bytes 786440 | tf_op jit(solution)/shard_map/ppermute | solution.py:35
  21.8 14.4 %collective-permute-start.9 = (bf16[512,256]{1,0:T(8,128)(2,1)S(1)}, bf16[512,256]{1,0:T(8,128)(2,1)S(1)}, u32[]{:S(2)}, u32[]{:S(2)}) collective-permute-start(bf16[512,256]{1,0:T(8,128)(2,1)S(1)} %shard_map.69.first), channel_id=1, source_target_pairs={{0,2},{1,3},{2,4},{3,5},{4,6},{5,7},{6,0},{7,1},{8,10},{9,11},{10,... | collective-permute-start | bytes 786440 | tf_op jit(solution)/shard_map/ppermute | solution.py:35
  22.7 20.3 %collective-permute-start.6 = (bf16[512,768]{1,0:T(8,128)(2,1)S(1)}, bf16[512,768]{1,0:T(8,128)(2,1)S(1)}, u32[]{:S(2)}, u32[]{:S(2)}) collective-permute-start(bf16[512,768]{1,0:T(8,128)(2,1)S(1)} %slice_bitcast_fusion.1), channel_id=1, source_target_pairs={{0,64},{1,65},{2,66},{3,67},{4,68},{5,69},{6,70},{7,71},{8,72},{9,... | collective-permute-start | bytes 2359304 | tf_op jit(solution)/shard_map/ppermute | solution.py:35
  44.1 25.1 %collective-permute-start.11 = (bf16[512,1024]{1,0:T(8,128)(2,1)S(1)}, bf16[512,1024]{1,0:T(8,128)(2,1)S(1)}, u32[]{:S(2)}, u32[]{:S(2)}) collective-permute-start(bf16[512,1024]{1,0:T(8,128)(2,1)S(1)} %shard_map.70.z0), channel_id=1, source_target_pairs={{0,24},{1,25},{2,26},{3,27},{4,28},{5,29},{6,30},{7,31},{8,0},{9,1... | collective-permute-start | bytes 3145736 | tf_op jit(solution)/shard_map/ppermute | solution.py:35
  48.2 24.4 %collective-permute-start.12 = (bf16[512,1024]{1,0:T(8,128)(2,1)S(1)}, bf16[512,1024]{1,0:T(8,128)(2,1)S(1)}, u32[]{:S(2)}, u32[]{:S(2)}) collective-permute-start(bf16[512,1024]{1,0:T(8,128)(2,1)S(1)} %shard_map.70.z0), channel_id=1, source_target_pairs={{0,8},{1,9},{2,10},{3,11},{4,12},{5,13},{6,14},{7,15},{8,16},{9,17... | collective-permute-start | bytes 3145736 | tf_op jit(solution)/shard_map/ppermute | solution.py:35
  48.2 19.1 %collective-permute-start.10 = (bf16[512,768]{1,0:T(8,128)(2,1)S(1)}, bf16[512,768]{1,0:T(8,128)(2,1)S(1)}, u32[]{:S(2)}, u32[]{:S(2)}) collective-permute-start(bf16[512,768]{1,0:T(8,128)(2,1)S(1)} %slice_bitcast_fusion), channel_id=1, source_target_pairs={{0,64},{1,65},{2,66},{3,67},{4,68},{5,69},{6,70},{7,71},{8,72},{9,... | collective-permute-start | bytes 2359304 | tf_op jit(solution)/shard_map/ppermute | solution.py:35
  50.4 24.3 %collective-permute-start.13 = (f16[256,2048]{1,0:T(8,128)(2,1)S(1)}, f16[256,2048]{1,0:T(8,128)(2,1)S(1)}, u32[]{:S(2)}, u32[]{:S(2)}) collective-permute-start(f16[256,2048]{1,0:T(8,128)(2,1)S(1)} %fusion.3), channel_id=1, source_target_pairs={{0,2},{1,3},{2,4},{3,5},{4,6},{5,7},{6,0},{7,1},{8,10},{9,11},{10,... | collective-permute-start | bytes 3145736 | tf_op jit(solution)/shard_map/ppermute | solution.py:35
  52.2 22.8 %collective-permute-start.14 = (f16[256,2048]{1,0:T(8,128)(2,1)S(1)}, f16[256,2048]{1,0:T(8,128)(2,1)S(1)}, u32[]{:S(2)}, u32[]{:S(2)}) collective-permute-start(f16[256,2048]{1,0:T(8,128)(2,1)S(1)} %fusion.4), channel_id=1, source_target_pairs={{0,6},{1,7},{2,0},{3,1},{4,2},{5,3},{6,4},{7,5},{8,14},{9,15},{10,... | collective-permute-start | bytes 3145736 | tf_op jit(solution)/shard_map/ppermute | solution.py:35
  75.0 6.0 %collective-permute-start.19 = (bf16[512,768]{1,0:T(8,128)(2,1)S(1)}, bf16[512,768]{1,0:T(8,128)(2,1)S(1)}, u32[]{:S(2)}, u32[]{:S(2)}) collective-permute-start(bf16[512,768]{1,0:T(8,128)(2,1)S(1)} %collective-permute-done.6.near_re.refs_6_), channel_id=1, source_target_pairs={{0,32},{1,33},{2,34},{3,35},{4,36},{5,37},{6,38},{7,39},{8,40},{9,... | collective-permute-start | bytes 2359304 | tf_op jit(solution)/shard_map/ppermute | solution.py:35
  75.0 6.0 %collective-permute-start.20 = (bf16[512,768]{1,0:T(8,128)(2,1)S(1)}, bf16[512,768]{1,0:T(8,128)(2,1)S(1)}, u32[]{:S(2)}, u32[]{:S(2)}) collective-permute-start(bf16[512,768]{1,0:T(8,128)(2,1)S(1)} %collective-permute-done.10.near_im.refs_7_), channel_id=1, source_target_pairs={{0,32},{1,33},{2,34},{3,35},{4,36},{5,37},{6,38},{7,39},{8,40},{9,... | collective-permute-start | bytes 2359304 | tf_op jit(solution)/shard_map/ppermute | solution.py:35
  75.5 27.5 %collective-permute-start.16 = (f16[256,2048]{1,0:T(8,128)(2,1)S(1)}, f16[256,2048]{1,0:T(8,128)(2,1)S(1)}, u32[]{:S(2)}, u32[]{:S(2)}) collective-permute-start(f16[256,2048]{1,0:T(8,128)(2,1)S(1)} %fusion.5), channel_id=1, source_target_pairs={{0,4},{1,5},{2,6},{3,7},{4,0},{5,1},{6,2},{7,3},{8,12},{9,13},{10,... | collective-permute-start | bytes 3145736 | tf_op jit(solution)/shard_map/ppermute | solution.py:35
  77.6 23.0 %collective-permute-start.17 = (bf16[512,512]{1,0:T(8,128)(2,1)S(1)}, bf16[512,512]{1,0:T(8,128)(2,1)S(1)}, u32[]{:S(2)}, u32[]{:S(2)}) collective-permute-start(bf16[512,512]{1,0:T(8,128)(2,1)S(1)} %slice.53), channel_id=1, source_target_pairs={{0,8},{1,9},{2,10},{3,11},{4,12},{5,13},{6,14},{7,15},{8,16},{9,17... | collective-permute-start | bytes 1572872 | tf_op jit(solution)/shard_map/ppermute | solution.py:35
  77.7 25.3 %collective-permute-start.18 = (bf16[512,512]{1,0:T(8,128)(2,1)S(1)}, bf16[512,512]{1,0:T(8,128)(2,1)S(1)}, u32[]{:S(2)}, u32[]{:S(2)}) collective-permute-start(bf16[512,512]{1,0:T(8,128)(2,1)S(1)} %slice.54), channel_id=1, source_target_pairs={{0,24},{1,25},{2,26},{3,27},{4,28},{5,29},{6,30},{7,31},{8,0},{9,1... | collective-permute-start | bytes 1572872 | tf_op jit(solution)/shard_map/ppermute | solution.py:35
  83.0 21.8 %collective-permute-start.21 = (f16[256,1024]{1,0:T(8,128)(2,1)S(1)}, f16[256,1024]{1,0:T(8,128)(2,1)S(1)}, u32[]{:S(2)}, u32[]{:S(2)}) collective-permute-start(f16[256,1024]{1,0:T(8,128)(2,1)S(1)} %fusion.66), channel_id=1, source_target_pairs={{0,16},{1,17},{2,18},{3,19},{4,20},{5,21},{6,22},{7,23},{8,24},{9,... | collective-permute-start | bytes 1572872 | tf_op jit(solution)/shard_map/ppermute | solution.py:35
  90.0 1.4 copy-start.1
  104.8 0.8 copy-start.3
  105.6 9.0 %copy-start.5 = (f16[256,1024]{1,0:T(8,128)(2,1)S(1)}, f16[256,1024]{1,0:T(8,128)(2,1)}, u32[]{:S(2)}) copy-start(f16[256,1024]{1,0:T(8,128)(2,1)} %fusion.60) | copy-start | bytes 1572868
  105.6 14.2 %collective-permute-start.22 = (f16[256,1024]{1,0:T(8,128)(2,1)}, f16[256,1024]{1,0:T(8,128)(2,1)S(1)}, u32[]{:S(2)}, u32[]{:S(2)}) collective-permute-start(f16[256,1024]{1,0:T(8,128)(2,1)} %fusion.63), channel_id=1, source_target_pairs={{0,8},{1,9},{2,10},{3,11},{4,12},{5,13},{6,14},{7,15},{8,16},{9,17... | collective-permute-start | bytes 1572872 | tf_op jit(solution)/shard_map/ppermute | solution.py:35
  106.9 36.3 %collective-permute-start.15 = (bf16[2,512,768]{2,1,0:T(8,128)(2,1)}, bf16[2,512,768]{2,1,0:T(8,128)(2,1)S(1)}, u32[]{:S(2)}, u32[]{:S(2)}) collective-permute-start(bf16[2,512,768]{2,1,0:T(8,128)(2,1)} %refs_3_.2), channel_id=1, source_target_pairs={{0,64},{1,65},{2,66},{3,67},{4,68},{5,69},{6,70},{7,71},{8,72},{9,... | collective-permute-start | bytes 4718600 | tf_op jit(solution)/shard_map/ppermute | solution.py:35
  114.6 11.8 %collective-permute-start.23 = (f16[256,1024]{1,0:T(8,128)(2,1)S(1)}, f16[256,1024]{1,0:T(8,128)(2,1)S(1)}, u32[]{:S(2)}, u32[]{:S(2)}) collective-permute-start(f16[256,1024]{1,0:T(8,128)(2,1)S(1)} %copy-done.5), channel_id=1, source_target_pairs={{0,24},{1,25},{2,26},{3,27},{4,28},{5,29},{6,30},{7,31},{8,0},{9,1... | collective-permute-start | bytes 1572872 | tf_op jit(solution)/shard_map/ppermute | solution.py:35
  116.6 26.5 %collective-permute-start.24 = (f16[256,1024]{1,0:T(8,128)(2,1)S(1)}, f16[256,1024]{1,0:T(8,128)(2,1)S(1)}, u32[]{:S(2)}, u32[]{:S(2)}) collective-permute-start(f16[256,1024]{1,0:T(8,128)(2,1)S(1)} %fusion.57), channel_id=1, source_target_pairs={{0,2},{1,3},{2,4},{3,5},{4,6},{5,7},{6,0},{7,1},{8,10},{9,11},{10,... | collective-permute-start | bytes 1572872 | tf_op jit(solution)/shard_map/ppermute | solution.py:35
  118.1 25.1 %collective-permute-start.25 = (f16[256,1024]{1,0:T(8,128)(2,1)S(1)}, f16[256,1024]{1,0:T(8,128)(2,1)S(1)}, u32[]{:S(2)}, u32[]{:S(2)}) collective-permute-start(f16[256,1024]{1,0:T(8,128)(2,1)S(1)} %fusion.54), channel_id=1, source_target_pairs={{0,6},{1,7},{2,0},{3,1},{4,2},{5,3},{6,4},{7,5},{8,14},{9,15},{10,... | collective-permute-start | bytes 1572872 | tf_op jit(solution)/shard_map/ppermute | solution.py:35
  119.9 23.3 %collective-permute-start.26 = (f16[256,1024]{1,0:T(8,128)(2,1)S(1)}, f16[256,1024]{1,0:T(8,128)(2,1)S(1)}, u32[]{:S(2)}, u32[]{:S(2)}) collective-permute-start(f16[256,1024]{1,0:T(8,128)(2,1)S(1)} %fusion.51), channel_id=1, source_target_pairs={{0,4},{1,5},{2,6},{3,7},{4,0},{5,1},{6,2},{7,3},{8,12},{9,13},{10,... | collective-permute-start | bytes 1572872 | tf_op jit(solution)/shard_map/ppermute | solution.py:35
  122.0 4.4 %copy-start.4 = (f16[256,1024]{1,0:T(8,128)(2,1)S(1)}, f16[256,1024]{1,0:T(8,128)(2,1)}, u32[]{:S(2)}) copy-start(f16[256,1024]{1,0:T(8,128)(2,1)} %copy-done.3) | copy-start | bytes 1572868
  144.8 12.2 %collective-permute-start.27 = (f16[64,3072]{1,0:T(8,128)(2,1)S(1)}, f16[64,3072]{1,0:T(8,128)(2,1)S(1)}, u32[]{:S(2)}, u32[]{:S(2)}) collective-permute-start(f16[64,3072]{1,0:T(8,128)(2,1)S(1)} %get-tuple-element.238), channel_id=1, source_target_pairs={{0,8},{1,9},{2,10},{3,11},{4,12},{5,13},{6,14},{7,15},{8,16},{9,17... | collective-permute-start | bytes 1179656 | tf_op jit(solution)/shard_map/ppermute | solution.py:35
  145.1 17.0 %collective-permute-start.28 = (f16[64,3072]{1,0:T(8,128)(2,1)S(1)}, f16[64,3072]{1,0:T(8,128)(2,1)S(1)}, u32[]{:S(2)}, u32[]{:S(2)}) collective-permute-start(f16[64,3072]{1,0:T(8,128)(2,1)S(1)} %get-tuple-element.240), channel_id=1, source_target_pairs={{0,24},{1,25},{2,26},{3,27},{4,28},{5,29},{6,30},{7,31},{8,0},{9,1... | collective-permute-start | bytes 1179656 | tf_op jit(solution)/shard_map/ppermute | solution.py:35
  148.1 15.6 %collective-permute-start.29 = (f16[64,3072]{1,0:T(8,128)(2,1)S(1)}, f16[64,3072]{1,0:T(8,128)(2,1)S(1)}, u32[]{:S(2)}, u32[]{:S(2)}) collective-permute-start(f16[64,3072]{1,0:T(8,128)(2,1)S(1)} %get-tuple-element.239), channel_id=1, source_target_pairs={{0,16},{1,17},{2,18},{3,19},{4,20},{5,21},{6,22},{7,23},{8,24},{9,... | collective-permute-start | bytes 1179656 | tf_op jit(solution)/shard_map/ppermute | solution.py:35
  148.6 22.2 %collective-permute-start.33 = (bf16[2,512,768]{2,1,0:T(8,128)(2,1)S(1)}, bf16[2,512,768]{2,1,0:T(8,128)(2,1)S(1)}, u32[]{:S(2)}, u32[]{:S(2)}) collective-permute-start(bf16[2,512,768]{2,1,0:T(8,128)(2,1)S(1)} %collective-permute-done.15.refs_6_.refs_7_), channel_id=1, source_target_pairs={{0,32},{1,33},{2,34},{3,35},{4,36},{5,37},{6,38},{7,39},{8,40},{9,... | collective-permute-start | bytes 4718600 | tf_op jit(solution)/shard_map/ppermute | solution.py:35
  148.7 15.1 %collective-permute-start.30 = (f32[64,1024]{1,0:T(8,128)S(1)}, f32[64,1024]{1,0:T(8,128)S(1)}, u32[]{:S(2)}, u32[]{:S(2)}) collective-permute-start(f32[64,1024]{1,0:T(8,128)S(1)} %get-tuple-element.243), channel_id=1, source_target_pairs={{0,2},{1,3},{2,4},{3,5},{4,6},{5,7},{6,0},{7,1},{8,10},{9,11},{10,... | collective-permute-start | bytes 786440 | tf_op jit(solution)/shard_map/ppermute | solution.py:35
  157.0 6.9 %collective-permute-start.31 = (f32[64,1024]{1,0:T(8,128)S(1)}, f32[64,1024]{1,0:T(8,128)S(1)}, u32[]{:S(2)}, u32[]{:S(2)}) collective-permute-start(f32[64,1024]{1,0:T(8,128)S(1)} %get-tuple-element.242), channel_id=1, source_target_pairs={{0,6},{1,7},{2,0},{3,1},{4,2},{5,3},{6,4},{7,5},{8,14},{9,15},{10,... | collective-permute-start | bytes 786440 | tf_op jit(solution)/shard_map/ppermute | solution.py:35
  162.1 7.9 %collective-permute-start.32 = (f32[64,1024]{1,0:T(8,128)S(1)}, f32[64,1024]{1,0:T(8,128)S(1)}, u32[]{:S(2)}, u32[]{:S(2)}) collective-permute-start(f32[64,1024]{1,0:T(8,128)S(1)} %get-tuple-element.241), channel_id=1, source_target_pairs={{0,4},{1,5},{2,6},{3,7},{4,0},{5,1},{6,2},{7,3},{8,12},{9,13},{10,... | collective-permute-start | bytes 786440 | tf_op jit(solution)/shard_map/ppermute | solution.py:35
  170.1 11.1 %collective-permute-start.34 = (f32[32,4096]{1,0:T(8,128)S(1)}, f32[32,4096]{1,0:T(8,128)S(1)}, u32[]{:S(2)}, u32[]{:S(2)}) collective-permute-start(f32[32,4096]{1,0:T(8,128)S(1)} %get-tuple-element.219), channel_id=1, source_target_pairs={{0,1},{1,0},{2,3},{3,2},{4,5},{5,4},{6,7},{7,6},{8,9},{9,8},{10,11... | collective-permute-start | bytes 1572872 | tf_op jit(solution)/shard_map/ppermute | solution.py:35
  181.2 8.0 %collective-permute-start.35 = (f32[32,2048]{1,0:T(8,128)S(1)}, f32[32,2048]{1,0:T(8,128)S(1)}, u32[]{:S(2)}, u32[]{:S(2)}) collective-permute-start(f32[32,2048]{1,0:T(8,128)S(1)} %get-tuple-element.228), channel_id=1, source_target_pairs={{0,64},{1,65},{2,66},{3,67},{4,68},{5,69},{6,70},{7,71},{8,72},{9,... | collective-permute-start | bytes 786440 | tf_op jit(solution)/shard_map/ppermute | solution.py:35

commit v4 on v3

--- a/solution.py
+++ b/solution.py
@@ -7,8 +7,8 @@
 from jax.experimental.pallas import tpu as pltpu
 from jax.sharding import PartitionSpec as P
 
-H_SCALE = 16.0
-S_SCALE = 1024.0
+ROOM = 8192.0
+TINY = 1e-30
 MIB = 1024 * 1024
 VMEM = pl.BlockSpec(memory_space=pltpu.VMEM)
 SMEM = pl.BlockSpec(memory_space=pltpu.SMEM)
@@ -53,17 +53,22 @@
     )(*args)
 
 
-def split_kernel(at, own, other, first, second, third, fourth):
+def split_kernel(at, largest, own, other, first, second, third, fourth):
     mz, mx, y_lo, y_hi, core = where_am_i(at)
     for k, out in enumerate((first, second, third, fourth)):
         band = (y_hi * 2 + core) ^ k
         cols = pl.ds(pl.multiple_of(band * 128, 128), 128)
-        out[y_lo] = own[:, :, cols]
-        out[1 - y_lo] = other[:, :, cols]
-
-
-def turn_kernel(at, first, second, third, fourth, out):
-    mz, mx, y_lo, y_hi, core = where_am_i(at)
+        out[y_lo, :, 0:64, :] = own[:, :, cols]
+        out[1 - y_lo, :, 0:64, :] = other[:, :, cols]
+        tail = jnp.concatenate([jnp.full((8, 128), largest[0], jnp.float32), jnp.full((8, 128), largest[1], jnp.float32)])
+        for low in range(2):
+            for c in range(2):
+                out[low, c, 64:80, :] = tail.astype(jnp.bfloat16)
+
+
+def turn_kernel(at, first, second, third, fourth, out, scales):
+    mz, mx, y_lo, y_hi, core = where_am_i(at)
+    tails = []
     for k, src in enumerate((first, second, third, fourth)):
         band = (y_hi * 2 + core) ^ k
         rows = jnp.concatenate(
@@ -71,6 +76,39 @@
         turned = rows.astype(jnp.float32).T.astype(jnp.bfloat16)
         for g in range(4):
             out[pl.ds(pl.multiple_of(g * 128 + band * 32, 32), 32), :] = turned[g * 32:g * 32 + 32, :]
+        tails.append(src[0, 0, 64:80, :].astype(jnp.float32))
+    chip = jnp.maximum(tails[0], tails[1])
+    psi = jnp.maximum(chip, jnp.maximum(tails[2], tails[3]))[0:8]
+    for m, right in ((0, chip[8:16]), (1, chip[0:8])):
+        factor = (ROOM / (1536.0 * psi * right + TINY)).astype(jnp.bfloat16).astype(jnp.float32)
+        for n in range(8):
+            scales[:, m * 1024 + n * 128:m * 1024 + n * 128 + 128] = factor
+        if m == 0:
+            first_factor = factor
+    tail = jnp.concatenate([first_factor, factor], axis=0).astype(jnp.bfloat16)
+    out[512:528, 0:128] = tail
+    out[512:528, 128:256] = tail
+
+
+def factor_kernel(at, x1, x2, x3, mine, up, far, down, out):
+    mz, mx, y_lo, y_hi, core = where_am_i(at)
+    lanes = lax.broadcasted_iota(jnp.int32, (16, 256), 1)
+
+    def put(row, pair):
+        for m in range(2):
+            out[row:row + 1, m * 1024:m * 1024 + 1024] = jnp.broadcast_to(pair[m], (1, 1024))
+
+    def pair(values):
+        return values[0:1, 0:1], values[8:9, 0:1]
+
+    for row, ref in enumerate((x3, x1, x2)):
+        put(row, [1.0 / v for v in pair(ref[512:528, 0:128].astype(jnp.float32))])
+    for row, ref in enumerate((down, up, far)):
+        values = ref[512:528, 0:256].astype(jnp.float32)
+        here = jnp.min(jnp.where((lanes >> 6) == mx, values, 3e38), axis=1, keepdims=True)
+        put(3 + row, [1.0 / v for v in pair(here)])
+        put(7 + row, [1.0 / v for v in pair(jnp.min(values, axis=1, keepdims=True))])
+    put(6, pair(jnp.min(mine[512:528, 0:256].astype(jnp.float32), axis=1, keepdims=True)))
 
 
 def merge_kernel(at, first, second, third, fourth, out, pieces):
@@ -198,14 +236,13 @@
 def final_kernel(at, own, got, h_out, s_out):
     mz, mx, y_lo, y_hi, core = where_am_i(at)
     for src, col_half in ((own, y_hi), (got, 1 - y_hi)):
-        for m, out, scale, h in ((0, h_out, H_SCALE, col_half), (1, s_out, S_SCALE, col_half),
-                                 (2, s_out, S_SCALE, 1 - col_half), (3, h_out, H_SCALE, 1 - col_half)):
+        for m, out, h in ((0, h_out, col_half), (1, s_out, col_half), (2, s_out, 1 - col_half), (3, h_out, 1 - col_half)):
             rows = pl.ds(pl.multiple_of(h * 32, 32), 32)
             for n in range(2):
                 for c in range(2):
                     cols = pl.ds(pl.multiple_of((col_half * 2 + (core ^ c)) * 128, 128), 128)
                     base = m * 512 + n * 256 + c * 128
-                    out[n, rows, cols] = src[:, base:base + 128] * (1.0 / scale)
+                    out[n, rows, cols] = src[:, base:base + 128]
 
 
 def after(value, *earlier):
@@ -222,8 +259,6 @@
     y_hi, core = band >> 1, band & 1
     mz, mx, y_lo = ga >> 3, (ga >> 1) & 3, ga & 1
     at = jnp.stack([mz, mx, y_lo, y_hi, core]).astype(jnp.int32)
-    column = lax.broadcasted_iota(jnp.int32, (1, 2048), 1)
-    scale = jnp.where(column < 1024, H_SCALE, S_SCALE).astype(jnp.float32)
 
     def lefts(first, second, both):
         sizes = [256] * (8 if both else 4)
@@ -233,21 +268,22 @@
     def for_peer(left, operand, factor):
         return (dot_rows(left, operand) * factor).astype(jnp.float16)
 
-    def gathered(mine, operand, factor, got):
-        total = dot_rows(mine, operand) * factor
-        for g in got:
-            total = total + g.astype(jnp.float32)
+    def gathered(mine, operand, factors, got):
+        total = dot_rows(mine, operand)
+        for factor, g in zip(factors, got):
+            total = total + g.astype(jnp.float32) * factor
         return total
 
     fence = lax.optimization_barrier
 
+    largest = jnp.stack([jnp.max(jnp.abs(psi)), jnp.max(jnp.abs(hpsi))]).astype(jnp.float32)
     rot_other = move(rot, y_lo=1)
     psi_mate = move(psi, core=1)
     hpsi_mate = move(hpsi, core=1)
     psi, hpsi, psi_mate, hpsi_mate, rot_other = fence((psi, hpsi, psi_mate, hpsi_mate, rot_other))
 
-    sent = call(split_kernel, [jax.ShapeDtypeStruct((2, 2, 64, 128), jnp.bfloat16)] * 4, at, rot, rot_other,
-                in_specs=[SMEM, VMEM, VMEM], out_specs=[VMEM] * 4)
+    sent = call(split_kernel, [jax.ShapeDtypeStruct((2, 2, 80, 128), jnp.bfloat16)] * 4, at, largest, rot,
+                rot_other, in_specs=[SMEM, SMEM, VMEM, VMEM], out_specs=[VMEM] * 4)
     got = [sent[0], move(sent[1], core=1), move(sent[2], y_hi=1), move(sent[3], core=1, y_hi=1)]
     right = call(right_kernel, jax.ShapeDtypeStruct((2048, 1536), jnp.bfloat16), at, psi, psi_mate,
                  after(hpsi, sent[0]), hpsi_mate, limit=32, in_specs=[SMEM] + [VMEM] * 4, out_specs=VMEM)
@@ -255,24 +291,29 @@
                      at, after(psi, right), psi_mate, in_specs=[SMEM, VMEM, VMEM], out_specs=[VMEM] * 4)
     psi, hpsi, got, right, near_left = fence((psi, hpsi, got, right, near_left))
 
-    turned = call(turn_kernel, jax.ShapeDtypeStruct((512, 256), jnp.bfloat16), at, *got,
-                  in_specs=[SMEM] + [VMEM] * 4, out_specs=VMEM)
+    turned, scale = call(turn_kernel, [jax.ShapeDtypeStruct((528, 256), jnp.bfloat16),
+                                       jax.ShapeDtypeStruct((8, 2048), jnp.float32)], at, *got,
+                         in_specs=[SMEM] + [VMEM] * 4, out_specs=[VMEM] * 2)
+    scale = scale[0:1]
+    scale_h, scale_s = scale[:, 0:1024], scale[:, 1024:2048]
     cross_re = move(psi[0], y_hi=1)
     xs = [turned, move(turned, dx=-1), move(turned, dx=2), move(turned, dx=1)]
     near_1 = for_peer(after(near_left[1], turned), right, scale)
     near_3 = for_peer(after(near_left[3], near_1), right, scale)
-    psi, hpsi, cross_re, xs, near_1, near_3, right = fence((psi, hpsi, cross_re, xs, near_1, near_3, right))
-
-    mine = call(merge_kernel, jax.ShapeDtypeStruct((512, 1024), jnp.bfloat16), at, *xs,
+    psi, hpsi, cross_re, near_1, near_3, right = fence((psi, hpsi, cross_re, near_1, near_3, right))
+    xs, right = fence((xs, right))
+
+    mine = call(merge_kernel, jax.ShapeDtypeStruct((528, 1024), jnp.bfloat16), at, *xs,
                 in_specs=[SMEM] + [VMEM] * 4, out_specs=VMEM,
-                scratch_shapes=[pltpu.VMEM((4, 512, 256), jnp.bfloat16)])
+                scratch_shapes=[pltpu.VMEM((4, 528, 256), jnp.bfloat16)])
     near_got = [move(near_1, dx=1), move(near_3, dx=3)]
     up, down = move(mine, dz=-1), move(mine, dz=1)
     cross_im = move(psi[1], y_hi=1)
     near_2 = for_peer(after(near_left[2], mine), right, scale)
-    near_own = dot_rows(after(near_left[0], near_2), right) * scale
-    hpsi, cross_re, cross_im, mine, up, down, near_got, near_2, near_own, right = fence(
-        (hpsi, cross_re, cross_im, mine, up, down, near_got, near_2, near_own, right))
+    near_own = dot_rows(after(near_left[0], near_2), right)
+    hpsi, cross_re, mine, up, down, near_got, near_2, near_own, right = fence(
+        (hpsi, cross_re, mine, up, down, near_got, near_2, near_own, right))
+    cross_im, near_2, up, down = fence((cross_im, near_2, up, down))
 
     mate_re, mate_im = move(cross_re, core=1), move(cross_im, core=1)
     near_got.append(move(near_2, dx=2))
@@ -282,13 +323,13 @@
     psi_cross, psi_cross_mate = [cross_re, cross_im], [mate_re, mate_im]
     away_left = lefts(psi_cross, psi_cross_mate, True)
     right_h, right_s = right[0:1024], right[1024:2048]
-    h_2 = for_peer(away_left[6], right_h, H_SCALE)
+    h_2 = for_peer(away_left[6], right_h, scale_h)
     got_h = [move(h_2, dz=2)]
-    h_1 = for_peer(after(away_left[5], h_2), right_h, H_SCALE)
-    h_3 = for_peer(after(away_left[7], h_1), right_h, H_SCALE)
-    s_1 = for_peer(after(away_left[1], h_3), right_s, S_SCALE)
-    s_3 = for_peer(after(away_left[3], s_1), right_s, S_SCALE)
-    s_2 = for_peer(after(away_left[2], s_3), right_s, S_SCALE)
+    h_1 = for_peer(after(away_left[5], h_2), right_h, scale_h)
+    h_3 = for_peer(after(away_left[7], h_1), right_h, scale_h)
+    s_1 = for_peer(after(away_left[1], h_3), right_s, scale_s)
+    s_3 = for_peer(after(away_left[3], s_1), right_s, scale_s)
+    s_2 = for_peer(after(away_left[2], s_3), right_s, scale_s)
     psi_near = rotate(at, after_all([mine, up, down], s_2), [psi, psi_mate])
     hpsi_near = rotate(at, after_all([mine, up, down], psi_near), [hpsi, hpsi_mate])
     coef = [mine, up, down, far0, far1]
@@ -299,21 +340,26 @@
     got_h += [move(h_1, dz=1), move(h_3, dz=3)]
     got_s = [move(s_1, dx=1), move(s_3, dx=3), move(s_2, dx=2)]
     rotated_psi = rotate(at, coef, [psi, psi_mate, psi_cross, psi_cross_mate], psi_near)
-    near_total = after(near_own, rotated_psi)
-    for g in near_got:
-        near_total = near_total + g.astype(jnp.float32)
-    away_h = gathered(after(away_left[4], near_total), right_h, H_SCALE, got_h)
+    factors = call(factor_kernel, jax.ShapeDtypeStruct((16, 2048), jnp.float32), after(at, rotated_psi), *xs[1:], mine, up,
+                   far0, down, in_specs=[SMEM] + [VMEM] * 7, out_specs=VMEM)
+    factor = [factors[n:n + 1] for n in range(10)]
+    near_total = near_own
+    for n, g in enumerate(near_got):
+        near_total = near_total + g.astype(jnp.float32) * factor[n]
+    got_h = [got_h[1], got_h[2], got_h[0]]
+    away_h = gathered(after(away_left[4], near_total), right_h, [f[:, 0:1024] for f in factor[3:6]], got_h)
     hpsi_cross, away_h, got_s, near_total, rotated_psi, right_s = fence(
         (hpsi_cross, away_h, got_s, near_total, rotated_psi, right_s))
 
     hpsi_cross_mate = move(hpsi_cross, core=1)
     by_x = [away_h[0:64]] + [move(away_h[d * 64:d * 64 + 64], dx=d) for d in (1, 3, 2)]
-    away_s = gathered(away_left[0], right_s, S_SCALE, got_s)
+    away_s = gathered(away_left[0], right_s, [f[:, 1024:2048] for f in factor[0:3]], got_s)
     by_z = jnp.concatenate([near_total, away_s], axis=1)
-    by_z = [by_z[0:64]] + [move(by_z[d * 64:d * 64 + 64].astype(jnp.float16), dz=d) for d in (1, 3, 2)]
+    factor = [jnp.concatenate([f, f[:, 1024:2048]], axis=1) for f in factor[6:10]]
+    by_z = [by_z[0:64]] + [move((by_z[d * 64:d * 64 + 64] * factor[0]).astype(jnp.float16), dz=d) for d in (1, 3, 2)]
     first = by_z[0]
-    for p in by_z[1:]:
-        first = first + p.astype(jnp.float32)
+    for p, f in zip(by_z[1:], factor[1:]):
+        first = first + p.astype(jnp.float32) * f
     keep, low = call(fold_kernel, [jax.ShapeDtypeStruct((32, 4096), jnp.float32)] * 2, first, *by_x,
                      in_specs=[VMEM] * 5, out_specs=[VMEM] * 2)
     low_got = move(low, y_lo=1)

time: 191 us -> 191 us (level)
  waiting for transfers between devices: 83.8 us -> 75.5 us
  other arithmetic: 1.13 us -> 7.09 us
  Pallas kernels: 33.8 us -> 37.4 us
  local copies, waits for them, and re-layouts: 4.27 us -> 2.01 us
    ppermute x36, waiting for transfers between devices: 83.8 us -> 75.5 us  [move(): return lax.ppermute(value, ('band', 'ga'), pairs)]
    reduce_max x0 -> x2, other arithmetic: none -> 4.49 us  [the longest x1 2.25 us: shards(): jnp.max(jnp.abs(psi))]
    pallas_call x14 -> x15, Pallas kernels: 33.8 us -> 37.4 us  [call(): pl.pallas_call(kernel, out_shape=outs, compiler_params=pltpu.CompilerPara...]
    unnamed x12, local copies, waits for them, and re-layouts: 3.52 us -> 1.39 us
  transfers between devices with their start and end apart: 36 -> 36, of which waited for: 19 -> 13; matrix products, arithmetic and copies ran while one was open for 9% -> 13% of each run, Pallas kernels for 16% -> 18%
where the time goes in v4:
time: 191 us
  waiting for transfers between devices  75.5 us (40%)
  starting transfers between devices  48.4 us (25%)
  Pallas kernels  37.4 us (20%)
  matrix products  19.2 us (10%)
  other arithmetic  7.09 us (4%)
  local copies, waits for them, and re-layouts  2.01 us (1%)
    ppermute x36, waiting for transfers between devices, move(): return lax.ppermute(value, ('band', 'ga'), pairs)  75.5 us
    ppermute x36, starting transfers between devices, move(): return lax.ppermute(value, ('band', 'ga'), pairs)  48.4 us
    pallas_call x15, Pallas kernels, call(): pl.pallas_call(kernel, out_shape=outs, compiler_params=pltpu.CompilerPara...  37.4 us
    dot_general x12, matrix products, dot_rows(): lax.dot_general(left, right, (((1,), (1,)), ((), ())), preferred_element_...  19.2 us
  transfers between devices with their start and end apart: 36, of which 13 were waited for; matrix products, arithmetic and copies ran while one was open for 13% of the time, Pallas kernels for 18%

profile of v4, /device:TPU:0, one launch (start us, length us, event | category | flops | bytes accessed | tf_op | source)
XLA Modules:
  0.0 190.6 jit_solution(11556967719501008167)
XLA Ops:
  1.2 1.7 collective-permute-start.2
  2.9 2.2 %abs_reduce_fusion.1 = bf16[]{:T(256)} fusion(bf16[2,512,768]{2,1,0:T(8,128)(2,1)} %refs_3_), kind=kLoop, calls=%fused_computation.28 | loop fusion | flops 1572863 | bytes 1572866 | tf_op jit(solution)/shard_map/reduce_max | solution.py:279
  5.2 2.2 %abs_reduce_fusion = bf16[]{:T(256)} fusion(bf16[2,512,768]{2,1,0:T(8,128)(2,1)} %refs_3_.2), kind=kLoop, calls=%fused_computation.27 | loop fusion | flops 1572863 | bytes 1572866 | tf_op jit(solution)/shard_map/reduce_max | solution.py:279
  7.5 1.3 maximum_convert_fusion.largest
  8.8 0.9 copy-done.2
  9.7 0.6 shard_map.66
  10.4 3.0 %collective-permute-start.4 = (bf16[2,2,80,128]{3,2,1,0:T(8,128)(2,1)S(1)}, bf16[2,2,80,128]{3,2,1,0:T(8,128)(2,1)S(1)}, u32[]{:S(2)}, u32[]{:S(2)}) collective-permute-start(bf16[2,2,80,128]{3,2,1,0:T(8,128)(2,1)S(1)} %get-tuple-element.132), channel_id=1, source_target_pairs={{0,64},{1,65},{2,66},{3,67},{4,68},{5,69},{6,70},{7,71},{8,72},{9,... | collective-permute-start | bytes 245768 | tf_op jit(solution)/shard_map/ppermute | solution.py:35
  13.8 2.3 %shard_map.67 = bf16[2048,1536]{1,0:T(8,128)(2,1)S(1)} custom-call(s32[5]{0:T(128)S(1)} %stack.32.at, bf16[2,512,768]{2,1,0:T(8,128)(2,1)S(1)} %copy-done, bf16[2,512,768]{2,1,0:T(8,128)(2,1)} %collective-permute-done.psi_mate.other.refs_2_.refs_3_.refs_4_.refs_5_, bf16[2,512,768]{2,1,0:T(8,128)(2,1)S(1)} %copy-done.1, ...), custom_call_target="tpu_custom_call" | custom-call | flops 1024 | bytes 1024 | tf_op jit(solution)/shard_map/pallas_call | solution.py:47
  16.1 1.8 shard_map.68
  17.9 1.4 collective-permute-done.5.fourth
  19.3 0.7 shard_map.69
  20.0 2.8 %collective-permute-start.7 = (bf16[528,256]{1,0:T(8,128)(2,1)S(1)}, bf16[528,256]{1,0:T(8,128)(2,1)S(1)}, u32[]{:S(2)}, u32[]{:S(2)}) collective-permute-start(bf16[528,256]{1,0:T(8,128)(2,1)S(1)} %get-tuple-element.158.first), channel_id=1, source_target_pairs={{0,6},{1,7},{2,0},{3,1},{4,2},{5,3},{6,4},{7,5},{8,14},{9,15},{10,... | collective-permute-start | bytes 811016 | tf_op jit(solution)/shard_map/ppermute | solution.py:35
  22.8 0.8 collective-permute-start.8
  23.6 0.9 collective-permute-start.9
  24.6 1.7 collective-permute-start.6
  26.3 1.9 fusion.2
  28.2 1.9 fusion.3
  30.1 14.9 %collective-permute-done.6.near_re.refs_6_ = bf16[512,768]{1,0:T(8,128)(2,1)S(1)} collective-permute-done((bf16[512,768]{1,0:T(8,128)(2,1)S(1)}, bf16[512,768]{1,0:T(8,128)(2,1)S(1)}, u32[]{:S(2)}, u32[]{:S(2)}) %collective-permute-start.6) | collective-permute-done | bytes 786464 | tf_op jit(solution)/shard_map/ppermute | solution.py:35
  44.9 1.0 shard_map.70.z0.mine
  45.9 4.1 %collective-permute-start.10 = (bf16[528,1024]{1,0:T(8,128)(2,1)S(1)}, bf16[528,1024]{1,0:T(8,128)(2,1)S(1)}, u32[]{:S(2)}, u32[]{:S(2)}) collective-permute-start(bf16[528,1024]{1,0:T(8,128)(2,1)S(1)} %shard_map.70.z0.mine), channel_id=1, source_target_pairs={{0,24},{1,25},{2,26},{3,27},{4,28},{5,29},{6,30},{7,31},{8,0},{9,1... | collective-permute-start | bytes 3244040 | tf_op jit(solution)/shard_map/ppermute | solution.py:35
  50.1 1.8 collective-permute-start.12
  51.9 1.4 collective-permute-start.13
  53.4 1.9 collective-permute-start.15
  55.2 1.8 fusion.4
  57.0 1.8 fusion.80
  58.9 15.6 %collective-permute-done.12 = f16[256,2048]{1,0:T(8,128)(2,1)S(1)} collective-permute-done((f16[256,2048]{1,0:T(8,128)(2,1)S(1)}, f16[256,2048]{1,0:T(8,128)(2,1)S(1)}, u32[]{:S(2)}, u32[]{:S(2)}) %collective-permute-start.12) | collective-permute-done | bytes 1048608 | tf_op jit(solution)/shard_map/ppermute | solution.py:35
  75.8 3.3 %collective-permute-start.18 = (bf16[528,512]{1,0:T(8,128)(2,1)S(1)}, bf16[528,512]{1,0:T(8,128)(2,1)S(1)}, u32[]{:S(2)}, u32[]{:S(2)}) collective-permute-start(bf16[528,512]{1,0:T(8,128)(2,1)S(1)} %slice.127), channel_id=1, source_target_pairs={{0,24},{1,25},{2,26},{3,27},{4,28},{5,29},{6,30},{7,31},{8,0},{9,1... | collective-permute-start | bytes 1622024 | tf_op jit(solution)/shard_map/ppermute | solution.py:35
  79.1 2.4 %collective-permute-start.16 = (f16[256,2048]{1,0:T(8,128)(2,1)S(1)}, f16[256,2048]{1,0:T(8,128)(2,1)S(1)}, u32[]{:S(2)}, u32[]{:S(2)}) collective-permute-start(f16[256,2048]{1,0:T(8,128)(2,1)S(1)} %fusion.4), channel_id=1, source_target_pairs={{0,4},{1,5},{2,6},{3,7},{4,0},{5,1},{6,2},{7,3},{8,12},{9,13},{10,... | collective-permute-start | bytes 3145736 | tf_op jit(solution)/shard_map/ppermute | solution.py:35
  81.6 2.0 %collective-permute-start.14 = (bf16[2,512,768]{2,1,0:T(8,128)(2,1)S(1)}, bf16[2,512,768]{2,1,0:T(8,128)(2,1)S(1)}, u32[]{:S(2)}, u32[]{:S(2)}) collective-permute-start(bf16[2,512,768]{2,1,0:T(8,128)(2,1)S(1)} %copy-done.1), channel_id=1, source_target_pairs={{0,64},{1,65},{2,66},{3,67},{4,68},{5,69},{6,70},{7,71},{8,72},{9,... | collective-permute-start | bytes 4718600 | tf_op jit(solution)/shard_map/ppermute | solution.py:35
  83.5 1.0 shard_map.71
  84.5 1.0 fusion.61
  85.5 0.8 collective-permute-start.21
  86.3 1.8 fusion.58
  88.1 1.8 fusion.55
  90.0 1.8 fusion.52
  91.8 1.0 fusion.49
  92.8 1.0 fusion.46
  93.8 4.5 %shard_map.72.refs_10_ = f32[2,512,768]{2,1,0:T(8,128)S(1)} custom-call(s32[5]{0:T(128)S(1)} %stack.32.at, bf16[528,1024]{1,0:T(8,128)(2,1)S(1)} %shard_map.70.z0.mine, bf16[528,1024]{1,0:T(8,128)(2,1)S(1)} %collective-permute-done.10.z1.up, bf16[528,1024]{1,0:T(8,128)(2,1)S(1)} %collective-permute-done.11.z3.down, bf16[2,512,768]{2,1,0:T(8,128)(2,1)S(1)} %copy-done, ...), custom_call_target="tpu_custom_call" | custom-call | flops 1024 | bytes 1024 | tf_op jit(solution)/shard_map/pallas_call | solution.py:47
  98.3 5.4 %shard_map.73.refs_10_ = f32[2,512,768]{2,1,0:T(8,128)} custom-call(s32[5]{0:T(128)S(1)} %stack.32.at, bf16[528,1024]{1,0:T(8,128)(2,1)S(1)} %shard_map.70.z0.mine, bf16[528,1024]{1,0:T(8,128)(2,1)S(1)} %collective-permute-done.10.z1.up, bf16[528,1024]{1,0:T(8,128)(2,1)S(1)} %collective-permute-done.11.z3.down, bf16[2,512,768]{2,1,0:T(8,128)(2,1)S(1)} %copy-done.1, ...), custom_call_target="tpu_custom_call" | custom-call | flops 1024 | bytes 1024 | tf_op jit(solution)/shard_map/pallas_call | solution.py:47
  103.7 1.5 collective-permute-done.16
  105.2 7.3 %shard_map.74 = f32[2,512,768]{2,1,0:T(8,128)} custom-call(s32[5]{0:T(128)S(1)} %stack.32.at, bf16[528,1024]{1,0:T(8,128)(2,1)S(1)} %shard_map.70.z0.mine, bf16[528,1024]{1,0:T(8,128)(2,1)S(1)} %collective-permute-done.10.z1.up, bf16[528,1024]{1,0:T(8,128)(2,1)S(1)} %collective-permute-done.11.z3.down, ...), custom_call_target="tpu_custom_call" | custom-call | flops 1024 | bytes 1024 | tf_op jit(solution)/shard_map/pallas_call | solution.py:47
  112.5 0.7 shard_map.75
  113.7 3.1 %collective-permute-start.23 = (f16[256,1024]{1,0:T(8,128)(2,1)S(1)}, f16[256,1024]{1,0:T(8,128)(2,1)S(1)}, u32[]{:S(2)}, u32[]{:S(2)}) collective-permute-start(f16[256,1024]{1,0:T(8,128)(2,1)S(1)} %copy-done.4), channel_id=1, source_target_pairs={{0,24},{1,25},{2,26},{3,27},{4,28},{5,29},{6,30},{7,31},{8,0},{9,1... | collective-permute-start | bytes 1572872 | tf_op jit(solution)/shard_map/ppermute | solution.py:35
  116.8 1.8 collective-permute-start.24
  118.5 1.5 collective-permute-start.25
  120.0 0.8 multiply_add_fusion
  120.9 6.3 %collective-permute-done.22 = f16[256,1024]{1,0:T(8,128)(2,1)S(1)} collective-permute-done((f16[256,1024]{1,0:T(8,128)(2,1)S(1)}, f16[256,1024]{1,0:T(8,128)(2,1)S(1)}, u32[]{:S(2)}, u32[]{:S(2)}) %collective-permute-start.22) | collective-permute-done | bytes 524320 | tf_op jit(solution)/shard_map/ppermute | solution.py:35
  127.2 2.3 %collective-permute-start.26 = (f16[256,1024]{1,0:T(8,128)(2,1)S(1)}, f16[256,1024]{1,0:T(8,128)(2,1)S(1)}, u32[]{:S(2)}, u32[]{:S(2)}) collective-permute-start(f16[256,1024]{1,0:T(8,128)(2,1)S(1)} %fusion.46), channel_id=1, source_target_pairs={{0,4},{1,5},{2,6},{3,7},{4,0},{5,1},{6,2},{7,3},{8,12},{9,13},{10,... | collective-permute-start | bytes 1572872 | tf_op jit(solution)/shard_map/ppermute | solution.py:35
  129.7 2.2 %fusion.43 = f32[256,1024]{1,0:T(8,128)S(1)} fusion(bf16[256,1536]{1,0:T(8,128)(2,1)S(1)} %get-tuple-element.214, bf16[2048,1536]{1,0:T(8,128)(2,1)S(1)} %shard_map.67, f16[256,1024]{1,0:T(8,128)(2,1)} %collective-permute-done.21, f16[256,1024]{1,0:T(8,128)(2,1)S(1)} %collective-permute-done.23, f16[256,1024]{1,0:T(8,128)(2,1)S(1)} %collective-permute-done.22, ...), kind=kOutput, calls=%fused_computation.40 | convolution fusion | flops 807665664 | bytes 6565888 | tf_op jit(solution)/shard_map/dot_general | solution.py:39
  132.0 10.0 %collective-permute-done.26 = f16[256,1024]{1,0:T(8,128)(2,1)S(1)} collective-permute-done((f16[256,1024]{1,0:T(8,128)(2,1)S(1)}, f16[256,1024]{1,0:T(8,128)(2,1)S(1)}, u32[]{:S(2)}, u32[]{:S(2)}) %collective-permute-start.26) | collective-permute-done | bytes 524320 | tf_op jit(solution)/shard_map/ppermute | solution.py:35
  142.0 1.1 fusion.39
  143.4 3.2 %collective-permute-start.28 = (f16[64,3072]{1,0:T(8,128)(2,1)S(1)}, f16[64,3072]{1,0:T(8,128)(2,1)S(1)}, u32[]{:S(2)}, u32[]{:S(2)}) collective-permute-start(f16[64,3072]{1,0:T(8,128)(2,1)S(1)} %get-tuple-element.252), channel_id=1, source_target_pairs={{0,24},{1,25},{2,26},{3,27},{4,28},{5,29},{6,30},{7,31},{8,0},{9,1... | collective-permute-start | bytes 1179656 | tf_op jit(solution)/shard_map/ppermute | solution.py:35
  146.7 1.2 collective-permute-start.30
  147.9 14.5 %collective-permute-done.27 = f16[64,3072]{1,0:T(8,128)(2,1)S(1)} collective-permute-done((f16[64,3072]{1,0:T(8,128)(2,1)S(1)}, f16[64,3072]{1,0:T(8,128)(2,1)S(1)}, u32[]{:S(2)}, u32[]{:S(2)}) %collective-permute-start.27) | collective-permute-done | bytes 393248 | tf_op jit(solution)/shard_map/ppermute | solution.py:35
  162.4 1.6 collective-permute-start.31
  164.0 1.2 collective-permute-start.32
  165.5 3.3 %collective-permute-done.31.h2 = f32[64,1024]{1,0:T(8,128)S(1)} collective-permute-done((f32[64,1024]{1,0:T(8,128)S(1)}, f32[64,1024]{1,0:T(8,128)S(1)}, u32[]{:S(2)}, u32[]{:S(2)}) %collective-permute-start.31) | collective-permute-done | bytes 262176 | tf_op jit(solution)/shard_map/ppermute | solution.py:35
  168.8 3.1 %collective-permute-done.32.h3 = f32[64,1024]{1,0:T(8,128)S(1)} collective-permute-done((f32[64,1024]{1,0:T(8,128)S(1)}, f32[64,1024]{1,0:T(8,128)S(1)}, u32[]{:S(2)}, u32[]{:S(2)}) %collective-permute-start.32) | collective-permute-done | bytes 262176 | tf_op jit(solution)/shard_map/ppermute | solution.py:35
  172.2 5.4 %shard_map.77.refs_10_ = f32[2,512,768]{2,1,0:T(8,128)} custom-call(s32[5]{0:T(128)S(1)} %stack.32.at, bf16[528,1024]{1,0:T(8,128)(2,1)S(1)} %shard_map.70.z0.mine, bf16[528,1024]{1,0:T(8,128)(2,1)S(1)} %collective-permute-done.10.z1.up, bf16[528,1024]{1,0:T(8,128)(2,1)S(1)} %collective-permute-done.11.z3.down, ...), custom_call_target="tpu_custom_call", output_to_operand_aliasing={{}: (14, {})} | custom-call | flops 1024 | bytes 1024 | tf_op jit(solution)/shard_map/pallas_call | solution.py:47
  177.6 3.7 %collective-permute-done.34.got = f32[32,4096]{1,0:T(8,128)S(1)} collective-permute-done((f32[32,4096]{1,0:T(8,128)S(1)}, f32[32,4096]{1,0:T(8,128)S(1)}, u32[]{:S(2)}, u32[]{:S(2)}) %collective-permute-start.34) | collective-permute-done | bytes 524320 | tf_op jit(solution)/shard_map/ppermute | solution.py:35
  181.3 2.0 %collective-permute-start.35 = (f32[32,2048]{1,0:T(8,128)S(1)}, f32[32,2048]{1,0:T(8,128)S(1)}, u32[]{:S(2)}, u32[]{:S(2)}) collective-permute-start(f32[32,2048]{1,0:T(8,128)S(1)} %get-tuple-element.240), channel_id=1, source_target_pairs={{0,64},{1,65},{2,66},{3,67},{4,68},{5,69},{6,70},{7,71},{8,72},{9,... | collective-permute-start | bytes 786440 | tf_op jit(solution)/shard_map/ppermute | solution.py:35
  183.3 5.3 %shard_map.79 = f32[2,512,768]{2,1,0:T(8,128)} custom-call(s32[5]{0:T(128)S(1)} %stack.32.at, bf16[528,1024]{1,0:T(8,128)(2,1)S(1)} %shard_map.70.z0.mine, bf16[528,1024]{1,0:T(8,128)(2,1)S(1)} %collective-permute-done.10.z1.up, bf16[528,1024]{1,0:T(8,128)(2,1)S(1)} %collective-permute-done.11.z3.down, ...), custom_call_target="tpu_custom_call", output_to_operand_aliasing={{}: (14, {})} | custom-call | flops 1024 | bytes 1024 | tf_op jit(solution)/shard_map/pallas_call | solution.py:47
  188.6 0.6 collective-permute-done.35.got
  189.3 1.4 shard_map.80
  (67 shorter events, 4.5 us)
Async XLA Ops:
  0.6 13.1 %copy-start = (bf16[2,512,768]{2,1,0:T(8,128)(2,1)S(1)}, bf16[2,512,768]{2,1,0:T(8,128)(2,1)}, u32[]{:S(2)}) copy-start(bf16[2,512,768]{2,1,0:T(8,128)(2,1)} %refs_3_) | copy-start | bytes 4718596
  0.6 13.1 %copy-start.1 = (bf16[2,512,768]{2,1,0:T(8,128)(2,1)S(1)}, bf16[2,512,768]{2,1,0:T(8,128)(2,1)}, u32[]{:S(2)}) copy-start(bf16[2,512,768]{2,1,0:T(8,128)(2,1)} %refs_3_.2) | copy-start | bytes 4718596
  0.7 8.1 %collective-permute-start = (bf16[2,512,768]{2,1,0:T(8,128)(2,1)}, bf16[2,512,768]{2,1,0:T(8,128)(2,1)}, u32[]{:S(2)}, u32[]{:S(2)}) collective-permute-start(bf16[2,512,768]{2,1,0:T(8,128)(2,1)} %refs_3_), channel_id=1, source_target_pairs={{0,32},{1,33},{2,34},{3,35},{4,36},{5,37},{6,38},{7,39},{8,40},{9,... | collective-permute-start | bytes 4718600 | tf_op jit(solution)/shard_map/ppermute | solution.py:35
  0.7 8.1 %collective-permute-start.1 = (bf16[2,512,768]{2,1,0:T(8,128)(2,1)}, bf16[2,512,768]{2,1,0:T(8,128)(2,1)}, u32[]{:S(2)}, u32[]{:S(2)}) collective-permute-start(bf16[2,512,768]{2,1,0:T(8,128)(2,1)} %refs_3_.2), channel_id=1, source_target_pairs={{0,32},{1,33},{2,34},{3,35},{4,36},{5,37},{6,38},{7,39},{8,40},{9,... | collective-permute-start | bytes 4718600 | tf_op jit(solution)/shard_map/ppermute | solution.py:35
  1.2 7.5 %collective-permute-start.2 = (bf16[2,64,512]{2,1,0:T(8,128)(2,1)}, bf16[2,64,512]{2,1,0:T(8,128)(2,1)S(1)}, u32[]{:S(2)}, u32[]{:S(2)}) collective-permute-start(bf16[2,64,512]{2,1,0:T(8,128)(2,1)} %own.1), channel_id=1, source_target_pairs={{0,1},{1,0},{2,3},{3,2},{4,5},{5,4},{6,7},{7,6},{8,9},{9,8},{10,11... | collective-permute-start | bytes 393224 | tf_op jit(solution)/shard_map/ppermute | solution.py:35
  8.8 0.9 copy-start.2
  10.3 7.5 %collective-permute-start.3 = (bf16[2,2,80,128]{3,2,1,0:T(8,128)(2,1)S(1)}, bf16[2,2,80,128]{3,2,1,0:T(8,128)(2,1)S(1)}, u32[]{:S(2)}, u32[]{:S(2)}) collective-permute-start(bf16[2,2,80,128]{3,2,1,0:T(8,128)(2,1)S(1)} %get-tuple-element.131), channel_id=1, source_target_pairs={{0,32},{1,33},{2,34},{3,35},{4,36},{5,37},{6,38},{7,39},{8,40},{9,... | collective-permute-start | bytes 245768 | tf_op jit(solution)/shard_map/ppermute | solution.py:35
  10.4 7.5 %collective-permute-start.4 = (bf16[2,2,80,128]{3,2,1,0:T(8,128)(2,1)S(1)}, bf16[2,2,80,128]{3,2,1,0:T(8,128)(2,1)S(1)}, u32[]{:S(2)}, u32[]{:S(2)}) collective-permute-start(bf16[2,2,80,128]{3,2,1,0:T(8,128)(2,1)S(1)} %get-tuple-element.132), channel_id=1, source_target_pairs={{0,64},{1,65},{2,66},{3,67},{4,68},{5,69},{6,70},{7,71},{8,72},{9,... | collective-permute-start | bytes 245768 | tf_op jit(solution)/shard_map/ppermute | solution.py:35
  13.4 5.9 %collective-permute-start.5 = (bf16[2,2,80,128]{3,2,1,0:T(8,128)(2,1)S(1)}, bf16[2,2,80,128]{3,2,1,0:T(8,128)(2,1)S(1)}, u32[]{:S(2)}, u32[]{:S(2)}) collective-permute-start(bf16[2,2,80,128]{3,2,1,0:T(8,128)(2,1)S(1)} %get-tuple-element.133), channel_id=1, source_target_pairs={{0,96},{1,97},{2,98},{3,99},{4,100},{5,101},{6,102},{7,103},{8,104... | collective-permute-start | bytes 245768 | tf_op jit(solution)/shard_map/ppermute | solution.py:35
  20.0 24.9 %collective-permute-start.7 = (bf16[528,256]{1,0:T(8,128)(2,1)S(1)}, bf16[528,256]{1,0:T(8,128)(2,1)S(1)}, u32[]{:S(2)}, u32[]{:S(2)}) collective-permute-start(bf16[528,256]{1,0:T(8,128)(2,1)S(1)} %get-tuple-element.158.first), channel_id=1, source_target_pairs={{0,6},{1,7},{2,0},{3,1},{4,2},{5,3},{6,4},{7,5},{8,14},{9,15},{10,... | collective-permute-start | bytes 811016 | tf_op jit(solution)/shard_map/ppermute | solution.py:35
  22.8 22.1 %collective-permute-start.8 = (bf16[528,256]{1,0:T(8,128)(2,1)S(1)}, bf16[528,256]{1,0:T(8,128)(2,1)S(1)}, u32[]{:S(2)}, u32[]{:S(2)}) collective-permute-start(bf16[528,256]{1,0:T(8,128)(2,1)S(1)} %get-tuple-element.158.first), channel_id=1, source_target_pairs={{0,4},{1,5},{2,6},{3,7},{4,0},{5,1},{6,2},{7,3},{8,12},{9,13},{10,... | collective-permute-start | bytes 811016 | tf_op jit(solution)/shard_map/ppermute | solution.py:35
  23.6 21.3 %collective-permute-start.9 = (bf16[528,256]{1,0:T(8,128)(2,1)S(1)}, bf16[528,256]{1,0:T(8,128)(2,1)S(1)}, u32[]{:S(2)}, u32[]{:S(2)}) collective-permute-start(bf16[528,256]{1,0:T(8,128)(2,1)S(1)} %get-tuple-element.158.first), channel_id=1, source_target_pairs={{0,2},{1,3},{2,4},{3,5},{4,6},{5,7},{6,0},{7,1},{8,10},{9,11},{10,... | collective-permute-start | bytes 811016 | tf_op jit(solution)/shard_map/ppermute | solution.py:35
  24.6 20.3 %collective-permute-start.6 = (bf16[512,768]{1,0:T(8,128)(2,1)S(1)}, bf16[512,768]{1,0:T(8,128)(2,1)S(1)}, u32[]{:S(2)}, u32[]{:S(2)}) collective-permute-start(bf16[512,768]{1,0:T(8,128)(2,1)S(1)} %slice_bitcast_fusion.1), channel_id=1, source_target_pairs={{0,64},{1,65},{2,66},{3,67},{4,68},{5,69},{6,70},{7,71},{8,72},{9,... | collective-permute-start | bytes 2359304 | tf_op jit(solution)/shard_map/ppermute | solution.py:35
  45.9 28.8 %collective-permute-start.10 = (bf16[528,1024]{1,0:T(8,128)(2,1)S(1)}, bf16[528,1024]{1,0:T(8,128)(2,1)S(1)}, u32[]{:S(2)}, u32[]{:S(2)}) collective-permute-start(bf16[528,1024]{1,0:T(8,128)(2,1)S(1)} %shard_map.70.z0.mine), channel_id=1, source_target_pairs={{0,24},{1,25},{2,26},{3,27},{4,28},{5,29},{6,30},{7,31},{8,0},{9,1... | collective-permute-start | bytes 3244040 | tf_op jit(solution)/shard_map/ppermute | solution.py:35
  50.1 25.1 %collective-permute-start.11 = (bf16[528,1024]{1,0:T(8,128)(2,1)S(1)}, bf16[528,1024]{1,0:T(8,128)(2,1)S(1)}, u32[]{:S(2)}, u32[]{:S(2)}) collective-permute-start(bf16[528,1024]{1,0:T(8,128)(2,1)S(1)} %shard_map.70.z0.mine), channel_id=1, source_target_pairs={{0,8},{1,9},{2,10},{3,11},{4,12},{5,13},{6,14},{7,15},{8,16},{9,17... | collective-permute-start | bytes 3244040 | tf_op jit(solution)/shard_map/ppermute | solution.py:35
  50.1 24.4 %collective-permute-start.12 = (f16[256,2048]{1,0:T(8,128)(2,1)S(1)}, f16[256,2048]{1,0:T(8,128)(2,1)S(1)}, u32[]{:S(2)}, u32[]{:S(2)}) collective-permute-start(f16[256,2048]{1,0:T(8,128)(2,1)S(1)} %fusion.2), channel_id=1, source_target_pairs={{0,2},{1,3},{2,4},{3,5},{4,6},{5,7},{6,0},{7,1},{8,10},{9,11},{10,... | collective-permute-start | bytes 3145736 | tf_op jit(solution)/shard_map/ppermute | solution.py:35
  51.9 22.9 %collective-permute-start.13 = (f16[256,2048]{1,0:T(8,128)(2,1)S(1)}, f16[256,2048]{1,0:T(8,128)(2,1)S(1)}, u32[]{:S(2)}, u32[]{:S(2)}) collective-permute-start(f16[256,2048]{1,0:T(8,128)(2,1)S(1)} %fusion.3), channel_id=1, source_target_pairs={{0,6},{1,7},{2,0},{3,1},{4,2},{5,3},{6,4},{7,5},{8,14},{9,15},{10,... | collective-permute-start | bytes 3145736 | tf_op jit(solution)/shard_map/ppermute | solution.py:35
  53.4 21.8 %collective-permute-start.15 = (bf16[512,768]{1,0:T(8,128)(2,1)S(1)}, bf16[512,768]{1,0:T(8,128)(2,1)S(1)}, u32[]{:S(2)}, u32[]{:S(2)}) collective-permute-start(bf16[512,768]{1,0:T(8,128)(2,1)S(1)} %slice_bitcast_fusion), channel_id=1, source_target_pairs={{0,64},{1,65},{2,66},{3,67},{4,68},{5,69},{6,70},{7,71},{8,72},{9,... | collective-permute-start | bytes 2359304 | tf_op jit(solution)/shard_map/ppermute | solution.py:35
  75.1 6.4 %collective-permute-start.20 = (bf16[512,768]{1,0:T(8,128)(2,1)S(1)}, bf16[512,768]{1,0:T(8,128)(2,1)S(1)}, u32[]{:S(2)}, u32[]{:S(2)}) collective-permute-start(bf16[512,768]{1,0:T(8,128)(2,1)S(1)} %collective-permute-done.15.near_im.refs_7_), channel_id=1, source_target_pairs={{0,32},{1,33},{2,34},{3,35},{4,36},{5,37},{6,38},{7,39},{8,40},{9,... | collective-permute-start | bytes 2359304 | tf_op jit(solution)/shard_map/ppermute | solution.py:35
  75.2 8.4 %collective-permute-start.19 = (bf16[512,768]{1,0:T(8,128)(2,1)S(1)}, bf16[512,768]{1,0:T(8,128)(2,1)S(1)}, u32[]{:S(2)}, u32[]{:S(2)}) collective-permute-start(bf16[512,768]{1,0:T(8,128)(2,1)S(1)} %collective-permute-done.6.near_re.refs_6_), channel_id=1, source_target_pairs={{0,32},{1,33},{2,34},{3,35},{4,36},{5,37},{6,38},{7,39},{8,40},{9,... | collective-permute-start | bytes 2359304 | tf_op jit(solution)/shard_map/ppermute | solution.py:35
  75.7 28.0 %collective-permute-start.17 = (bf16[528,512]{1,0:T(8,128)(2,1)S(1)}, bf16[528,512]{1,0:T(8,128)(2,1)S(1)}, u32[]{:S(2)}, u32[]{:S(2)}) collective-permute-start(bf16[528,512]{1,0:T(8,128)(2,1)S(1)} %slice.126), channel_id=1, source_target_pairs={{0,8},{1,9},{2,10},{3,11},{4,12},{5,13},{6,14},{7,15},{8,16},{9,17... | collective-permute-start | bytes 1622024 | tf_op jit(solution)/shard_map/ppermute | solution.py:35
  75.8 27.9 %collective-permute-start.18 = (bf16[528,512]{1,0:T(8,128)(2,1)S(1)}, bf16[528,512]{1,0:T(8,128)(2,1)S(1)}, u32[]{:S(2)}, u32[]{:S(2)}) collective-permute-start(bf16[528,512]{1,0:T(8,128)(2,1)S(1)} %slice.127), channel_id=1, source_target_pairs={{0,24},{1,25},{2,26},{3,27},{4,28},{5,29},{6,30},{7,31},{8,0},{9,1... | collective-permute-start | bytes 1622024 | tf_op jit(solution)/shard_map/ppermute | solution.py:35
  79.1 26.1 %collective-permute-start.16 = (f16[256,2048]{1,0:T(8,128)(2,1)S(1)}, f16[256,2048]{1,0:T(8,128)(2,1)S(1)}, u32[]{:S(2)}, u32[]{:S(2)}) collective-permute-start(f16[256,2048]{1,0:T(8,128)(2,1)S(1)} %fusion.4), channel_id=1, source_target_pairs={{0,4},{1,5},{2,6},{3,7},{4,0},{5,1},{6,2},{7,3},{8,12},{9,13},{10,... | collective-permute-start | bytes 3145736 | tf_op jit(solution)/shard_map/ppermute | solution.py:35
  81.6 50.4 %collective-permute-start.14 = (bf16[2,512,768]{2,1,0:T(8,128)(2,1)S(1)}, bf16[2,512,768]{2,1,0:T(8,128)(2,1)S(1)}, u32[]{:S(2)}, u32[]{:S(2)}) collective-permute-start(bf16[2,512,768]{2,1,0:T(8,128)(2,1)S(1)} %copy-done.1), channel_id=1, source_target_pairs={{0,64},{1,65},{2,66},{3,67},{4,68},{5,69},{6,70},{7,71},{8,72},{9,... | collective-permute-start | bytes 4718600 | tf_op jit(solution)/shard_map/ppermute | solution.py:35
  85.5 19.7 %collective-permute-start.21 = (f16[256,1024]{1,0:T(8,128)(2,1)S(1)}, f16[256,1024]{1,0:T(8,128)(2,1)}, u32[]{:S(2)}, u32[]{:S(2)}) collective-permute-start(f16[256,1024]{1,0:T(8,128)(2,1)S(1)} %fusion.61), channel_id=1, source_target_pairs={{0,16},{1,17},{2,18},{3,19},{4,20},{5,21},{6,22},{7,23},{8,24},{9,... | collective-permute-start | bytes 1572872 | tf_op jit(solution)/shard_map/ppermute | solution.py:35
  112.5 1.0 copy-start.5
  112.5 1.2 copy-start.4
  112.5 4.3 %copy-start.3 = (f16[256,1024]{1,0:T(8,128)(2,1)S(1)}, f16[256,1024]{1,0:T(8,128)(2,1)}, u32[]{:S(2)}) copy-start(f16[256,1024]{1,0:T(8,128)(2,1)} %fusion.52) | copy-start | bytes 1572868
  113.5 13.6 %collective-permute-start.22 = (f16[256,1024]{1,0:T(8,128)(2,1)S(1)}, f16[256,1024]{1,0:T(8,128)(2,1)S(1)}, u32[]{:S(2)}, u32[]{:S(2)}) collective-permute-start(f16[256,1024]{1,0:T(8,128)(2,1)S(1)} %copy-done.5), channel_id=1, source_target_pairs={{0,8},{1,9},{2,10},{3,11},{4,12},{5,13},{6,14},{7,15},{8,16},{9,17... | collective-permute-start | bytes 1572872 | tf_op jit(solution)/shard_map/ppermute | solution.py:35
  113.7 16.0 %collective-permute-start.23 = (f16[256,1024]{1,0:T(8,128)(2,1)S(1)}, f16[256,1024]{1,0:T(8,128)(2,1)S(1)}, u32[]{:S(2)}, u32[]{:S(2)}) collective-permute-start(f16[256,1024]{1,0:T(8,128)(2,1)S(1)} %copy-done.4), channel_id=1, source_target_pairs={{0,24},{1,25},{2,26},{3,27},{4,28},{5,29},{6,30},{7,31},{8,0},{9,1... | collective-permute-start | bytes 1572872 | tf_op jit(solution)/shard_map/ppermute | solution.py:35
  116.8 15.2 %collective-permute-start.24 = (f16[256,1024]{1,0:T(8,128)(2,1)S(1)}, f16[256,1024]{1,0:T(8,128)(2,1)S(1)}, u32[]{:S(2)}, u32[]{:S(2)}) collective-permute-start(f16[256,1024]{1,0:T(8,128)(2,1)S(1)} %copy-done.3), channel_id=1, source_target_pairs={{0,2},{1,3},{2,4},{3,5},{4,6},{5,7},{6,0},{7,1},{8,10},{9,11},{10,... | collective-permute-start | bytes 1572872 | tf_op jit(solution)/shard_map/ppermute | solution.py:35
  118.5 13.4 %collective-permute-start.25 = (f16[256,1024]{1,0:T(8,128)(2,1)S(1)}, f16[256,1024]{1,0:T(8,128)(2,1)S(1)}, u32[]{:S(2)}, u32[]{:S(2)}) collective-permute-start(f16[256,1024]{1,0:T(8,128)(2,1)S(1)} %fusion.49), channel_id=1, source_target_pairs={{0,6},{1,7},{2,0},{3,1},{4,2},{5,3},{6,4},{7,5},{8,14},{9,15},{10,... | collective-permute-start | bytes 1572872 | tf_op jit(solution)/shard_map/ppermute | solution.py:35
  127.2 14.8 %collective-permute-start.26 = (f16[256,1024]{1,0:T(8,128)(2,1)S(1)}, f16[256,1024]{1,0:T(8,128)(2,1)S(1)}, u32[]{:S(2)}, u32[]{:S(2)}) collective-permute-start(f16[256,1024]{1,0:T(8,128)(2,1)S(1)} %fusion.46), channel_id=1, source_target_pairs={{0,4},{1,5},{2,6},{3,7},{4,0},{5,1},{6,2},{7,3},{8,12},{9,13},{10,... | collective-permute-start | bytes 1572872 | tf_op jit(solution)/shard_map/ppermute | solution.py:35
  143.3 19.1 %collective-permute-start.27 = (f16[64,3072]{1,0:T(8,128)(2,1)S(1)}, f16[64,3072]{1,0:T(8,128)(2,1)S(1)}, u32[]{:S(2)}, u32[]{:S(2)}) collective-permute-start(f16[64,3072]{1,0:T(8,128)(2,1)S(1)} %get-tuple-element.250), channel_id=1, source_target_pairs={{0,8},{1,9},{2,10},{3,11},{4,12},{5,13},{6,14},{7,15},{8,16},{9,17... | collective-permute-start | bytes 1179656 | tf_op jit(solution)/shard_map/ppermute | solution.py:35
  143.4 20.6 %collective-permute-start.28 = (f16[64,3072]{1,0:T(8,128)(2,1)S(1)}, f16[64,3072]{1,0:T(8,128)(2,1)S(1)}, u32[]{:S(2)}, u32[]{:S(2)}) collective-permute-start(f16[64,3072]{1,0:T(8,128)(2,1)S(1)} %get-tuple-element.252), channel_id=1, source_target_pairs={{0,24},{1,25},{2,26},{3,27},{4,28},{5,29},{6,30},{7,31},{8,0},{9,1... | collective-permute-start | bytes 1179656 | tf_op jit(solution)/shard_map/ppermute | solution.py:35
  146.6 18.6 %collective-permute-start.29 = (f16[64,3072]{1,0:T(8,128)(2,1)S(1)}, f16[64,3072]{1,0:T(8,128)(2,1)S(1)}, u32[]{:S(2)}, u32[]{:S(2)}) collective-permute-start(f16[64,3072]{1,0:T(8,128)(2,1)S(1)} %get-tuple-element.251), channel_id=1, source_target_pairs={{0,16},{1,17},{2,18},{3,19},{4,20},{5,21},{6,22},{7,23},{8,24},{9,... | collective-permute-start | bytes 1179656 | tf_op jit(solution)/shard_map/ppermute | solution.py:35
  146.6 25.6 %collective-permute-start.33 = (bf16[2,512,768]{2,1,0:T(8,128)(2,1)S(1)}, bf16[2,512,768]{2,1,0:T(8,128)(2,1)S(1)}, u32[]{:S(2)}, u32[]{:S(2)}) collective-permute-start(bf16[2,512,768]{2,1,0:T(8,128)(2,1)S(1)} %collective-permute-done.14.refs_6_.refs_7_), channel_id=1, source_target_pairs={{0,32},{1,33},{2,34},{3,35},{4,36},{5,37},{6,38},{7,39},{8,40},{9,... | collective-permute-start | bytes 4718600 | tf_op jit(solution)/shard_map/ppermute | solution.py:35
  146.7 18.8 %collective-permute-start.30 = (f32[64,1024]{1,0:T(8,128)S(1)}, f32[64,1024]{1,0:T(8,128)S(1)}, u32[]{:S(2)}, u32[]{:S(2)}) collective-permute-start(f32[64,1024]{1,0:T(8,128)S(1)} %get-tuple-element.255), channel_id=1, source_target_pairs={{0,2},{1,3},{2,4},{3,5},{4,6},{5,7},{6,0},{7,1},{8,10},{9,11},{10,... | collective-permute-start | bytes 786440 | tf_op jit(solution)/shard_map/ppermute | solution.py:35
  162.4 6.4 %collective-permute-start.31 = (f32[64,1024]{1,0:T(8,128)S(1)}, f32[64,1024]{1,0:T(8,128)S(1)}, u32[]{:S(2)}, u32[]{:S(2)}) collective-permute-start(f32[64,1024]{1,0:T(8,128)S(1)} %get-tuple-element.254), channel_id=1, source_target_pairs={{0,6},{1,7},{2,0},{3,1},{4,2},{5,3},{6,4},{7,5},{8,14},{9,15},{10,... | collective-permute-start | bytes 786440 | tf_op jit(solution)/shard_map/ppermute | solution.py:35
  164.0 7.9 %collective-permute-start.32 = (f32[64,1024]{1,0:T(8,128)S(1)}, f32[64,1024]{1,0:T(8,128)S(1)}, u32[]{:S(2)}, u32[]{:S(2)}) collective-permute-start(f32[64,1024]{1,0:T(8,128)S(1)} %get-tuple-element.253), channel_id=1, source_target_pairs={{0,4},{1,5},{2,6},{3,7},{4,0},{5,1},{6,2},{7,3},{8,12},{9,13},{10,... | collective-permute-start | bytes 786440 | tf_op jit(solution)/shard_map/ppermute | solution.py:35
  172.0 9.3 %collective-permute-start.34 = (f32[32,4096]{1,0:T(8,128)S(1)}, f32[32,4096]{1,0:T(8,128)S(1)}, u32[]{:S(2)}, u32[]{:S(2)}) collective-permute-start(f32[32,4096]{1,0:T(8,128)S(1)} %get-tuple-element.231), channel_id=1, source_target_pairs={{0,1},{1,0},{2,3},{3,2},{4,5},{5,4},{6,7},{7,6},{8,9},{9,8},{10,11... | collective-permute-start | bytes 1572872 | tf_op jit(solution)/shard_map/ppermute | solution.py:35
  181.3 8.0 %collective-permute-start.35 = (f32[32,2048]{1,0:T(8,128)S(1)}, f32[32,2048]{1,0:T(8,128)S(1)}, u32[]{:S(2)}, u32[]{:S(2)}) collective-permute-start(f32[32,2048]{1,0:T(8,128)S(1)} %get-tuple-element.240), channel_id=1, source_target_pairs={{0,64},{1,65},{2,66},{3,67},{4,68},{5,69},{6,70},{7,71},{8,72},{9,... | collective-permute-start | bytes 786440 | tf_op jit(solution)/shard_map/ppermute | solution.py:35

commit v5 on v4

--- a/solution.py
+++ b/solution.py
@@ -136,8 +136,10 @@
                     out[base + 256:base + 288, 768:1536] = -re
 
 
-def left_kernel(both, at, near_re, near_im, other_re, other_im, *outs):
-    mz, mx, y_lo, y_hi, core = where_am_i(at)
+def left_kernel(both, at, *refs):
+    mz, mx, y_lo, y_hi, core = where_am_i(at)
+    pieces = 2 if both else 1
+    nears, others, outs = refs[:pieces], refs[pieces:2 * pieces], refs[2 * pieces:]
     for dz in range(4):
         z = (mz + dz) & 3
         is_near = (z >> 1) == core
@@ -146,27 +148,38 @@
             for dy in range(2):
                 rows = pl.ds(pl.multiple_of((z & 1) * 256 + x * 64 + (y_lo ^ dy) * 32, 32), 32)
                 by_x, by_z = dz * 64 + dy * 32, dx * 64 + dy * 32
-                for c, (near, other) in enumerate(((near_re, other_re), (near_im, other_im))):
-                    value = jnp.where(is_near, near[rows, :], other[rows, :])
-                    outs[dx][by_x:by_x + 32, c * 768:c * 768 + 768] = value
-                    if both:
-                        outs[4 + dz][by_z:by_z + 32, c * 768:c * 768 + 768] = value
-
-
-def whole_left_kernel(both, at, near, other, *outs):
-    left_kernel(both, at, near.at[0], near.at[1], other.at[0], other.at[1], *outs)
-
-
-def rotate_kernel(early, at, z0, z1, z3, *refs):
+                for c in range(2):
+                    base = c * 768
+                    for near, other in zip(nears, others):
+                        value = jnp.where(is_near, near[c, rows, :], other[c, rows, :])
+                        cols = slice(base, base + value.shape[1])
+                        base += value.shape[1]
+                        outs[dx][by_x:by_x + 32, cols] = value
+                        if both:
+                            outs[4 + dz][by_z:by_z + 32, cols] = value
+
+
+def planes(refs):
+    return lambda c, rows: refs[c][rows, :]
+
+
+def columns(refs):
+    return lambda c, rows: jnp.concatenate([r[c, rows, :] for r in refs], axis=1)
+
+
+def rotate_kernel(early, split, at, z0, z1, z3, *refs):
     mz, mx, y_lo, y_hi, core = where_am_i(at)
     out = refs[-1]
     if early:
-        pairs = ((y_hi, refs[0:2], refs[2:4], ((0, z0), (1, z1), (3, z3))),)
+        near, other = planes(refs[0:2]), planes(refs[2:4])
+        pairs = ((y_hi, near, other, ((0, z0), (1, z1), (3, z3))),)
         total = None
     else:
         far0, far1, acc = refs[0], refs[1], refs[10]
-        pairs = ((y_hi, refs[2:4], refs[4:6], ((2, None),)),
-                 (1 - y_hi, refs[6:8], refs[8:10], ((0, z0), (1, z1), (2, None), (3, z3))))
+        near, other = planes(refs[2:4]), planes(refs[4:6])
+        cross = (columns if split else planes)(refs[6:8]), (columns if split else planes)(refs[8:10])
+        pairs = ((y_hi, near, other, ((2, None),)),
+                 (1 - y_hi, *cross, ((0, z0), (1, z1), (2, None), (3, z3))))
         total = jnp.concatenate([acc[0], acc[1]], axis=0)
     for h, near, other, pieces in pairs:
         for dz, piece in pieces:
@@ -184,8 +197,8 @@
                 jnp.concatenate([im, re], axis=1),
             ], axis=0)
             right = jnp.concatenate([
-                jnp.where(is_near, near[0][rows, :], other[0][rows, :]),
-                jnp.where(is_near, near[1][rows, :], other[1][rows, :]),
+                jnp.where(is_near, near(0, rows), other(0, rows)),
+                jnp.where(is_near, near(1, rows), other(1, rows)),
             ], axis=0)
             term = jnp.dot(left, right, preferred_element_type=jnp.float32)
             total = term if total is None else total + term
@@ -208,7 +221,7 @@
         args.append(acc)
         specs.append(tile)
     return call(
-        functools.partial(rotate_kernel, acc is None),
+        functools.partial(rotate_kernel, acc is None, isinstance(blocks[-1], list)),
         jax.ShapeDtypeStruct((2, 512, 768), jnp.float32),
         *args,
         limit=20 if acc is None else 32,
@@ -260,10 +273,10 @@
     mz, mx, y_lo = ga >> 3, (ga >> 1) & 3, ga & 1
     at = jnp.stack([mz, mx, y_lo, y_hi, core]).astype(jnp.int32)
 
-    def lefts(first, second, both):
-        sizes = [256] * (8 if both else 4)
-        return call(functools.partial(left_kernel, both), [jax.ShapeDtypeStruct((n, 1536), jnp.bfloat16) for n in sizes],
-                    at, *first, *second, in_specs=[SMEM] + [VMEM] * 4, out_specs=[VMEM] * len(sizes))
+    def lefts(both, *blocks):
+        count = 8 if both else 4
+        return call(functools.partial(left_kernel, both), [jax.ShapeDtypeStruct((256, 1536), jnp.bfloat16)] * count,
+                    at, *blocks, in_specs=[SMEM] + [VMEM] * len(blocks), out_specs=[VMEM] * count)
 
     def for_peer(left, operand, factor):
         return (dot_rows(left, operand) * factor).astype(jnp.float16)
@@ -287,8 +300,7 @@
     got = [sent[0], move(sent[1], core=1), move(sent[2], y_hi=1), move(sent[3], core=1, y_hi=1)]
     right = call(right_kernel, jax.ShapeDtypeStruct((2048, 1536), jnp.bfloat16), at, psi, psi_mate,
                  after(hpsi, sent[0]), hpsi_mate, limit=32, in_specs=[SMEM] + [VMEM] * 4, out_specs=VMEM)
-    near_left = call(functools.partial(whole_left_kernel, False), [jax.ShapeDtypeStruct((256, 1536), jnp.bfloat16)] * 4,
-                     at, after(psi, right), psi_mate, in_specs=[SMEM, VMEM, VMEM], out_specs=[VMEM] * 4)
+    near_left = lefts(False, after(psi, right), psi_mate)
     psi, hpsi, got, right, near_left = fence((psi, hpsi, got, right, near_left))
 
     turned, scale = call(turn_kernel, [jax.ShapeDtypeStruct((528, 256), jnp.bfloat16),
@@ -296,11 +308,11 @@
                          in_specs=[SMEM] + [VMEM] * 4, out_specs=[VMEM] * 2)
     scale = scale[0:1]
     scale_h, scale_s = scale[:, 0:1024], scale[:, 1024:2048]
-    cross_re = move(psi[0], y_hi=1)
+    cross_a = move(psi[:, :, 0:256], y_hi=1)
     xs = [turned, move(turned, dx=-1), move(turned, dx=2), move(turned, dx=1)]
     near_1 = for_peer(after(near_left[1], turned), right, scale)
     near_3 = for_peer(after(near_left[3], near_1), right, scale)
-    psi, hpsi, cross_re, near_1, near_3, right = fence((psi, hpsi, cross_re, near_1, near_3, right))
+    psi, hpsi, cross_a, near_1, near_3, right = fence((psi, hpsi, cross_a, near_1, near_3, right))
     xs, right = fence((xs, right))
 
     mine = call(merge_kernel, jax.ShapeDtypeStruct((528, 1024), jnp.bfloat16), at, *xs,
@@ -308,20 +320,20 @@
                 scratch_shapes=[pltpu.VMEM((4, 528, 256), jnp.bfloat16)])
     near_got = [move(near_1, dx=1), move(near_3, dx=3)]
     up, down = move(mine, dz=-1), move(mine, dz=1)
-    cross_im = move(psi[1], y_hi=1)
+    cross_b = move(psi[:, :, 256:768], y_hi=1)
     near_2 = for_peer(after(near_left[2], mine), right, scale)
     near_own = dot_rows(after(near_left[0], near_2), right)
-    hpsi, cross_re, mine, up, down, near_got, near_2, near_own, right = fence(
-        (hpsi, cross_re, mine, up, down, near_got, near_2, near_own, right))
-    cross_im, near_2, up, down = fence((cross_im, near_2, up, down))
-
-    mate_re, mate_im = move(cross_re, core=1), move(cross_im, core=1)
+    hpsi, cross_a, mine, up, down, near_got, near_2, near_own, right = fence(
+        (hpsi, cross_a, mine, up, down, near_got, near_2, near_own, right))
+    cross_b, near_2, up, down = fence((cross_b, near_2, up, down))
+
+    mate_a, mate_b = move(cross_a, core=1), move(cross_b, core=1)
     near_got.append(move(near_2, dx=2))
     down_half, up_half = down[:, 0:512], up[:, 512:1024]
     far0, far1 = move(down_half, dz=1), move(up_half, dz=-1)
     hpsi_cross = move(hpsi, y_hi=1)
-    psi_cross, psi_cross_mate = [cross_re, cross_im], [mate_re, mate_im]
-    away_left = lefts(psi_cross, psi_cross_mate, True)
+    psi_cross, psi_cross_mate = [cross_a, cross_b], [mate_a, mate_b]
+    away_left = lefts(True, *psi_cross, *psi_cross_mate)
     right_h, right_s = right[0:1024], right[1024:2048]
     h_2 = for_peer(away_left[6], right_h, scale_h)
     got_h = [move(h_2, dz=2)]
@@ -342,18 +354,19 @@
     rotated_psi = rotate(at, coef, [psi, psi_mate, psi_cross, psi_cross_mate], psi_near)
     factors = call(factor_kernel, jax.ShapeDtypeStruct((16, 2048), jnp.float32), after(at, rotated_psi), *xs[1:], mine, up,
                    far0, down, in_specs=[SMEM] + [VMEM] * 7, out_specs=VMEM)
+    hpsi_cross, got_h, got_s, near_got, near_own, rotated_psi, factors, right = fence(
+        (hpsi_cross, got_h, got_s, near_got, near_own, rotated_psi, factors, right))
+
+    right_h, right_s = right[0:1024], right[1024:2048]
     factor = [factors[n:n + 1] for n in range(10)]
-    near_total = near_own
+    got_h = [got_h[1], got_h[2], got_h[0]]
+    away_h = gathered(away_left[4], right_h, [f[:, 0:1024] for f in factor[3:6]], got_h)
+    by_x = [away_h[0:64]] + [move(away_h[d * 64:d * 64 + 64], dx=d) for d in (1, 3, 2)]
+    near_total = after(near_own, away_h)
     for n, g in enumerate(near_got):
         near_total = near_total + g.astype(jnp.float32) * factor[n]
-    got_h = [got_h[1], got_h[2], got_h[0]]
-    away_h = gathered(after(away_left[4], near_total), right_h, [f[:, 0:1024] for f in factor[3:6]], got_h)
-    hpsi_cross, away_h, got_s, near_total, rotated_psi, right_s = fence(
-        (hpsi_cross, away_h, got_s, near_total, rotated_psi, right_s))
-
+    away_s = gathered(after(away_left[0], near_total), right_s, [f[:, 1024:2048] for f in factor[0:3]], got_s)
     hpsi_cross_mate = move(hpsi_cross, core=1)
-    by_x = [away_h[0:64]] + [move(away_h[d * 64:d * 64 + 64], dx=d) for d in (1, 3, 2)]
-    away_s = gathered(away_left[0], right_s, [f[:, 1024:2048] for f in factor[0:3]], got_s)
     by_z = jnp.concatenate([near_total, away_s], axis=1)
     factor = [jnp.concatenate([f, f[:, 1024:2048]], axis=1) for f in factor[6:10]]
     by_z = [by_z[0:64]] + [move((by_z[d * 64:d * 64 + 64] * factor[0]).astype(jnp.float16), dz=d) for d in (1, 3, 2)]

time: 191 us -> 185 us (0.969)
  waiting for transfers between devices: 75.5 us -> 68.3 us
    ppermute x36, waiting for transfers between devices: 75.5 us -> 68.3 us  [move(): return lax.ppermute(value, ('band', 'ga'), pairs)]
  transfers between devices with their start and end apart: 36 -> 36, of which waited for: 13 -> 15; matrix products, arithmetic and copies ran while one was open for 13% -> 13% of each run, Pallas kernels for 18% -> 18%
where the time goes in v5:
time: 185 us; the launch traced here: 184 us
  waiting for transfers between devices  68.3 us (37%)
  starting transfers between devices  48.1 us (26%)
  Pallas kernels  37.4 us (20%)
  matrix products  20.9 us (11%)
  other arithmetic  7.12 us (4%)
    ppermute x36, waiting for transfers between devices, move(): return lax.ppermute(value, ('band', 'ga'), pairs)  68.3 us
    ppermute x36, starting transfers between devices, move(): return lax.ppermute(value, ('band', 'ga'), pairs)  48.1 us
    pallas_call x15, Pallas kernels, call(): pl.pallas_call(kernel, out_shape=outs, compiler_params=pltpu.CompilerPara...  37.4 us
    dot_general x12, matrix products, dot_rows(): lax.dot_general(left, right, (((1,), (1,)), ((), ())), preferred_element_...  20.9 us
  transfers between devices with their start and end apart: 36, of which 15 were waited for; matrix products, arithmetic and copies ran while one was open for 13% of the time, Pallas kernels for 18%

profile of v5, /device:TPU:0, one launch (start us, length us, event | category | flops | bytes accessed | tf_op | source)
XLA Modules:
  0.0 184.1 jit_solution(4076415867453665237)
XLA Ops:
  1.2 1.7 collective-permute-start.2
  2.9 2.2 %abs_reduce_fusion.1 = bf16[]{:T(256)} fusion(bf16[2,512,768]{2,1,0:T(8,128)(2,1)} %refs_3_), kind=kLoop, calls=%fused_computation.30 | loop fusion | flops 1572863 | bytes 1572866 | tf_op jit(solution)/shard_map/reduce_max | solution.py:292
  5.1 2.2 %abs_reduce_fusion = bf16[]{:T(256)} fusion(bf16[2,512,768]{2,1,0:T(8,128)(2,1)} %refs_3_.2), kind=kLoop, calls=%fused_computation.29 | loop fusion | flops 1572863 | bytes 1572866 | tf_op jit(solution)/shard_map/reduce_max | solution.py:292
  7.5 1.3 maximum_convert_fusion.largest
  8.8 0.9 copy-done.2
  9.7 0.6 shard_map.66
  10.4 3.0 %collective-permute-start.4 = (bf16[2,2,80,128]{3,2,1,0:T(8,128)(2,1)S(1)}, bf16[2,2,80,128]{3,2,1,0:T(8,128)(2,1)S(1)}, u32[]{:S(2)}, u32[]{:S(2)}) collective-permute-start(bf16[2,2,80,128]{3,2,1,0:T(8,128)(2,1)S(1)} %get-tuple-element.139), channel_id=1, source_target_pairs={{0,64},{1,65},{2,66},{3,67},{4,68},{5,69},{6,70},{7,71},{8,72},{9,... | collective-permute-start | bytes 245768 | tf_op jit(solution)/shard_map/ppermute | solution.py:35
  13.8 2.3 %shard_map.67 = bf16[2048,1536]{1,0:T(8,128)(2,1)S(1)} custom-call(s32[5]{0:T(128)S(1)} %stack.32.at, bf16[2,512,768]{2,1,0:T(8,128)(2,1)S(1)} %copy-done.1, bf16[2,512,768]{2,1,0:T(8,128)(2,1)} %collective-permute-done.psi_mate.refs_1_.refs_2_.refs_3_.refs_4_.refs_5_, bf16[2,512,768]{2,1,0:T(8,128)(2,1)S(1)} %copy-done, ...), custom_call_target="tpu_custom_call" | custom-call | flops 1024 | bytes 1024 | tf_op jit(solution)/shard_map/pallas_call | solution.py:47
  16.1 1.8 shard_map.68
  17.9 1.4 collective-permute-done.5.fourth
  19.3 0.7 shard_map.69
  20.0 2.8 %collective-permute-start.7 = (bf16[528,256]{1,0:T(8,128)(2,1)S(1)}, bf16[528,256]{1,0:T(8,128)(2,1)S(1)}, u32[]{:S(2)}, u32[]{:S(2)}) collective-permute-start(bf16[528,256]{1,0:T(8,128)(2,1)S(1)} %get-tuple-element.165.first), channel_id=1, source_target_pairs={{0,6},{1,7},{2,0},{3,1},{4,2},{5,3},{6,4},{7,5},{8,14},{9,15},{10,... | collective-permute-start | bytes 811016 | tf_op jit(solution)/shard_map/ppermute | solution.py:35
  22.8 0.8 collective-permute-start.8
  23.6 0.9 collective-permute-start.9
  24.5 1.8 fusion.4
  26.4 1.7 collective-permute-start.6
  28.1 1.8 fusion.5
  29.9 11.2 %collective-permute-done.6.refs_0_.refs_6_ = bf16[2,512,256]{2,1,0:T(8,128)(2,1)S(1)} collective-permute-done((bf16[2,512,256]{2,1,0:T(8,128)(2,1)S(1)}, bf16[2,512,256]{2,1,0:T(8,128)(2,1)S(1)}, u32[]{:S(2)}, u32[]{:S(2)}) %collective-permute-start.6) | collective-permute-done | bytes 524320 | tf_op jit(solution)/shard_map/ppermute | solution.py:35
  41.1 1.0 shard_map.70.z0.mine
  42.1 4.1 %collective-permute-start.10 = (bf16[528,1024]{1,0:T(8,128)(2,1)S(1)}, bf16[528,1024]{1,0:T(8,128)(2,1)S(1)}, u32[]{:S(2)}, u32[]{:S(2)}) collective-permute-start(bf16[528,1024]{1,0:T(8,128)(2,1)S(1)} %shard_map.70.z0.mine), channel_id=1, source_target_pairs={{0,24},{1,25},{2,26},{3,27},{4,28},{5,29},{6,30},{7,31},{8,0},{9,1... | collective-permute-start | bytes 3244040 | tf_op jit(solution)/shard_map/ppermute | solution.py:35
  46.3 1.8 collective-permute-start.12
  48.1 1.4 collective-permute-start.13
  49.6 1.9 %collective-permute-start.15 = (bf16[2,512,512]{2,1,0:T(8,128)(2,1)S(1)}, bf16[2,512,512]{2,1,0:T(8,128)(2,1)S(1)}, u32[]{:S(2)}, u32[]{:S(2)}) collective-permute-start(bf16[2,512,512]{2,1,0:T(8,128)(2,1)S(1)} %slice.125), channel_id=1, source_target_pairs={{0,64},{1,65},{2,66},{3,67},{4,68},{5,69},{6,70},{7,71},{8,72},{9,... | collective-permute-start | bytes 3145736 | tf_op jit(solution)/shard_map/ppermute | solution.py:35
  51.4 1.8 fusion.6
  53.3 1.8 %fusion.89 = f32[256,2048]{1,0:T(8,128)S(1)} fusion(bf16[256,1536]{1,0:T(8,128)(2,1)S(1)} %get-tuple-element.175, bf16[2048,1536]{1,0:T(8,128)(2,1)S(1)} %shard_map.67), kind=kOutput, calls=%fused_computation.71 | convolution fusion | flops 1610612736 | bytes 9175040 | tf_op jit(solution)/shard_map/dot_general | solution.py:39
  55.1 15.5 %collective-permute-done.12 = f16[256,2048]{1,0:T(8,128)(2,1)S(1)} collective-permute-done((f16[256,2048]{1,0:T(8,128)(2,1)S(1)}, f16[256,2048]{1,0:T(8,128)(2,1)S(1)}, u32[]{:S(2)}, u32[]{:S(2)}) %collective-permute-start.12) | collective-permute-done | bytes 1048608 | tf_op jit(solution)/shard_map/ppermute | solution.py:35
  71.3 2.4 %collective-permute-done.15.refs_1_.refs_7_ = bf16[2,512,512]{2,1,0:T(8,128)(2,1)S(1)} collective-permute-done((bf16[2,512,512]{2,1,0:T(8,128)(2,1)S(1)}, bf16[2,512,512]{2,1,0:T(8,128)(2,1)S(1)}, u32[]{:S(2)}, u32[]{:S(2)}) %collective-permute-start.15) | collective-permute-done | bytes 1048608 | tf_op jit(solution)/shard_map/ppermute | solution.py:35
  74.5 3.3 %collective-permute-start.18 = (bf16[528,512]{1,0:T(8,128)(2,1)S(1)}, bf16[528,512]{1,0:T(8,128)(2,1)S(1)}, u32[]{:S(2)}, u32[]{:S(2)}) collective-permute-start(bf16[528,512]{1,0:T(8,128)(2,1)S(1)} %slice.127), channel_id=1, source_target_pairs={{0,24},{1,25},{2,26},{3,27},{4,28},{5,29},{6,30},{7,31},{8,0},{9,1... | collective-permute-start | bytes 1622024 | tf_op jit(solution)/shard_map/ppermute | solution.py:35
  77.7 1.2 collective-permute-start.16
  79.0 1.9 %collective-permute-start.14 = (bf16[2,512,768]{2,1,0:T(8,128)(2,1)S(1)}, bf16[2,512,768]{2,1,0:T(8,128)(2,1)S(1)}, u32[]{:S(2)}, u32[]{:S(2)}) collective-permute-start(bf16[2,512,768]{2,1,0:T(8,128)(2,1)S(1)} %copy-done), channel_id=1, source_target_pairs={{0,64},{1,65},{2,66},{3,67},{4,68},{5,69},{6,70},{7,71},{8,72},{9,... | collective-permute-start | bytes 4718600 | tf_op jit(solution)/shard_map/ppermute | solution.py:35
  80.9 1.0 shard_map.71
  81.9 1.0 fusion.70
  82.9 1.4 collective-permute-start.21
  84.3 1.8 fusion.67
  86.1 1.8 fusion.64
  87.9 1.8 fusion.61
  89.7 1.8 fusion.58
  91.5 1.8 fusion.55
  93.3 4.5 %shard_map.72.refs_10_ = f32[2,512,768]{2,1,0:T(8,128)S(1)} custom-call(s32[5]{0:T(128)S(1)} %stack.32.at, bf16[528,1024]{1,0:T(8,128)(2,1)S(1)} %shard_map.70.z0.mine, bf16[528,1024]{1,0:T(8,128)(2,1)S(1)} %collective-permute-done.10.z1.up, bf16[528,1024]{1,0:T(8,128)(2,1)S(1)} %collective-permute-done.11.z3.down, bf16[2,512,768]{2,1,0:T(8,128)(2,1)S(1)} %copy-done.1, ...), custom_call_target="tpu_custom_call" | custom-call | flops 1024 | bytes 1024 | tf_op jit(solution)/shard_map/pallas_call | solution.py:47
  97.8 5.4 %shard_map.73.refs_10_ = f32[2,512,768]{2,1,0:T(8,128)} custom-call(s32[5]{0:T(128)S(1)} %stack.32.at, bf16[528,1024]{1,0:T(8,128)(2,1)S(1)} %shard_map.70.z0.mine, bf16[528,1024]{1,0:T(8,128)(2,1)S(1)} %collective-permute-done.10.z1.up, bf16[528,1024]{1,0:T(8,128)(2,1)S(1)} %collective-permute-done.11.z3.down, bf16[2,512,768]{2,1,0:T(8,128)(2,1)S(1)} %copy-done, ...), custom_call_target="tpu_custom_call" | custom-call | flops 1024 | bytes 1024 | tf_op jit(solution)/shard_map/pallas_call | solution.py:47
  103.8 0.9 collective-permute-start.22
  104.7 2.3 %collective-permute-start.23 = (f16[256,1024]{1,0:T(8,128)(2,1)}, f16[256,1024]{1,0:T(8,128)(2,1)}, u32[]{:S(2)}, u32[]{:S(2)}) collective-permute-start(f16[256,1024]{1,0:T(8,128)(2,1)} %fusion.64), channel_id=1, source_target_pairs={{0,24},{1,25},{2,26},{3,27},{4,28},{5,29},{6,30},{7,31},{8,0},{9,1... | collective-permute-start | bytes 1572872 | tf_op jit(solution)/shard_map/ppermute | solution.py:35
  107.6 2.6 %collective-permute-start.25 = (f16[256,1024]{1,0:T(8,128)(2,1)}, f16[256,1024]{1,0:T(8,128)(2,1)S(1)}, u32[]{:S(2)}, u32[]{:S(2)}) collective-permute-start(f16[256,1024]{1,0:T(8,128)(2,1)} %fusion.58), channel_id=1, source_target_pairs={{0,6},{1,7},{2,0},{3,1},{4,2},{5,3},{6,4},{7,5},{8,14},{9,15},{10,... | collective-permute-start | bytes 1572872 | tf_op jit(solution)/shard_map/ppermute | solution.py:35
  110.3 5.7 %collective-permute-done.14.refs_6_.refs_7_ = bf16[2,512,768]{2,1,0:T(8,128)(2,1)S(1)} collective-permute-done((bf16[2,512,768]{2,1,0:T(8,128)(2,1)S(1)}, bf16[2,512,768]{2,1,0:T(8,128)(2,1)S(1)}, u32[]{:S(2)}, u32[]{:S(2)}) %collective-permute-start.14) | collective-permute-done | bytes 1572896 | tf_op jit(solution)/shard_map/ppermute | solution.py:35
  116.0 2.3 %collective-permute-start.26 = (f16[256,1024]{1,0:T(8,128)(2,1)}, f16[256,1024]{1,0:T(8,128)(2,1)S(1)}, u32[]{:S(2)}, u32[]{:S(2)}) collective-permute-start(f16[256,1024]{1,0:T(8,128)(2,1)} %fusion.55), channel_id=1, source_target_pairs={{0,4},{1,5},{2,6},{3,7},{4,0},{5,1},{6,2},{7,3},{8,12},{9,13},{10,... | collective-permute-start | bytes 1572872 | tf_op jit(solution)/shard_map/ppermute | solution.py:35
  118.3 7.3 %shard_map.74 = f32[2,512,768]{2,1,0:T(8,128)} custom-call(s32[5]{0:T(128)S(1)} %stack.32.at, bf16[528,1024]{1,0:T(8,128)(2,1)S(1)} %shard_map.70.z0.mine, bf16[528,1024]{1,0:T(8,128)(2,1)S(1)} %collective-permute-done.10.z1.up, bf16[528,1024]{1,0:T(8,128)(2,1)S(1)} %collective-permute-done.11.z3.down, ...), custom_call_target="tpu_custom_call" | custom-call | flops 1024 | bytes 1024 | tf_op jit(solution)/shard_map/pallas_call | solution.py:47
  125.6 0.7 shard_map.75
  126.3 4.6 %collective-permute-done.25 = f16[256,1024]{1,0:T(8,128)(2,1)S(1)} collective-permute-done((f16[256,1024]{1,0:T(8,128)(2,1)}, f16[256,1024]{1,0:T(8,128)(2,1)S(1)}, u32[]{:S(2)}, u32[]{:S(2)}) %collective-permute-start.25) | collective-permute-done | bytes 524320 | tf_op jit(solution)/shard_map/ppermute | solution.py:35
  130.9 0.8 collective-permute-done.26
  131.7 2.3 %fusion.52 = f32[256,1024]{1,0:T(8,128)S(1)} fusion(bf16[256,1536]{1,0:T(8,128)(2,1)S(1)} %get-tuple-element.229, bf16[2048,1536]{1,0:T(8,128)(2,1)S(1)} %shard_map.67, f16[256,1024]{1,0:T(8,128)(2,1)S(1)} %copy-done.4, f16[256,1024]{1,0:T(8,128)(2,1)} %collective-permute-done.23, f16[256,1024]{1,0:T(8,128)(2,1)} %collective-permute-done.22, ...), kind=kOutput, calls=%fused_computation.42 | convolution fusion | flops 807665664 | bytes 6565888 | tf_op jit(solution)/shard_map/dot_general | solution.py:39
  134.2 0.8 multiply_add_fusion
  135.0 1.1 fusion.46
  136.5 3.2 %collective-permute-start.28 = (f16[64,3072]{1,0:T(8,128)(2,1)S(1)}, f16[64,3072]{1,0:T(8,128)(2,1)S(1)}, u32[]{:S(2)}, u32[]{:S(2)}) collective-permute-start(f16[64,3072]{1,0:T(8,128)(2,1)S(1)} %get-tuple-element.266), channel_id=1, source_target_pairs={{0,24},{1,25},{2,26},{3,27},{4,28},{5,29},{6,30},{7,31},{8,0},{9,1... | collective-permute-start | bytes 1179656 | tf_op jit(solution)/shard_map/ppermute | solution.py:35
  139.7 1.1 collective-permute-start.30
  140.9 14.5 %collective-permute-done.27 = f16[64,3072]{1,0:T(8,128)(2,1)S(1)} collective-permute-done((f16[64,3072]{1,0:T(8,128)(2,1)S(1)}, f16[64,3072]{1,0:T(8,128)(2,1)S(1)}, u32[]{:S(2)}, u32[]{:S(2)}) %collective-permute-start.27) | collective-permute-done | bytes 393248 | tf_op jit(solution)/shard_map/ppermute | solution.py:35
  155.4 2.1 %collective-permute-start.31 = (f32[64,1024]{1,0:T(8,128)S(1)}, f32[64,1024]{1,0:T(8,128)S(1)}, u32[]{:S(2)}, u32[]{:S(2)}) collective-permute-start(f32[64,1024]{1,0:T(8,128)S(1)} %get-tuple-element.268), channel_id=1, source_target_pairs={{0,6},{1,7},{2,0},{3,1},{4,2},{5,3},{6,4},{7,5},{8,14},{9,15},{10,... | collective-permute-start | bytes 786440 | tf_op jit(solution)/shard_map/ppermute | solution.py:35
  157.5 0.8 collective-permute-start.32
  158.5 5.7 %collective-permute-done.31.h2 = f32[64,1024]{1,0:T(8,128)S(1)} collective-permute-done((f32[64,1024]{1,0:T(8,128)S(1)}, f32[64,1024]{1,0:T(8,128)S(1)}, u32[]{:S(2)}, u32[]{:S(2)}) %collective-permute-start.31) | collective-permute-done | bytes 262176 | tf_op jit(solution)/shard_map/ppermute | solution.py:35
  164.2 1.1 collective-permute-done.32.h3
  165.8 5.4 %shard_map.77.refs_10_ = f32[2,512,768]{2,1,0:T(8,128)} custom-call(s32[5]{0:T(128)S(1)} %stack.32.at, bf16[528,1024]{1,0:T(8,128)(2,1)S(1)} %shard_map.70.z0.mine, bf16[528,1024]{1,0:T(8,128)(2,1)S(1)} %collective-permute-done.10.z1.up, bf16[528,1024]{1,0:T(8,128)(2,1)S(1)} %collective-permute-done.11.z3.down, ...), custom_call_target="tpu_custom_call", output_to_operand_aliasing={{}: (14, {})} | custom-call | flops 1024 | bytes 1024 | tf_op jit(solution)/shard_map/pallas_call | solution.py:47
  171.2 3.6 %collective-permute-done.34.got = f32[32,4096]{1,0:T(8,128)S(1)} collective-permute-done((f32[32,4096]{1,0:T(8,128)S(1)}, f32[32,4096]{1,0:T(8,128)S(1)}, u32[]{:S(2)}, u32[]{:S(2)}) %collective-permute-start.34) | collective-permute-done | bytes 524320 | tf_op jit(solution)/shard_map/ppermute | solution.py:35
  174.8 2.1 %collective-permute-start.35 = (f32[32,2048]{1,0:T(8,128)S(1)}, f32[32,2048]{1,0:T(8,128)S(1)}, u32[]{:S(2)}, u32[]{:S(2)}) collective-permute-start(f32[32,2048]{1,0:T(8,128)S(1)} %get-tuple-element.254), channel_id=1, source_target_pairs={{0,64},{1,65},{2,66},{3,67},{4,68},{5,69},{6,70},{7,71},{8,72},{9,... | collective-permute-start | bytes 786440 | tf_op jit(solution)/shard_map/ppermute | solution.py:35
  176.9 5.3 %shard_map.79 = f32[2,512,768]{2,1,0:T(8,128)} custom-call(s32[5]{0:T(128)S(1)} %stack.32.at, bf16[528,1024]{1,0:T(8,128)(2,1)S(1)} %shard_map.70.z0.mine, bf16[528,1024]{1,0:T(8,128)(2,1)S(1)} %collective-permute-done.10.z1.up, bf16[528,1024]{1,0:T(8,128)(2,1)S(1)} %collective-permute-done.11.z3.down, ...), custom_call_target="tpu_custom_call", output_to_operand_aliasing={{}: (14, {})} | custom-call | flops 1024 | bytes 1024 | tf_op jit(solution)/shard_map/pallas_call | solution.py:47
  182.7 1.4 shard_map.80
  (64 shorter events, 5.6 us)
Async XLA Ops:
  0.6 13.1 %copy-start.1 = (bf16[2,512,768]{2,1,0:T(8,128)(2,1)S(1)}, bf16[2,512,768]{2,1,0:T(8,128)(2,1)}, u32[]{:S(2)}) copy-start(bf16[2,512,768]{2,1,0:T(8,128)(2,1)} %refs_3_) | copy-start | bytes 4718596
  0.6 13.1 %copy-start = (bf16[2,512,768]{2,1,0:T(8,128)(2,1)S(1)}, bf16[2,512,768]{2,1,0:T(8,128)(2,1)}, u32[]{:S(2)}) copy-start(bf16[2,512,768]{2,1,0:T(8,128)(2,1)} %refs_3_.2) | copy-start | bytes 4718596
  0.7 8.1 %collective-permute-start = (bf16[2,512,768]{2,1,0:T(8,128)(2,1)}, bf16[2,512,768]{2,1,0:T(8,128)(2,1)}, u32[]{:S(2)}, u32[]{:S(2)}) collective-permute-start(bf16[2,512,768]{2,1,0:T(8,128)(2,1)} %refs_3_), channel_id=1, source_target_pairs={{0,32},{1,33},{2,34},{3,35},{4,36},{5,37},{6,38},{7,39},{8,40},{9,... | collective-permute-start | bytes 4718600 | tf_op jit(solution)/shard_map/ppermute | solution.py:35
  0.7 8.1 %collective-permute-start.1 = (bf16[2,512,768]{2,1,0:T(8,128)(2,1)}, bf16[2,512,768]{2,1,0:T(8,128)(2,1)}, u32[]{:S(2)}, u32[]{:S(2)}) collective-permute-start(bf16[2,512,768]{2,1,0:T(8,128)(2,1)} %refs_3_.2), channel_id=1, source_target_pairs={{0,32},{1,33},{2,34},{3,35},{4,36},{5,37},{6,38},{7,39},{8,40},{9,... | collective-permute-start | bytes 4718600 | tf_op jit(solution)/shard_map/ppermute | solution.py:35
  1.2 7.5 %collective-permute-start.2 = (bf16[2,64,512]{2,1,0:T(8,128)(2,1)}, bf16[2,64,512]{2,1,0:T(8,128)(2,1)S(1)}, u32[]{:S(2)}, u32[]{:S(2)}) collective-permute-start(bf16[2,64,512]{2,1,0:T(8,128)(2,1)} %own.1), channel_id=1, source_target_pairs={{0,1},{1,0},{2,3},{3,2},{4,5},{5,4},{6,7},{7,6},{8,9},{9,8},{10,11... | collective-permute-start | bytes 393224 | tf_op jit(solution)/shard_map/ppermute | solution.py:35
  8.8 0.9 copy-start.2
  10.3 7.5 %collective-permute-start.3 = (bf16[2,2,80,128]{3,2,1,0:T(8,128)(2,1)S(1)}, bf16[2,2,80,128]{3,2,1,0:T(8,128)(2,1)S(1)}, u32[]{:S(2)}, u32[]{:S(2)}) collective-permute-start(bf16[2,2,80,128]{3,2,1,0:T(8,128)(2,1)S(1)} %get-tuple-element.138), channel_id=1, source_target_pairs={{0,32},{1,33},{2,34},{3,35},{4,36},{5,37},{6,38},{7,39},{8,40},{9,... | collective-permute-start | bytes 245768 | tf_op jit(solution)/shard_map/ppermute | solution.py:35
  10.4 7.5 %collective-permute-start.4 = (bf16[2,2,80,128]{3,2,1,0:T(8,128)(2,1)S(1)}, bf16[2,2,80,128]{3,2,1,0:T(8,128)(2,1)S(1)}, u32[]{:S(2)}, u32[]{:S(2)}) collective-permute-start(bf16[2,2,80,128]{3,2,1,0:T(8,128)(2,1)S(1)} %get-tuple-element.139), channel_id=1, source_target_pairs={{0,64},{1,65},{2,66},{3,67},{4,68},{5,69},{6,70},{7,71},{8,72},{9,... | collective-permute-start | bytes 245768 | tf_op jit(solution)/shard_map/ppermute | solution.py:35
  13.4 5.9 %collective-permute-start.5 = (bf16[2,2,80,128]{3,2,1,0:T(8,128)(2,1)S(1)}, bf16[2,2,80,128]{3,2,1,0:T(8,128)(2,1)S(1)}, u32[]{:S(2)}, u32[]{:S(2)}) collective-permute-start(bf16[2,2,80,128]{3,2,1,0:T(8,128)(2,1)S(1)} %get-tuple-element.140), channel_id=1, source_target_pairs={{0,96},{1,97},{2,98},{3,99},{4,100},{5,101},{6,102},{7,103},{8,104... | collective-permute-start | bytes 245768 | tf_op jit(solution)/shard_map/ppermute | solution.py:35
  20.0 21.1 %collective-permute-start.7 = (bf16[528,256]{1,0:T(8,128)(2,1)S(1)}, bf16[528,256]{1,0:T(8,128)(2,1)S(1)}, u32[]{:S(2)}, u32[]{:S(2)}) collective-permute-start(bf16[528,256]{1,0:T(8,128)(2,1)S(1)} %get-tuple-element.165.first), channel_id=1, source_target_pairs={{0,6},{1,7},{2,0},{3,1},{4,2},{5,3},{6,4},{7,5},{8,14},{9,15},{10,... | collective-permute-start | bytes 811016 | tf_op jit(solution)/shard_map/ppermute | solution.py:35
  22.8 18.3 %collective-permute-start.8 = (bf16[528,256]{1,0:T(8,128)(2,1)S(1)}, bf16[528,256]{1,0:T(8,128)(2,1)S(1)}, u32[]{:S(2)}, u32[]{:S(2)}) collective-permute-start(bf16[528,256]{1,0:T(8,128)(2,1)S(1)} %get-tuple-element.165.first), channel_id=1, source_target_pairs={{0,4},{1,5},{2,6},{3,7},{4,0},{5,1},{6,2},{7,3},{8,12},{9,13},{10,... | collective-permute-start | bytes 811016 | tf_op jit(solution)/shard_map/ppermute | solution.py:35
  23.6 17.5 %collective-permute-start.9 = (bf16[528,256]{1,0:T(8,128)(2,1)S(1)}, bf16[528,256]{1,0:T(8,128)(2,1)S(1)}, u32[]{:S(2)}, u32[]{:S(2)}) collective-permute-start(bf16[528,256]{1,0:T(8,128)(2,1)S(1)} %get-tuple-element.165.first), channel_id=1, source_target_pairs={{0,2},{1,3},{2,4},{3,5},{4,6},{5,7},{6,0},{7,1},{8,10},{9,11},{10,... | collective-permute-start | bytes 811016 | tf_op jit(solution)/shard_map/ppermute | solution.py:35
  26.4 14.7 %collective-permute-start.6 = (bf16[2,512,256]{2,1,0:T(8,128)(2,1)S(1)}, bf16[2,512,256]{2,1,0:T(8,128)(2,1)S(1)}, u32[]{:S(2)}, u32[]{:S(2)}) collective-permute-start(bf16[2,512,256]{2,1,0:T(8,128)(2,1)S(1)} %slice.123), channel_id=1, source_target_pairs={{0,64},{1,65},{2,66},{3,67},{4,68},{5,69},{6,70},{7,71},{8,72},{9,... | collective-permute-start | bytes 1572872 | tf_op jit(solution)/shard_map/ppermute | solution.py:35
  42.1 28.8 %collective-permute-start.10 = (bf16[528,1024]{1,0:T(8,128)(2,1)S(1)}, bf16[528,1024]{1,0:T(8,128)(2,1)S(1)}, u32[]{:S(2)}, u32[]{:S(2)}) collective-permute-start(bf16[528,1024]{1,0:T(8,128)(2,1)S(1)} %shard_map.70.z0.mine), channel_id=1, source_target_pairs={{0,24},{1,25},{2,26},{3,27},{4,28},{5,29},{6,30},{7,31},{8,0},{9,1... | collective-permute-start | bytes 3244040 | tf_op jit(solution)/shard_map/ppermute | solution.py:35
  46.3 25.1 %collective-permute-start.11 = (bf16[528,1024]{1,0:T(8,128)(2,1)S(1)}, bf16[528,1024]{1,0:T(8,128)(2,1)S(1)}, u32[]{:S(2)}, u32[]{:S(2)}) collective-permute-start(bf16[528,1024]{1,0:T(8,128)(2,1)S(1)} %shard_map.70.z0.mine), channel_id=1, source_target_pairs={{0,8},{1,9},{2,10},{3,11},{4,12},{5,13},{6,14},{7,15},{8,16},{9,17... | collective-permute-start | bytes 3244040 | tf_op jit(solution)/shard_map/ppermute | solution.py:35
  46.3 24.4 %collective-permute-start.12 = (f16[256,2048]{1,0:T(8,128)(2,1)S(1)}, f16[256,2048]{1,0:T(8,128)(2,1)S(1)}, u32[]{:S(2)}, u32[]{:S(2)}) collective-permute-start(f16[256,2048]{1,0:T(8,128)(2,1)S(1)} %fusion.4), channel_id=1, source_target_pairs={{0,2},{1,3},{2,4},{3,5},{4,6},{5,7},{6,0},{7,1},{8,10},{9,11},{10,... | collective-permute-start | bytes 3145736 | tf_op jit(solution)/shard_map/ppermute | solution.py:35
  48.1 22.9 %collective-permute-start.13 = (f16[256,2048]{1,0:T(8,128)(2,1)S(1)}, f16[256,2048]{1,0:T(8,128)(2,1)S(1)}, u32[]{:S(2)}, u32[]{:S(2)}) collective-permute-start(f16[256,2048]{1,0:T(8,128)(2,1)S(1)} %fusion.5), channel_id=1, source_target_pairs={{0,6},{1,7},{2,0},{3,1},{4,2},{5,3},{6,4},{7,5},{8,14},{9,15},{10,... | collective-permute-start | bytes 3145736 | tf_op jit(solution)/shard_map/ppermute | solution.py:35
  49.6 24.2 %collective-permute-start.15 = (bf16[2,512,512]{2,1,0:T(8,128)(2,1)S(1)}, bf16[2,512,512]{2,1,0:T(8,128)(2,1)S(1)}, u32[]{:S(2)}, u32[]{:S(2)}) collective-permute-start(bf16[2,512,512]{2,1,0:T(8,128)(2,1)S(1)} %slice.125), channel_id=1, source_target_pairs={{0,64},{1,65},{2,66},{3,67},{4,68},{5,69},{6,70},{7,71},{8,72},{9,... | collective-permute-start | bytes 3145736 | tf_op jit(solution)/shard_map/ppermute | solution.py:35
  73.8 7.2 %collective-permute-start.20 = (bf16[2,512,512]{2,1,0:T(8,128)(2,1)S(1)}, bf16[2,512,512]{2,1,0:T(8,128)(2,1)S(1)}, u32[]{:S(2)}, u32[]{:S(2)}) collective-permute-start(bf16[2,512,512]{2,1,0:T(8,128)(2,1)S(1)} %collective-permute-done.15.refs_1_.refs_7_), channel_id=1, source_target_pairs={{0,32},{1,33},{2,34},{3,35},{4,36},{5,37},{6,38},{7,39},{8,40},{9,... | collective-permute-start | bytes 3145736 | tf_op jit(solution)/shard_map/ppermute | solution.py:35
  73.8 5.2 %collective-permute-start.19 = (bf16[2,512,256]{2,1,0:T(8,128)(2,1)S(1)}, bf16[2,512,256]{2,1,0:T(8,128)(2,1)S(1)}, u32[]{:S(2)}, u32[]{:S(2)}) collective-permute-start(bf16[2,512,256]{2,1,0:T(8,128)(2,1)S(1)} %collective-permute-done.6.refs_0_.refs_6_), channel_id=1, source_target_pairs={{0,32},{1,33},{2,34},{3,35},{4,36},{5,37},{6,38},{7,39},{8,40},{9,... | collective-permute-start | bytes 1572872 | tf_op jit(solution)/shard_map/ppermute | solution.py:35
  74.3 28.9 %collective-permute-start.17 = (bf16[528,512]{1,0:T(8,128)(2,1)S(1)}, bf16[528,512]{1,0:T(8,128)(2,1)S(1)}, u32[]{:S(2)}, u32[]{:S(2)}) collective-permute-start(bf16[528,512]{1,0:T(8,128)(2,1)S(1)} %slice.126), channel_id=1, source_target_pairs={{0,8},{1,9},{2,10},{3,11},{4,12},{5,13},{6,14},{7,15},{8,16},{9,17... | collective-permute-start | bytes 1622024 | tf_op jit(solution)/shard_map/ppermute | solution.py:35
  74.5 28.8 %collective-permute-start.18 = (bf16[528,512]{1,0:T(8,128)(2,1)S(1)}, bf16[528,512]{1,0:T(8,128)(2,1)S(1)}, u32[]{:S(2)}, u32[]{:S(2)}) collective-permute-start(bf16[528,512]{1,0:T(8,128)(2,1)S(1)} %slice.127), channel_id=1, source_target_pairs={{0,24},{1,25},{2,26},{3,27},{4,28},{5,29},{6,30},{7,31},{8,0},{9,1... | collective-permute-start | bytes 1622024 | tf_op jit(solution)/shard_map/ppermute | solution.py:35
  77.7 26.0 %collective-permute-start.16 = (f16[256,2048]{1,0:T(8,128)(2,1)S(1)}, f16[256,2048]{1,0:T(8,128)(2,1)S(1)}, u32[]{:S(2)}, u32[]{:S(2)}) collective-permute-start(f16[256,2048]{1,0:T(8,128)(2,1)S(1)} %fusion.6), channel_id=1, source_target_pairs={{0,4},{1,5},{2,6},{3,7},{4,0},{5,1},{6,2},{7,3},{8,12},{9,13},{10,... | collective-permute-start | bytes 3145736 | tf_op jit(solution)/shard_map/ppermute | solution.py:35
  79.0 37.0 %collective-permute-start.14 = (bf16[2,512,768]{2,1,0:T(8,128)(2,1)S(1)}, bf16[2,512,768]{2,1,0:T(8,128)(2,1)S(1)}, u32[]{:S(2)}, u32[]{:S(2)}) collective-permute-start(bf16[2,512,768]{2,1,0:T(8,128)(2,1)S(1)} %copy-done), channel_id=1, source_target_pairs={{0,64},{1,65},{2,66},{3,67},{4,68},{5,69},{6,70},{7,71},{8,72},{9,... | collective-permute-start | bytes 4718600 | tf_op jit(solution)/shard_map/ppermute | solution.py:35
  82.9 20.9 %collective-permute-start.21 = (f16[256,1024]{1,0:T(8,128)(2,1)S(1)}, f16[256,1024]{1,0:T(8,128)(2,1)S(1)}, u32[]{:S(2)}, u32[]{:S(2)}) collective-permute-start(f16[256,1024]{1,0:T(8,128)(2,1)S(1)} %fusion.70), channel_id=1, source_target_pairs={{0,16},{1,17},{2,18},{3,19},{4,20},{5,21},{6,22},{7,23},{8,24},{9,... | collective-permute-start | bytes 1572872 | tf_op jit(solution)/shard_map/ppermute | solution.py:35
  103.8 12.2 %copy-start.3 = (f16[256,1024]{1,0:T(8,128)(2,1)}, f16[256,1024]{1,0:T(8,128)(2,1)S(1)}, u32[]{:S(2)}) copy-start(f16[256,1024]{1,0:T(8,128)(2,1)S(1)} %collective-permute-done.21) | copy-start | bytes 1572868
  103.8 22.5 %collective-permute-start.22 = (f16[256,1024]{1,0:T(8,128)(2,1)}, f16[256,1024]{1,0:T(8,128)(2,1)}, u32[]{:S(2)}, u32[]{:S(2)}) collective-permute-start(f16[256,1024]{1,0:T(8,128)(2,1)} %fusion.67), channel_id=1, source_target_pairs={{0,8},{1,9},{2,10},{3,11},{4,12},{5,13},{6,14},{7,15},{8,16},{9,17... | collective-permute-start | bytes 1572872 | tf_op jit(solution)/shard_map/ppermute | solution.py:35
  104.7 21.6 %collective-permute-start.23 = (f16[256,1024]{1,0:T(8,128)(2,1)}, f16[256,1024]{1,0:T(8,128)(2,1)}, u32[]{:S(2)}, u32[]{:S(2)}) collective-permute-start(f16[256,1024]{1,0:T(8,128)(2,1)} %fusion.64), channel_id=1, source_target_pairs={{0,24},{1,25},{2,26},{3,27},{4,28},{5,29},{6,30},{7,31},{8,0},{9,1... | collective-permute-start | bytes 1572872 | tf_op jit(solution)/shard_map/ppermute | solution.py:35
  107.0 19.3 %collective-permute-start.24 = (f16[256,1024]{1,0:T(8,128)(2,1)}, f16[256,1024]{1,0:T(8,128)(2,1)S(1)}, u32[]{:S(2)}, u32[]{:S(2)}) collective-permute-start(f16[256,1024]{1,0:T(8,128)(2,1)} %fusion.61), channel_id=1, source_target_pairs={{0,2},{1,3},{2,4},{3,5},{4,6},{5,7},{6,0},{7,1},{8,10},{9,11},{10,... | collective-permute-start | bytes 1572872 | tf_op jit(solution)/shard_map/ppermute | solution.py:35
  107.6 23.3 %collective-permute-start.25 = (f16[256,1024]{1,0:T(8,128)(2,1)}, f16[256,1024]{1,0:T(8,128)(2,1)S(1)}, u32[]{:S(2)}, u32[]{:S(2)}) collective-permute-start(f16[256,1024]{1,0:T(8,128)(2,1)} %fusion.58), channel_id=1, source_target_pairs={{0,6},{1,7},{2,0},{3,1},{4,2},{5,3},{6,4},{7,5},{8,14},{9,15},{10,... | collective-permute-start | bytes 1572872 | tf_op jit(solution)/shard_map/ppermute | solution.py:35
  116.0 15.7 %collective-permute-start.26 = (f16[256,1024]{1,0:T(8,128)(2,1)}, f16[256,1024]{1,0:T(8,128)(2,1)S(1)}, u32[]{:S(2)}, u32[]{:S(2)}) collective-permute-start(f16[256,1024]{1,0:T(8,128)(2,1)} %fusion.55), channel_id=1, source_target_pairs={{0,4},{1,5},{2,6},{3,7},{4,0},{5,1},{6,2},{7,3},{8,12},{9,13},{10,... | collective-permute-start | bytes 1572872 | tf_op jit(solution)/shard_map/ppermute | solution.py:35
  125.6 6.1 %copy-start.4 = (f16[256,1024]{1,0:T(8,128)(2,1)S(1)}, f16[256,1024]{1,0:T(8,128)(2,1)}, u32[]{:S(2)}) copy-start(f16[256,1024]{1,0:T(8,128)(2,1)} %copy-done.3) | copy-start | bytes 1572868
  136.4 19.0 %collective-permute-start.27 = (f16[64,3072]{1,0:T(8,128)(2,1)S(1)}, f16[64,3072]{1,0:T(8,128)(2,1)S(1)}, u32[]{:S(2)}, u32[]{:S(2)}) collective-permute-start(f16[64,3072]{1,0:T(8,128)(2,1)S(1)} %get-tuple-element.264), channel_id=1, source_target_pairs={{0,8},{1,9},{2,10},{3,11},{4,12},{5,13},{6,14},{7,15},{8,16},{9,17... | collective-permute-start | bytes 1179656 | tf_op jit(solution)/shard_map/ppermute | solution.py:35
  136.5 21.0 %collective-permute-start.28 = (f16[64,3072]{1,0:T(8,128)(2,1)S(1)}, f16[64,3072]{1,0:T(8,128)(2,1)S(1)}, u32[]{:S(2)}, u32[]{:S(2)}) collective-permute-start(f16[64,3072]{1,0:T(8,128)(2,1)S(1)} %get-tuple-element.266), channel_id=1, source_target_pairs={{0,24},{1,25},{2,26},{3,27},{4,28},{5,29},{6,30},{7,31},{8,0},{9,1... | collective-permute-start | bytes 1179656 | tf_op jit(solution)/shard_map/ppermute | solution.py:35
  139.7 18.6 %collective-permute-start.29 = (f16[64,3072]{1,0:T(8,128)(2,1)S(1)}, f16[64,3072]{1,0:T(8,128)(2,1)S(1)}, u32[]{:S(2)}, u32[]{:S(2)}) collective-permute-start(f16[64,3072]{1,0:T(8,128)(2,1)S(1)} %get-tuple-element.265), channel_id=1, source_target_pairs={{0,16},{1,17},{2,18},{3,19},{4,20},{5,21},{6,22},{7,23},{8,24},{9,... | collective-permute-start | bytes 1179656 | tf_op jit(solution)/shard_map/ppermute | solution.py:35
  139.7 18.8 %collective-permute-start.30 = (f32[64,1024]{1,0:T(8,128)S(1)}, f32[64,1024]{1,0:T(8,128)S(1)}, u32[]{:S(2)}, u32[]{:S(2)}) collective-permute-start(f32[64,1024]{1,0:T(8,128)S(1)} %get-tuple-element.269), channel_id=1, source_target_pairs={{0,2},{1,3},{2,4},{3,5},{4,6},{5,7},{6,0},{7,1},{8,10},{9,11},{10,... | collective-permute-start | bytes 786440 | tf_op jit(solution)/shard_map/ppermute | solution.py:35
  140.8 25.0 %collective-permute-start.33 = (bf16[2,512,768]{2,1,0:T(8,128)(2,1)S(1)}, bf16[2,512,768]{2,1,0:T(8,128)(2,1)S(1)}, u32[]{:S(2)}, u32[]{:S(2)}) collective-permute-start(bf16[2,512,768]{2,1,0:T(8,128)(2,1)S(1)} %collective-permute-done.14.refs_6_.refs_7_), channel_id=1, source_target_pairs={{0,32},{1,33},{2,34},{3,35},{4,36},{5,37},{6,38},{7,39},{8,40},{9,... | collective-permute-start | bytes 4718600 | tf_op jit(solution)/shard_map/ppermute | solution.py:35
  155.4 8.8 %collective-permute-start.31 = (f32[64,1024]{1,0:T(8,128)S(1)}, f32[64,1024]{1,0:T(8,128)S(1)}, u32[]{:S(2)}, u32[]{:S(2)}) collective-permute-start(f32[64,1024]{1,0:T(8,128)S(1)} %get-tuple-element.268), channel_id=1, source_target_pairs={{0,6},{1,7},{2,0},{3,1},{4,2},{5,3},{6,4},{7,5},{8,14},{9,15},{10,... | collective-permute-start | bytes 786440 | tf_op jit(solution)/shard_map/ppermute | solution.py:35
  157.5 7.9 %collective-permute-start.32 = (f32[64,1024]{1,0:T(8,128)S(1)}, f32[64,1024]{1,0:T(8,128)S(1)}, u32[]{:S(2)}, u32[]{:S(2)}) collective-permute-start(f32[64,1024]{1,0:T(8,128)S(1)} %get-tuple-element.267), channel_id=1, source_target_pairs={{0,4},{1,5},{2,6},{3,7},{4,0},{5,1},{6,2},{7,3},{8,12},{9,13},{10,... | collective-permute-start | bytes 786440 | tf_op jit(solution)/shard_map/ppermute | solution.py:35
  165.5 9.3 %collective-permute-start.34 = (f32[32,4096]{1,0:T(8,128)S(1)}, f32[32,4096]{1,0:T(8,128)S(1)}, u32[]{:S(2)}, u32[]{:S(2)}) collective-permute-start(f32[32,4096]{1,0:T(8,128)S(1)} %get-tuple-element.245), channel_id=1, source_target_pairs={{0,1},{1,0},{2,3},{3,2},{4,5},{5,4},{6,7},{7,6},{8,9},{9,8},{10,11... | collective-permute-start | bytes 1572872 | tf_op jit(solution)/shard_map/ppermute | solution.py:35
  174.8 8.0 %collective-permute-start.35 = (f32[32,2048]{1,0:T(8,128)S(1)}, f32[32,2048]{1,0:T(8,128)S(1)}, u32[]{:S(2)}, u32[]{:S(2)}) collective-permute-start(f32[32,2048]{1,0:T(8,128)S(1)} %get-tuple-element.254), channel_id=1, source_target_pairs={{0,64},{1,65},{2,66},{3,67},{4,68},{5,69},{6,70},{7,71},{8,72},{9,... | collective-permute-start | bytes 786440 | tf_op jit(solution)/shard_map/ppermute | solution.py:35

commit v6 on v5

--- a/solution.py
+++ b/solution.py
@@ -51,6 +51,15 @@
         cost_estimate=pl.CostEstimate(flops=1024, bytes_accessed=1024, transcendentals=0),
         **kw,
     )(*args)
+
+
+def largest_kernel(psi, hpsi, out):
+    for m, ref in enumerate((psi, hpsi)):
+        most = jnp.abs(ref[0, 0:16, :])
+        for c in range(2):
+            for n in range(32):
+                most = jnp.maximum(most, jnp.abs(ref[c, n * 16:n * 16 + 16, :]))
+        out[m] = jnp.max(most.astype(jnp.float32))
 
 
 def split_kernel(at, largest, own, other, first, second, third, fourth):
@@ -165,6 +174,11 @@
 
 def columns(refs):
     return lambda c, rows: jnp.concatenate([r[c, rows, :] for r in refs], axis=1)
+
+
+def own_kernel(left_h, left_s, right, out_h, out_s):
+    out_h[...] = dot_rows(left_h[...], right[0:1024, :])
+    out_s[...] = dot_rows(left_s[...], right[1024:2048, :])
 
 
 def rotate_kernel(early, split, at, z0, z1, z3, *refs):
@@ -232,8 +246,7 @@
     )
 
 
-def fold_kernel(first, h0, h1, h2, h3, keep, low):
-    h = h0[...] + h1[...] + h2[...] + h3[...]
+def fold_kernel(first, h, keep, low):
     for rows, out in ((slice(0, 32), keep), (slice(32, 64), low)):
         out[:, 0:3072] = first[rows, :]
         out[:, 3072:4096] = h[rows, :]
@@ -281,15 +294,15 @@
     def for_peer(left, operand, factor):
         return (dot_rows(left, operand) * factor).astype(jnp.float16)
 
-    def gathered(mine, operand, factors, got):
-        total = dot_rows(mine, operand)
+    def gathered(total, factors, got):
         for factor, g in zip(factors, got):
             total = total + g.astype(jnp.float32) * factor
         return total
 
     fence = lax.optimization_barrier
 
-    largest = jnp.stack([jnp.max(jnp.abs(psi)), jnp.max(jnp.abs(hpsi))]).astype(jnp.float32)
+    largest = call(largest_kernel, jax.ShapeDtypeStruct((2,), jnp.float32), psi, hpsi,
+                   in_specs=[VMEM] * 2, out_specs=SMEM)
     rot_other = move(rot, y_lo=1)
     psi_mate = move(psi, core=1)
     hpsi_mate = move(hpsi, core=1)
@@ -354,27 +367,29 @@
     rotated_psi = rotate(at, coef, [psi, psi_mate, psi_cross, psi_cross_mate], psi_near)
     factors = call(factor_kernel, jax.ShapeDtypeStruct((16, 2048), jnp.float32), after(at, rotated_psi), *xs[1:], mine, up,
                    far0, down, in_specs=[SMEM] + [VMEM] * 7, out_specs=VMEM)
-    hpsi_cross, got_h, got_s, near_got, near_own, rotated_psi, factors, right = fence(
-        (hpsi_cross, got_h, got_s, near_got, near_own, rotated_psi, factors, right))
-
-    right_h, right_s = right[0:1024], right[1024:2048]
+    own_h, own_s = call(own_kernel, [jax.ShapeDtypeStruct((256, 1024), jnp.float32)] * 2, after(away_left[4], factors),
+                        away_left[0], right, in_specs=[VMEM] * 3, out_specs=[VMEM] * 2)
+    hpsi_cross, got_h, got_s, near_got, near_own, rotated_psi, factors, own_h, own_s = fence(
+        (hpsi_cross, got_h, got_s, near_got, near_own, rotated_psi, factors, own_h, own_s))
+
     factor = [factors[n:n + 1] for n in range(10)]
     got_h = [got_h[1], got_h[2], got_h[0]]
-    away_h = gathered(away_left[4], right_h, [f[:, 0:1024] for f in factor[3:6]], got_h)
+    away_h = gathered(own_h, [f[:, 0:1024] for f in factor[3:6]], got_h)
     by_x = [away_h[0:64]] + [move(away_h[d * 64:d * 64 + 64], dx=d) for d in (1, 3, 2)]
     near_total = after(near_own, away_h)
     for n, g in enumerate(near_got):
         near_total = near_total + g.astype(jnp.float32) * factor[n]
-    away_s = gathered(after(away_left[0], near_total), right_s, [f[:, 1024:2048] for f in factor[0:3]], got_s)
+    away_s = gathered(after(own_s, near_total), [f[:, 1024:2048] for f in factor[0:3]], got_s)
     hpsi_cross_mate = move(hpsi_cross, core=1)
     by_z = jnp.concatenate([near_total, away_s], axis=1)
     factor = [jnp.concatenate([f, f[:, 1024:2048]], axis=1) for f in factor[6:10]]
     by_z = [by_z[0:64]] + [move((by_z[d * 64:d * 64 + 64] * factor[0]).astype(jnp.float16), dz=d) for d in (1, 3, 2)]
-    first = by_z[0]
+    sum_h = by_x[0] + by_x[1] + by_x[2] + by_x[3]
+    first = after(by_z[0], sum_h)
     for p, f in zip(by_z[1:], factor[1:]):
         first = first + p.astype(jnp.float32) * f
-    keep, low = call(fold_kernel, [jax.ShapeDtypeStruct((32, 4096), jnp.float32)] * 2, first, *by_x,
-                     in_specs=[VMEM] * 5, out_specs=[VMEM] * 2)
+    keep, low = call(fold_kernel, [jax.ShapeDtypeStruct((32, 4096), jnp.float32)] * 2, first, sum_h,
+                     in_specs=[VMEM] * 2, out_specs=[VMEM] * 2)
     low_got = move(low, y_lo=1)
     blocks = [hpsi, hpsi_mate, hpsi_cross, hpsi_cross_mate]
     part_1 = rotate(at, after_all(coef, low), blocks, hpsi_near, rows=0)

time: 185 us -> 179 us (0.968)
  waiting for transfers between devices: 68.3 us -> 60.3 us
  Pallas kernels: 37.4 us -> 40.2 us
  local copies, waits for them, and re-layouts: 1.35 us -> 4.14 us
  matrix products: 20.9 us -> 18.4 us
  other arithmetic: 7.12 us -> 4.8 us
  starting transfers between devices: 48.1 us -> 50 us
    ppermute x36, waiting for transfers between devices: 68.3 us -> 60.3 us  [move(): return lax.ppermute(value, ('band', 'ga'), pairs)]
    reduce_max x2 -> x0, other arithmetic: 4.49 us -> none  [the longest x1 2.25 us: shards(): jnp.max(jnp.abs(hpsi))]
    add x0 -> x3, other arithmetic: none -> 3.43 us  [the longest x2 3.36 us: gathered(): total = total + g.astype(jnp.float32) * factor]
    unnamed x10 -> x14, local copies, waits for them, and re-layouts: 0.92 us -> 3.73 us
    pallas_call x15 -> x17, Pallas kernels: 37.4 us -> 40.2 us  [call(): pl.pallas_call(kernel, out_shape=outs, compiler_params=pltpu.CompilerPara...]
    dot_general x12 -> x10, matrix products: 20.9 us -> 18.4 us  [dot_rows(): lax.dot_general(left, right, (((1,), (1,)), ((), ())), preferred_element_...]
    ppermute x36, starting transfers between devices: 48.1 us -> 50 us  [move(): return lax.ppermute(value, ('band', 'ga'), pairs)]
  transfers between devices with their start and end apart: 36 -> 36, of which waited for: 15 -> 16; matrix products, arithmetic and copies ran while one was open for 13% -> 12% of each run, Pallas kernels for 18% -> 20%
where the time goes in v6:
time: 179 us
  waiting for transfers between devices  60.3 us (34%)
  starting transfers between devices  50 us (28%)
  Pallas kernels  40.2 us (22%)
  matrix products  18.4 us (10%)
  other arithmetic  4.8 us (3%)
  local copies, waits for them, and re-layouts  4.14 us (2%)
    ppermute x36, waiting for transfers between devices, move(): return lax.ppermute(value, ('band', 'ga'), pairs)  60.3 us
    ppermute x36, starting transfers between devices, move(): return lax.ppermute(value, ('band', 'ga'), pairs)  50 us
    pallas_call x17, Pallas kernels, call(): pl.pallas_call(kernel, out_shape=outs, compiler_params=pltpu.CompilerPara...  40.2 us
    dot_general x10, matrix products, dot_rows(): lax.dot_general(left, right, (((1,), (1,)), ((), ())), preferred_element_...  18.4 us
    unnamed x14, local copies, waits for them, and re-layouts  3.73 us
  transfers between devices with their start and end apart: 36, of which 16 were waited for; matrix products, arithmetic and copies ran while one was open for 12% of the time, Pallas kernels for 20%

profile of v6, /device:TPU:0, one launch (start us, length us, event | category | flops | bytes accessed | tf_op | source)
XLA Modules:
  0.0 178.8 jit_solution(11012050389157328313)
XLA Ops:
  1.2 1.7 collective-permute-start.2
  2.9 1.4 copy-done
  4.3 1.4 copy-done.2
  5.7 0.9 shard_map.66.largest
  6.9 0.9 copy-done.4
  8.5 3.4 %collective-permute-start.4 = (bf16[2,2,80,128]{3,2,1,0:T(8,128)(2,1)S(1)}, bf16[2,2,80,128]{3,2,1,0:T(8,128)(2,1)S(1)}, u32[]{:S(2)}, u32[]{:S(2)}) collective-permute-start(bf16[2,2,80,128]{3,2,1,0:T(8,128)(2,1)S(1)} %get-tuple-element.144), channel_id=1, source_target_pairs={{0,64},{1,65},{2,66},{3,67},{4,68},{5,69},{6,70},{7,71},{8,72},{9,... | collective-permute-start | bytes 245768 | tf_op jit(solution)/shard_map/ppermute | solution.py:35
  12.0 2.3 %shard_map.68.right = bf16[2048,1536]{1,0:T(8,128)(2,1)S(1)} custom-call(s32[5]{0:T(128)S(1)} %stack.23.at, bf16[2,512,768]{2,1,0:T(8,128)(2,1)S(1)} %copy-done.3, bf16[2,512,768]{2,1,0:T(8,128)(2,1)} %collective-permute-done.psi_mate.refs_1_.refs_2_.refs_3_.refs_4_.refs_5_, bf16[2,512,768]{2,1,0:T(8,128)(2,1)S(1)} %copy-done.1, ...), custom_call_target="tpu_custom_call" | custom-call | flops 1024 | bytes 1024 | tf_op jit(solution)/shard_map/pallas_call | solution.py:47
  14.3 1.8 shard_map.69
  16.0 1.8 collective-permute-done.5.fourth
  18.5 2.8 %collective-permute-start.7 = (bf16[528,256]{1,0:T(8,128)(2,1)S(1)}, bf16[528,256]{1,0:T(8,128)(2,1)S(1)}, u32[]{:S(2)}, u32[]{:S(2)}) collective-permute-start(bf16[528,256]{1,0:T(8,128)(2,1)S(1)} %get-tuple-element.170.first), channel_id=1, source_target_pairs={{0,6},{1,7},{2,0},{3,1},{4,2},{5,3},{6,4},{7,5},{8,14},{9,15},{10,... | collective-permute-start | bytes 811016 | tf_op jit(solution)/shard_map/ppermute | solution.py:35
  21.3 0.8 collective-permute-start.8
  22.1 0.9 collective-permute-start.9
  23.0 1.8 %fusion = f16[256,2048]{1,0:T(8,128)(2,1)S(1)} fusion(bf16[256,1536]{1,0:T(8,128)(2,1)S(1)} %get-tuple-element.162, bf16[2048,1536]{1,0:T(8,128)(2,1)S(1)} %shard_map.68.right, f32[2048]{0:T(1024)S(1)} %bitcast.48), kind=kOutput, calls=%fused_computation.9 | convolution fusion | flops 1611661312 | bytes 8134656 | tf_op jit(solution)/shard_map/dot_general | solution.py:39
  24.9 1.7 collective-permute-start.6
  26.6 1.8 %fusion.1 = f16[256,2048]{1,0:T(8,128)(2,1)S(1)} fusion(bf16[256,1536]{1,0:T(8,128)(2,1)S(1)} %get-tuple-element.166, bf16[2048,1536]{1,0:T(8,128)(2,1)S(1)} %shard_map.68.right, f32[2048]{0:T(1024)S(1)} %bitcast.49), kind=kOutput, calls=%fused_computation.10 | convolution fusion | flops 1611661312 | bytes 8134656 | tf_op jit(solution)/shard_map/dot_general | solution.py:39
  28.4 11.2 %collective-permute-done.6.refs_0_.refs_6_ = bf16[2,512,256]{2,1,0:T(8,128)(2,1)S(1)} collective-permute-done((bf16[2,512,256]{2,1,0:T(8,128)(2,1)S(1)}, bf16[2,512,256]{2,1,0:T(8,128)(2,1)S(1)}, u32[]{:S(2)}, u32[]{:S(2)}) %collective-permute-start.6) | collective-permute-done | bytes 524320 | tf_op jit(solution)/shard_map/ppermute | solution.py:35
  39.6 1.0 shard_map.71.z0.mine
  40.7 4.1 %collective-permute-start.10 = (bf16[528,1024]{1,0:T(8,128)(2,1)S(1)}, bf16[528,1024]{1,0:T(8,128)(2,1)S(1)}, u32[]{:S(2)}, u32[]{:S(2)}) collective-permute-start(bf16[528,1024]{1,0:T(8,128)(2,1)S(1)} %shard_map.71.z0.mine), channel_id=1, source_target_pairs={{0,24},{1,25},{2,26},{3,27},{4,28},{5,29},{6,30},{7,31},{8,0},{9,1... | collective-permute-start | bytes 3244040 | tf_op jit(solution)/shard_map/ppermute | solution.py:35
  44.8 1.8 %collective-permute-start.12 = (f16[256,2048]{1,0:T(8,128)(2,1)S(1)}, f16[256,2048]{1,0:T(8,128)(2,1)S(1)}, u32[]{:S(2)}, u32[]{:S(2)}) collective-permute-start(f16[256,2048]{1,0:T(8,128)(2,1)S(1)} %fusion), channel_id=1, source_target_pairs={{0,2},{1,3},{2,4},{3,5},{4,6},{5,7},{6,0},{7,1},{8,10},{9,11},{10,... | collective-permute-start | bytes 3145736 | tf_op jit(solution)/shard_map/ppermute | solution.py:35
  46.6 1.4 collective-permute-start.13
  48.1 1.9 %collective-permute-start.15 = (bf16[2,512,512]{2,1,0:T(8,128)(2,1)S(1)}, bf16[2,512,512]{2,1,0:T(8,128)(2,1)S(1)}, u32[]{:S(2)}, u32[]{:S(2)}) collective-permute-start(bf16[2,512,512]{2,1,0:T(8,128)(2,1)S(1)} %slice.119), channel_id=1, source_target_pairs={{0,64},{1,65},{2,66},{3,67},{4,68},{5,69},{6,70},{7,71},{8,72},{9,... | collective-permute-start | bytes 3145736 | tf_op jit(solution)/shard_map/ppermute | solution.py:35
  50.0 2.8 %fusion.2 = f16[256,2048]{1,0:T(8,128)(2,1)} fusion(bf16[256,1536]{1,0:T(8,128)(2,1)S(1)} %get-tuple-element.177, bf16[2048,1536]{1,0:T(8,128)(2,1)S(1)} %shard_map.68.right, f32[2048]{0:T(1024)S(1)} %bitcast.50), kind=kOutput, calls=%fused_computation.11 | convolution fusion | flops 1611661312 | bytes 8134656 | tf_op jit(solution)/shard_map/dot_general | solution.py:39
  52.8 1.8 %fusion.66 = f32[256,2048]{1,0:T(8,128)S(1)} fusion(bf16[256,1536]{1,0:T(8,128)(2,1)S(1)} %get-tuple-element.180, bf16[2048,1536]{1,0:T(8,128)(2,1)S(1)} %shard_map.68.right), kind=kOutput, calls=%fused_computation.61 | convolution fusion | flops 1610612736 | bytes 9175040 | tf_op jit(solution)/shard_map/dot_general | solution.py:39
  54.6 14.6 %collective-permute-done.12 = f16[256,2048]{1,0:T(8,128)(2,1)S(1)} collective-permute-done((f16[256,2048]{1,0:T(8,128)(2,1)S(1)}, f16[256,2048]{1,0:T(8,128)(2,1)S(1)}, u32[]{:S(2)}, u32[]{:S(2)}) %collective-permute-start.12) | collective-permute-done | bytes 1048608 | tf_op jit(solution)/shard_map/ppermute | solution.py:35
  69.8 2.4 %collective-permute-done.15.refs_1_.refs_7_ = bf16[2,512,512]{2,1,0:T(8,128)(2,1)S(1)} collective-permute-done((bf16[2,512,512]{2,1,0:T(8,128)(2,1)S(1)}, bf16[2,512,512]{2,1,0:T(8,128)(2,1)S(1)}, u32[]{:S(2)}, u32[]{:S(2)}) %collective-permute-start.15) | collective-permute-done | bytes 1048608 | tf_op jit(solution)/shard_map/ppermute | solution.py:35
  73.0 3.3 %collective-permute-start.18 = (bf16[528,512]{1,0:T(8,128)(2,1)S(1)}, bf16[528,512]{1,0:T(8,128)(2,1)S(1)}, u32[]{:S(2)}, u32[]{:S(2)}) collective-permute-start(bf16[528,512]{1,0:T(8,128)(2,1)S(1)} %slice.121), channel_id=1, source_target_pairs={{0,24},{1,25},{2,26},{3,27},{4,28},{5,29},{6,30},{7,31},{8,0},{9,1... | collective-permute-start | bytes 1622024 | tf_op jit(solution)/shard_map/ppermute | solution.py:35
  76.3 1.2 collective-permute-start.16
  77.5 1.9 %collective-permute-start.14 = (bf16[2,512,768]{2,1,0:T(8,128)(2,1)S(1)}, bf16[2,512,768]{2,1,0:T(8,128)(2,1)S(1)}, u32[]{:S(2)}, u32[]{:S(2)}) collective-permute-start(bf16[2,512,768]{2,1,0:T(8,128)(2,1)S(1)} %copy-done.1), channel_id=1, source_target_pairs={{0,64},{1,65},{2,66},{3,67},{4,68},{5,69},{6,70},{7,71},{8,72},{9,... | collective-permute-start | bytes 4718600 | tf_op jit(solution)/shard_map/ppermute | solution.py:35
  79.4 1.0 shard_map.72
  80.4 1.0 fusion.48
  81.4 1.4 collective-permute-start.21
  82.8 1.9 %fusion.45 = f16[256,1024]{1,0:T(8,128)(2,1)} fusion(bf16[256,1536]{1,0:T(8,128)(2,1)S(1)} %get-tuple-element.197, bf16[2048,1536]{1,0:T(8,128)(2,1)S(1)} %shard_map.68.right, f32[1024]{0:T(1024)S(1)} %bitcast.55), kind=kOutput, calls=%fused_computation.35 | convolution fusion | flops 805830656 | bytes 4460544 | tf_op jit(solution)/shard_map/dot_general | solution.py:39
  84.7 1.8 %fusion.42 = f16[256,1024]{1,0:T(8,128)(2,1)} fusion(bf16[256,1536]{1,0:T(8,128)(2,1)S(1)} %get-tuple-element.199, bf16[2048,1536]{1,0:T(8,128)(2,1)S(1)} %shard_map.68.right, f32[1024]{0:T(1024)S(1)} %bitcast.56), kind=kOutput, calls=%fused_computation.34 | convolution fusion | flops 805830656 | bytes 4460544 | tf_op jit(solution)/shard_map/dot_general | solution.py:39
  86.5 1.8 %fusion.39 = f16[256,1024]{1,0:T(8,128)(2,1)} fusion(bf16[256,1536]{1,0:T(8,128)(2,1)S(1)} %get-tuple-element.201, bf16[2048,1536]{1,0:T(8,128)(2,1)S(1)} %shard_map.68.right, f32[1024]{0:T(1024)S(1)} %bitcast.51), kind=kOutput, calls=%fused_computation.33 | convolution fusion | flops 805830656 | bytes 4460544 | tf_op jit(solution)/shard_map/dot_general | solution.py:39
  88.3 1.8 %fusion.36 = f16[256,1024]{1,0:T(8,128)(2,1)} fusion(bf16[256,1536]{1,0:T(8,128)(2,1)S(1)} %get-tuple-element.203, bf16[2048,1536]{1,0:T(8,128)(2,1)S(1)} %shard_map.68.right, f32[1024]{0:T(1024)S(1)} %bitcast.52), kind=kOutput, calls=%fused_computation.32 | convolution fusion | flops 805830656 | bytes 4460544 | tf_op jit(solution)/shard_map/dot_general | solution.py:39
  90.1 1.8 %fusion.33 = f16[256,1024]{1,0:T(8,128)(2,1)} fusion(bf16[256,1536]{1,0:T(8,128)(2,1)S(1)} %get-tuple-element.205, bf16[2048,1536]{1,0:T(8,128)(2,1)S(1)} %shard_map.68.right, f32[1024]{0:T(1024)S(1)} %bitcast.53), kind=kOutput, calls=%fused_computation.31 | convolution fusion | flops 805830656 | bytes 4460544 | tf_op jit(solution)/shard_map/dot_general | solution.py:39
  91.9 4.5 %shard_map.73.refs_10_ = f32[2,512,768]{2,1,0:T(8,128)S(1)} custom-call(s32[5]{0:T(128)S(1)} %stack.23.at, bf16[528,1024]{1,0:T(8,128)(2,1)S(1)} %shard_map.71.z0.mine, bf16[528,1024]{1,0:T(8,128)(2,1)S(1)} %collective-permute-done.10.z1.up, bf16[528,1024]{1,0:T(8,128)(2,1)S(1)} %collective-permute-done.11.z3.down, bf16[2,512,768]{2,1,0:T(8,128)(2,1)S(1)} %copy-done.3, ...), custom_call_target="tpu_custom_call" | custom-call | flops 1024 | bytes 1024 | tf_op jit(solution)/shard_map/pallas_call | solution.py:47
  96.4 5.4 %shard_map.74.refs_10_ = f32[2,512,768]{2,1,0:T(8,128)} custom-call(s32[5]{0:T(128)S(1)} %stack.23.at, bf16[528,1024]{1,0:T(8,128)(2,1)S(1)} %shard_map.71.z0.mine, bf16[528,1024]{1,0:T(8,128)(2,1)S(1)} %collective-permute-done.10.z1.up, bf16[528,1024]{1,0:T(8,128)(2,1)S(1)} %collective-permute-done.11.z3.down, bf16[2,512,768]{2,1,0:T(8,128)(2,1)S(1)} %copy-done.1, ...), custom_call_target="tpu_custom_call" | custom-call | flops 1024 | bytes 1024 | tf_op jit(solution)/shard_map/pallas_call | solution.py:47
  102.5 0.7 collective-permute-start.22
  103.2 2.5 %collective-permute-start.23 = (f16[256,1024]{1,0:T(8,128)(2,1)}, f16[256,1024]{1,0:T(8,128)(2,1)}, u32[]{:S(2)}, u32[]{:S(2)}) collective-permute-start(f16[256,1024]{1,0:T(8,128)(2,1)} %fusion.42), channel_id=1, source_target_pairs={{0,24},{1,25},{2,26},{3,27},{4,28},{5,29},{6,30},{7,31},{8,0},{9,1... | collective-permute-start | bytes 1572872 | tf_op jit(solution)/shard_map/ppermute | solution.py:35
  106.3 2.6 %collective-permute-start.25 = (f16[256,1024]{1,0:T(8,128)(2,1)}, f16[256,1024]{1,0:T(8,128)(2,1)}, u32[]{:S(2)}, u32[]{:S(2)}) collective-permute-start(f16[256,1024]{1,0:T(8,128)(2,1)} %fusion.36), channel_id=1, source_target_pairs={{0,6},{1,7},{2,0},{3,1},{4,2},{5,3},{6,4},{7,5},{8,14},{9,15},{10,... | collective-permute-start | bytes 1572872 | tf_op jit(solution)/shard_map/ppermute | solution.py:35
  109.0 5.5 %collective-permute-done.14.refs_6_.refs_7_ = bf16[2,512,768]{2,1,0:T(8,128)(2,1)S(1)} collective-permute-done((bf16[2,512,768]{2,1,0:T(8,128)(2,1)S(1)}, bf16[2,512,768]{2,1,0:T(8,128)(2,1)S(1)}, u32[]{:S(2)}, u32[]{:S(2)}) %collective-permute-start.14) | collective-permute-done | bytes 1572896 | tf_op jit(solution)/shard_map/ppermute | solution.py:35
  114.5 2.3 %collective-permute-start.26 = (f16[256,1024]{1,0:T(8,128)(2,1)}, f16[256,1024]{1,0:T(8,128)(2,1)}, u32[]{:S(2)}, u32[]{:S(2)}) collective-permute-start(f16[256,1024]{1,0:T(8,128)(2,1)} %fusion.33), channel_id=1, source_target_pairs={{0,4},{1,5},{2,6},{3,7},{4,0},{5,1},{6,2},{7,3},{8,12},{9,13},{10,... | collective-permute-start | bytes 1572872 | tf_op jit(solution)/shard_map/ppermute | solution.py:35
  116.8 7.3 %shard_map.75 = f32[2,512,768]{2,1,0:T(8,128)} custom-call(s32[5]{0:T(128)S(1)} %stack.23.at, bf16[528,1024]{1,0:T(8,128)(2,1)S(1)} %shard_map.71.z0.mine, bf16[528,1024]{1,0:T(8,128)(2,1)S(1)} %collective-permute-done.10.z1.up, bf16[528,1024]{1,0:T(8,128)(2,1)S(1)} %collective-permute-done.11.z3.down, ...), custom_call_target="tpu_custom_call" | custom-call | flops 1024 | bytes 1024 | tf_op jit(solution)/shard_map/pallas_call | solution.py:47
  124.8 1.8 %shard_map.77 = (f32[256,1024]{1,0:T(8,128)S(1)}, f32[256,1024]{1,0:T(8,128)S(1)}) custom-call(bf16[256,1536]{1,0:T(8,128)(2,1)S(1)} %get-tuple-element.232.left_h, bf16[256,1536]{1,0:T(8,128)(2,1)S(1)} %get-tuple-element.233.left_s, bf16[2048,1536]{1,0:T(8,128)(2,1)S(1)} %shard_map.68.right), custom_call_target="tpu_custom_call" | custom-call | flops 1024 | bytes 1024 | tf_op jit(solution)/shard_map/pallas_call | solution.py:47
  126.7 3.0 %collective-permute-done.25 = f16[256,1024]{1,0:T(8,128)(2,1)} collective-permute-done((f16[256,1024]{1,0:T(8,128)(2,1)}, f16[256,1024]{1,0:T(8,128)(2,1)}, u32[]{:S(2)}, u32[]{:S(2)}) %collective-permute-start.25) | collective-permute-done | bytes 524320 | tf_op jit(solution)/shard_map/ppermute | solution.py:35
  129.6 0.7 collective-permute-done.26
  130.4 1.6 multiply_add_fusion.2
  132.1 1.2 collective-permute-start.27
  133.3 2.1 %collective-permute-start.28 = (f32[64,1024]{1,0:T(8,128)S(1)}, f32[64,1024]{1,0:T(8,128)S(1)}, u32[]{:S(2)}, u32[]{:S(2)}) collective-permute-start(f32[64,1024]{1,0:T(8,128)S(1)} %get-tuple-element.280), channel_id=1, source_target_pairs={{0,6},{1,7},{2,0},{3,1},{4,2},{5,3},{6,4},{7,5},{8,14},{9,15},{10,... | collective-permute-start | bytes 786440 | tf_op jit(solution)/shard_map/ppermute | solution.py:35
  135.4 1.2 collective-permute-start.29
  136.6 0.8 multiply_add_fusion
  137.4 1.8 multiply_add_fusion.1
  139.5 3.2 %collective-permute-start.31 = (f16[64,3072]{1,0:T(8,128)(2,1)S(1)}, f16[64,3072]{1,0:T(8,128)(2,1)S(1)}, u32[]{:S(2)}, u32[]{:S(2)}) collective-permute-start(f16[64,3072]{1,0:T(8,128)(2,1)S(1)} %get-tuple-element.276), channel_id=1, source_target_pairs={{0,24},{1,25},{2,26},{3,27},{4,28},{5,29},{6,30},{7,31},{8,0},{9,1... | collective-permute-start | bytes 1179656 | tf_op jit(solution)/shard_map/ppermute | solution.py:35
  142.8 0.9 collective-permute-start.32
  143.7 1.0 collective-permute-done.28
  144.8 1.0 collective-permute-done.29
  145.8 11.1 %collective-permute-done.30 = f16[64,3072]{1,0:T(8,128)(2,1)S(1)} collective-permute-done((f16[64,3072]{1,0:T(8,128)(2,1)S(1)}, f16[64,3072]{1,0:T(8,128)(2,1)S(1)}, u32[]{:S(2)}, u32[]{:S(2)}) %collective-permute-start.30) | collective-permute-done | bytes 393248 | tf_op jit(solution)/shard_map/ppermute | solution.py:35
  157.3 0.9 collective-permute-start.34
  158.2 5.4 %shard_map.79.refs_10_ = f32[2,512,768]{2,1,0:T(8,128)} custom-call(s32[5]{0:T(128)S(1)} %stack.23.at, bf16[528,1024]{1,0:T(8,128)(2,1)S(1)} %shard_map.71.z0.mine, bf16[528,1024]{1,0:T(8,128)(2,1)S(1)} %collective-permute-done.10.z1.up, bf16[528,1024]{1,0:T(8,128)(2,1)S(1)} %collective-permute-done.11.z3.down, ...), custom_call_target="tpu_custom_call", output_to_operand_aliasing={{}: (14, {})} | custom-call | flops 1024 | bytes 1024 | tf_op jit(solution)/shard_map/pallas_call | solution.py:47
  163.6 5.8 %collective-permute-done.34.got = f32[32,4096]{1,0:T(8,128)S(1)} collective-permute-done((f32[32,4096]{1,0:T(8,128)S(1)}, f32[32,4096]{1,0:T(8,128)S(1)}, u32[]{:S(2)}, u32[]{:S(2)}) %collective-permute-start.34) | collective-permute-done | bytes 524320 | tf_op jit(solution)/shard_map/ppermute | solution.py:35
  169.5 2.0 %collective-permute-start.35 = (f32[32,2048]{1,0:T(8,128)S(1)}, f32[32,2048]{1,0:T(8,128)S(1)}, u32[]{:S(2)}, u32[]{:S(2)}) collective-permute-start(f32[32,2048]{1,0:T(8,128)S(1)} %get-tuple-element.264), channel_id=1, source_target_pairs={{0,64},{1,65},{2,66},{3,67},{4,68},{5,69},{6,70},{7,71},{8,72},{9,... | collective-permute-start | bytes 786440 | tf_op jit(solution)/shard_map/ppermute | solution.py:35
  171.5 5.4 %shard_map.81 = f32[2,512,768]{2,1,0:T(8,128)} custom-call(s32[5]{0:T(128)S(1)} %stack.23.at, bf16[528,1024]{1,0:T(8,128)(2,1)S(1)} %shard_map.71.z0.mine, bf16[528,1024]{1,0:T(8,128)(2,1)S(1)} %collective-permute-done.10.z1.up, bf16[528,1024]{1,0:T(8,128)(2,1)S(1)} %collective-permute-done.11.z3.down, ...), custom_call_target="tpu_custom_call", output_to_operand_aliasing={{}: (14, {})} | custom-call | flops 1024 | bytes 1024 | tf_op jit(solution)/shard_map/pallas_call | solution.py:47
  177.4 1.4 shard_map.82
  (68 shorter events, 7.3 us)
Async XLA Ops:
  0.6 6.3 %collective-permute-start = (bf16[2,512,768]{2,1,0:T(8,128)(2,1)}, bf16[2,512,768]{2,1,0:T(8,128)(2,1)}, u32[]{:S(2)}, u32[]{:S(2)}) collective-permute-start(bf16[2,512,768]{2,1,0:T(8,128)(2,1)} %refs_3_), channel_id=1, source_target_pairs={{0,32},{1,33},{2,34},{3,35},{4,36},{5,37},{6,38},{7,39},{8,40},{9,... | collective-permute-start | bytes 4718600 | tf_op jit(solution)/shard_map/ppermute | solution.py:35
  0.7 6.2 %collective-permute-start.1 = (bf16[2,512,768]{2,1,0:T(8,128)(2,1)}, bf16[2,512,768]{2,1,0:T(8,128)(2,1)}, u32[]{:S(2)}, u32[]{:S(2)}) collective-permute-start(bf16[2,512,768]{2,1,0:T(8,128)(2,1)} %refs_3_.2), channel_id=1, source_target_pairs={{0,32},{1,33},{2,34},{3,35},{4,36},{5,37},{6,38},{7,39},{8,40},{9,... | collective-permute-start | bytes 4718600 | tf_op jit(solution)/shard_map/ppermute | solution.py:35
  1.2 5.7 %collective-permute-start.2 = (bf16[2,64,512]{2,1,0:T(8,128)(2,1)}, bf16[2,64,512]{2,1,0:T(8,128)(2,1)S(1)}, u32[]{:S(2)}, u32[]{:S(2)}) collective-permute-start(bf16[2,64,512]{2,1,0:T(8,128)(2,1)} %own.1), channel_id=1, source_target_pairs={{0,1},{1,0},{2,3},{3,2},{4,5},{5,4},{6,7},{7,6},{8,9},{9,8},{10,11... | collective-permute-start | bytes 393224 | tf_op jit(solution)/shard_map/ppermute | solution.py:35
  2.9 1.4 copy-start
  4.3 1.4 copy-start.2
  5.7 6.3 %copy-start.1 = (bf16[2,512,768]{2,1,0:T(8,128)(2,1)S(1)}, bf16[2,512,768]{2,1,0:T(8,128)(2,1)}, u32[]{:S(2)}) copy-start(bf16[2,512,768]{2,1,0:T(8,128)(2,1)} %refs_3_.2) | copy-start | bytes 4718596
  5.7 6.3 %copy-start.3 = (bf16[2,512,768]{2,1,0:T(8,128)(2,1)S(1)}, bf16[2,512,768]{2,1,0:T(8,128)(2,1)}, u32[]{:S(2)}) copy-start(bf16[2,512,768]{2,1,0:T(8,128)(2,1)} %refs_3_) | copy-start | bytes 4718596
  6.9 0.9 copy-start.4
  8.4 7.6 %collective-permute-start.3 = (bf16[2,2,80,128]{3,2,1,0:T(8,128)(2,1)S(1)}, bf16[2,2,80,128]{3,2,1,0:T(8,128)(2,1)S(1)}, u32[]{:S(2)}, u32[]{:S(2)}) collective-permute-start(bf16[2,2,80,128]{3,2,1,0:T(8,128)(2,1)S(1)} %get-tuple-element.143), channel_id=1, source_target_pairs={{0,32},{1,33},{2,34},{3,35},{4,36},{5,37},{6,38},{7,39},{8,40},{9,... | collective-permute-start | bytes 245768 | tf_op jit(solution)/shard_map/ppermute | solution.py:35
  8.5 7.5 %collective-permute-start.4 = (bf16[2,2,80,128]{3,2,1,0:T(8,128)(2,1)S(1)}, bf16[2,2,80,128]{3,2,1,0:T(8,128)(2,1)S(1)}, u32[]{:S(2)}, u32[]{:S(2)}) collective-permute-start(bf16[2,2,80,128]{3,2,1,0:T(8,128)(2,1)S(1)} %get-tuple-element.144), channel_id=1, source_target_pairs={{0,64},{1,65},{2,66},{3,67},{4,68},{5,69},{6,70},{7,71},{8,72},{9,... | collective-permute-start | bytes 245768 | tf_op jit(solution)/shard_map/ppermute | solution.py:35
  11.9 5.9 %collective-permute-start.5 = (bf16[2,2,80,128]{3,2,1,0:T(8,128)(2,1)S(1)}, bf16[2,2,80,128]{3,2,1,0:T(8,128)(2,1)S(1)}, u32[]{:S(2)}, u32[]{:S(2)}) collective-permute-start(bf16[2,2,80,128]{3,2,1,0:T(8,128)(2,1)S(1)} %get-tuple-element.145), channel_id=1, source_target_pairs={{0,96},{1,97},{2,98},{3,99},{4,100},{5,101},{6,102},{7,103},{8,104... | collective-permute-start | bytes 245768 | tf_op jit(solution)/shard_map/ppermute | solution.py:35
  18.5 21.1 %collective-permute-start.7 = (bf16[528,256]{1,0:T(8,128)(2,1)S(1)}, bf16[528,256]{1,0:T(8,128)(2,1)S(1)}, u32[]{:S(2)}, u32[]{:S(2)}) collective-permute-start(bf16[528,256]{1,0:T(8,128)(2,1)S(1)} %get-tuple-element.170.first), channel_id=1, source_target_pairs={{0,6},{1,7},{2,0},{3,1},{4,2},{5,3},{6,4},{7,5},{8,14},{9,15},{10,... | collective-permute-start | bytes 811016 | tf_op jit(solution)/shard_map/ppermute | solution.py:35
  21.3 18.3 %collective-permute-start.8 = (bf16[528,256]{1,0:T(8,128)(2,1)S(1)}, bf16[528,256]{1,0:T(8,128)(2,1)S(1)}, u32[]{:S(2)}, u32[]{:S(2)}) collective-permute-start(bf16[528,256]{1,0:T(8,128)(2,1)S(1)} %get-tuple-element.170.first), channel_id=1, source_target_pairs={{0,4},{1,5},{2,6},{3,7},{4,0},{5,1},{6,2},{7,3},{8,12},{9,13},{10,... | collective-permute-start | bytes 811016 | tf_op jit(solution)/shard_map/ppermute | solution.py:35
  22.1 17.5 %collective-permute-start.9 = (bf16[528,256]{1,0:T(8,128)(2,1)S(1)}, bf16[528,256]{1,0:T(8,128)(2,1)S(1)}, u32[]{:S(2)}, u32[]{:S(2)}) collective-permute-start(bf16[528,256]{1,0:T(8,128)(2,1)S(1)} %get-tuple-element.170.first), channel_id=1, source_target_pairs={{0,2},{1,3},{2,4},{3,5},{4,6},{5,7},{6,0},{7,1},{8,10},{9,11},{10,... | collective-permute-start | bytes 811016 | tf_op jit(solution)/shard_map/ppermute | solution.py:35
  24.9 14.7 %collective-permute-start.6 = (bf16[2,512,256]{2,1,0:T(8,128)(2,1)S(1)}, bf16[2,512,256]{2,1,0:T(8,128)(2,1)S(1)}, u32[]{:S(2)}, u32[]{:S(2)}) collective-permute-start(bf16[2,512,256]{2,1,0:T(8,128)(2,1)S(1)} %slice.117), channel_id=1, source_target_pairs={{0,64},{1,65},{2,66},{3,67},{4,68},{5,69},{6,70},{7,71},{8,72},{9,... | collective-permute-start | bytes 1572872 | tf_op jit(solution)/shard_map/ppermute | solution.py:35
  40.7 28.8 %collective-permute-start.10 = (bf16[528,1024]{1,0:T(8,128)(2,1)S(1)}, bf16[528,1024]{1,0:T(8,128)(2,1)S(1)}, u32[]{:S(2)}, u32[]{:S(2)}) collective-permute-start(bf16[528,1024]{1,0:T(8,128)(2,1)S(1)} %shard_map.71.z0.mine), channel_id=1, source_target_pairs={{0,24},{1,25},{2,26},{3,27},{4,28},{5,29},{6,30},{7,31},{8,0},{9,1... | collective-permute-start | bytes 3244040 | tf_op jit(solution)/shard_map/ppermute | solution.py:35
  44.8 25.1 %collective-permute-start.11 = (bf16[528,1024]{1,0:T(8,128)(2,1)S(1)}, bf16[528,1024]{1,0:T(8,128)(2,1)S(1)}, u32[]{:S(2)}, u32[]{:S(2)}) collective-permute-start(bf16[528,1024]{1,0:T(8,128)(2,1)S(1)} %shard_map.71.z0.mine), channel_id=1, source_target_pairs={{0,8},{1,9},{2,10},{3,11},{4,12},{5,13},{6,14},{7,15},{8,16},{9,17... | collective-permute-start | bytes 3244040 | tf_op jit(solution)/shard_map/ppermute | solution.py:35
  44.8 24.4 %collective-permute-start.12 = (f16[256,2048]{1,0:T(8,128)(2,1)S(1)}, f16[256,2048]{1,0:T(8,128)(2,1)S(1)}, u32[]{:S(2)}, u32[]{:S(2)}) collective-permute-start(f16[256,2048]{1,0:T(8,128)(2,1)S(1)} %fusion), channel_id=1, source_target_pairs={{0,2},{1,3},{2,4},{3,5},{4,6},{5,7},{6,0},{7,1},{8,10},{9,11},{10,... | collective-permute-start | bytes 3145736 | tf_op jit(solution)/shard_map/ppermute | solution.py:35
  46.6 22.9 %collective-permute-start.13 = (f16[256,2048]{1,0:T(8,128)(2,1)S(1)}, f16[256,2048]{1,0:T(8,128)(2,1)S(1)}, u32[]{:S(2)}, u32[]{:S(2)}) collective-permute-start(f16[256,2048]{1,0:T(8,128)(2,1)S(1)} %fusion.1), channel_id=1, source_target_pairs={{0,6},{1,7},{2,0},{3,1},{4,2},{5,3},{6,4},{7,5},{8,14},{9,15},{10,... | collective-permute-start | bytes 3145736 | tf_op jit(solution)/shard_map/ppermute | solution.py:35
  48.1 24.2 %collective-permute-start.15 = (bf16[2,512,512]{2,1,0:T(8,128)(2,1)S(1)}, bf16[2,512,512]{2,1,0:T(8,128)(2,1)S(1)}, u32[]{:S(2)}, u32[]{:S(2)}) collective-permute-start(bf16[2,512,512]{2,1,0:T(8,128)(2,1)S(1)} %slice.119), channel_id=1, source_target_pairs={{0,64},{1,65},{2,66},{3,67},{4,68},{5,69},{6,70},{7,71},{8,72},{9,... | collective-permute-start | bytes 3145736 | tf_op jit(solution)/shard_map/ppermute | solution.py:35
  72.3 7.2 %collective-permute-start.20 = (bf16[2,512,512]{2,1,0:T(8,128)(2,1)S(1)}, bf16[2,512,512]{2,1,0:T(8,128)(2,1)S(1)}, u32[]{:S(2)}, u32[]{:S(2)}) collective-permute-start(bf16[2,512,512]{2,1,0:T(8,128)(2,1)S(1)} %collective-permute-done.15.refs_1_.refs_7_), channel_id=1, source_target_pairs={{0,32},{1,33},{2,34},{3,35},{4,36},{5,37},{6,38},{7,39},{8,40},{9,... | collective-permute-start | bytes 3145736 | tf_op jit(solution)/shard_map/ppermute | solution.py:35
  72.3 5.2 %collective-permute-start.19 = (bf16[2,512,256]{2,1,0:T(8,128)(2,1)S(1)}, bf16[2,512,256]{2,1,0:T(8,128)(2,1)S(1)}, u32[]{:S(2)}, u32[]{:S(2)}) collective-permute-start(bf16[2,512,256]{2,1,0:T(8,128)(2,1)S(1)} %collective-permute-done.6.refs_0_.refs_6_), channel_id=1, source_target_pairs={{0,32},{1,33},{2,34},{3,35},{4,36},{5,37},{6,38},{7,39},{8,40},{9,... | collective-permute-start | bytes 1572872 | tf_op jit(solution)/shard_map/ppermute | solution.py:35
  72.8 29.0 %collective-permute-start.17 = (bf16[528,512]{1,0:T(8,128)(2,1)S(1)}, bf16[528,512]{1,0:T(8,128)(2,1)S(1)}, u32[]{:S(2)}, u32[]{:S(2)}) collective-permute-start(bf16[528,512]{1,0:T(8,128)(2,1)S(1)} %slice.120), channel_id=1, source_target_pairs={{0,8},{1,9},{2,10},{3,11},{4,12},{5,13},{6,14},{7,15},{8,16},{9,17... | collective-permute-start | bytes 1622024 | tf_op jit(solution)/shard_map/ppermute | solution.py:35
  73.0 28.8 %collective-permute-start.18 = (bf16[528,512]{1,0:T(8,128)(2,1)S(1)}, bf16[528,512]{1,0:T(8,128)(2,1)S(1)}, u32[]{:S(2)}, u32[]{:S(2)}) collective-permute-start(bf16[528,512]{1,0:T(8,128)(2,1)S(1)} %slice.121), channel_id=1, source_target_pairs={{0,24},{1,25},{2,26},{3,27},{4,28},{5,29},{6,30},{7,31},{8,0},{9,1... | collective-permute-start | bytes 1622024 | tf_op jit(solution)/shard_map/ppermute | solution.py:35
  76.3 26.2 %collective-permute-start.16 = (f16[256,2048]{1,0:T(8,128)(2,1)}, f16[256,2048]{1,0:T(8,128)(2,1)S(1)}, u32[]{:S(2)}, u32[]{:S(2)}) collective-permute-start(f16[256,2048]{1,0:T(8,128)(2,1)} %fusion.2), channel_id=1, source_target_pairs={{0,4},{1,5},{2,6},{3,7},{4,0},{5,1},{6,2},{7,3},{8,12},{9,13},{10,... | collective-permute-start | bytes 3145736 | tf_op jit(solution)/shard_map/ppermute | solution.py:35
  77.5 37.0 %collective-permute-start.14 = (bf16[2,512,768]{2,1,0:T(8,128)(2,1)S(1)}, bf16[2,512,768]{2,1,0:T(8,128)(2,1)S(1)}, u32[]{:S(2)}, u32[]{:S(2)}) collective-permute-start(bf16[2,512,768]{2,1,0:T(8,128)(2,1)S(1)} %copy-done.1), channel_id=1, source_target_pairs={{0,64},{1,65},{2,66},{3,67},{4,68},{5,69},{6,70},{7,71},{8,72},{9,... | collective-permute-start | bytes 4718600 | tf_op jit(solution)/shard_map/ppermute | solution.py:35
  81.4 21.1 %collective-permute-start.21 = (f16[256,1024]{1,0:T(8,128)(2,1)S(1)}, f16[256,1024]{1,0:T(8,128)(2,1)S(1)}, u32[]{:S(2)}, u32[]{:S(2)}) collective-permute-start(f16[256,1024]{1,0:T(8,128)(2,1)S(1)} %fusion.48), channel_id=1, source_target_pairs={{0,16},{1,17},{2,18},{3,19},{4,20},{5,21},{6,22},{7,23},{8,24},{9,... | collective-permute-start | bytes 1572872 | tf_op jit(solution)/shard_map/ppermute | solution.py:35
  102.5 12.0 %copy-start.5 = (f16[256,1024]{1,0:T(8,128)(2,1)}, f16[256,1024]{1,0:T(8,128)(2,1)S(1)}, u32[]{:S(2)}) copy-start(f16[256,1024]{1,0:T(8,128)(2,1)S(1)} %collective-permute-done.21) | copy-start | bytes 1572868
  102.5 24.1 %collective-permute-start.22 = (f16[256,1024]{1,0:T(8,128)(2,1)}, f16[256,1024]{1,0:T(8,128)(2,1)}, u32[]{:S(2)}, u32[]{:S(2)}) collective-permute-start(f16[256,1024]{1,0:T(8,128)(2,1)} %fusion.45), channel_id=1, source_target_pairs={{0,8},{1,9},{2,10},{3,11},{4,12},{5,13},{6,14},{7,15},{8,16},{9,17... | collective-permute-start | bytes 1572872 | tf_op jit(solution)/shard_map/ppermute | solution.py:35
  103.2 23.4 %collective-permute-start.23 = (f16[256,1024]{1,0:T(8,128)(2,1)}, f16[256,1024]{1,0:T(8,128)(2,1)}, u32[]{:S(2)}, u32[]{:S(2)}) collective-permute-start(f16[256,1024]{1,0:T(8,128)(2,1)} %fusion.42), channel_id=1, source_target_pairs={{0,24},{1,25},{2,26},{3,27},{4,28},{5,29},{6,30},{7,31},{8,0},{9,1... | collective-permute-start | bytes 1572872 | tf_op jit(solution)/shard_map/ppermute | solution.py:35
  105.8 20.9 %collective-permute-start.24 = (f16[256,1024]{1,0:T(8,128)(2,1)}, f16[256,1024]{1,0:T(8,128)(2,1)}, u32[]{:S(2)}, u32[]{:S(2)}) collective-permute-start(f16[256,1024]{1,0:T(8,128)(2,1)} %fusion.39), channel_id=1, source_target_pairs={{0,2},{1,3},{2,4},{3,5},{4,6},{5,7},{6,0},{7,1},{8,10},{9,11},{10,... | collective-permute-start | bytes 1572872 | tf_op jit(solution)/shard_map/ppermute | solution.py:35
  106.3 23.3 %collective-permute-start.25 = (f16[256,1024]{1,0:T(8,128)(2,1)}, f16[256,1024]{1,0:T(8,128)(2,1)}, u32[]{:S(2)}, u32[]{:S(2)}) collective-permute-start(f16[256,1024]{1,0:T(8,128)(2,1)} %fusion.36), channel_id=1, source_target_pairs={{0,6},{1,7},{2,0},{3,1},{4,2},{5,3},{6,4},{7,5},{8,14},{9,15},{10,... | collective-permute-start | bytes 1572872 | tf_op jit(solution)/shard_map/ppermute | solution.py:35
  114.5 15.8 %collective-permute-start.26 = (f16[256,1024]{1,0:T(8,128)(2,1)}, f16[256,1024]{1,0:T(8,128)(2,1)}, u32[]{:S(2)}, u32[]{:S(2)}) collective-permute-start(f16[256,1024]{1,0:T(8,128)(2,1)} %fusion.33), channel_id=1, source_target_pairs={{0,4},{1,5},{2,6},{3,7},{4,0},{5,1},{6,2},{7,3},{8,12},{9,13},{10,... | collective-permute-start | bytes 1572872 | tf_op jit(solution)/shard_map/ppermute | solution.py:35
  124.8 5.6 %copy-start.6 = (f16[256,1024]{1,0:T(8,128)(2,1)S(1)}, f16[256,1024]{1,0:T(8,128)(2,1)}, u32[]{:S(2)}) copy-start(f16[256,1024]{1,0:T(8,128)(2,1)} %copy-done.5) | copy-start | bytes 1572868
  132.1 10.7 %collective-permute-start.27 = (f32[64,1024]{1,0:T(8,128)S(1)}, f32[64,1024]{1,0:T(8,128)S(1)}, u32[]{:S(2)}, u32[]{:S(2)}) collective-permute-start(f32[64,1024]{1,0:T(8,128)S(1)} %get-tuple-element.278), channel_id=1, source_target_pairs={{0,2},{1,3},{2,4},{3,5},{4,6},{5,7},{6,0},{7,1},{8,10},{9,11},{10,... | collective-permute-start | bytes 786440 | tf_op jit(solution)/shard_map/ppermute | solution.py:35
  133.3 11.4 %collective-permute-start.28 = (f32[64,1024]{1,0:T(8,128)S(1)}, f32[64,1024]{1,0:T(8,128)S(1)}, u32[]{:S(2)}, u32[]{:S(2)}) collective-permute-start(f32[64,1024]{1,0:T(8,128)S(1)} %get-tuple-element.280), channel_id=1, source_target_pairs={{0,6},{1,7},{2,0},{3,1},{4,2},{5,3},{6,4},{7,5},{8,14},{9,15},{10,... | collective-permute-start | bytes 786440 | tf_op jit(solution)/shard_map/ppermute | solution.py:35
  135.4 10.4 %collective-permute-start.29 = (f32[64,1024]{1,0:T(8,128)S(1)}, f32[64,1024]{1,0:T(8,128)S(1)}, u32[]{:S(2)}, u32[]{:S(2)}) collective-permute-start(f32[64,1024]{1,0:T(8,128)S(1)} %get-tuple-element.279), channel_id=1, source_target_pairs={{0,4},{1,5},{2,6},{3,7},{4,0},{5,1},{6,2},{7,3},{8,12},{9,13},{10,... | collective-permute-start | bytes 786440 | tf_op jit(solution)/shard_map/ppermute | solution.py:35
  139.4 17.5 %collective-permute-start.30 = (f16[64,3072]{1,0:T(8,128)(2,1)S(1)}, f16[64,3072]{1,0:T(8,128)(2,1)S(1)}, u32[]{:S(2)}, u32[]{:S(2)}) collective-permute-start(f16[64,3072]{1,0:T(8,128)(2,1)S(1)} %get-tuple-element.274), channel_id=1, source_target_pairs={{0,8},{1,9},{2,10},{3,11},{4,12},{5,13},{6,14},{7,15},{8,16},{9,17... | collective-permute-start | bytes 1179656 | tf_op jit(solution)/shard_map/ppermute | solution.py:35
  139.5 17.5 %collective-permute-start.31 = (f16[64,3072]{1,0:T(8,128)(2,1)S(1)}, f16[64,3072]{1,0:T(8,128)(2,1)S(1)}, u32[]{:S(2)}, u32[]{:S(2)}) collective-permute-start(f16[64,3072]{1,0:T(8,128)(2,1)S(1)} %get-tuple-element.276), channel_id=1, source_target_pairs={{0,24},{1,25},{2,26},{3,27},{4,28},{5,29},{6,30},{7,31},{8,0},{9,1... | collective-permute-start | bytes 1179656 | tf_op jit(solution)/shard_map/ppermute | solution.py:35
  142.8 14.2 %collective-permute-start.32 = (f16[64,3072]{1,0:T(8,128)(2,1)S(1)}, f16[64,3072]{1,0:T(8,128)(2,1)S(1)}, u32[]{:S(2)}, u32[]{:S(2)}) collective-permute-start(f16[64,3072]{1,0:T(8,128)(2,1)S(1)} %get-tuple-element.275), channel_id=1, source_target_pairs={{0,16},{1,17},{2,18},{3,19},{4,20},{5,21},{6,22},{7,23},{8,24},{9,... | collective-permute-start | bytes 1179656 | tf_op jit(solution)/shard_map/ppermute | solution.py:35
  144.7 13.5 %collective-permute-start.33 = (bf16[2,512,768]{2,1,0:T(8,128)(2,1)S(1)}, bf16[2,512,768]{2,1,0:T(8,128)(2,1)S(1)}, u32[]{:S(2)}, u32[]{:S(2)}) collective-permute-start(bf16[2,512,768]{2,1,0:T(8,128)(2,1)S(1)} %collective-permute-done.14.refs_6_.refs_7_), channel_id=1, source_target_pairs={{0,32},{1,33},{2,34},{3,35},{4,36},{5,37},{6,38},{7,39},{8,40},{9,... | collective-permute-start | bytes 4718600 | tf_op jit(solution)/shard_map/ppermute | solution.py:35
  157.3 12.1 %collective-permute-start.34 = (f32[32,4096]{1,0:T(8,128)S(1)}, f32[32,4096]{1,0:T(8,128)S(1)}, u32[]{:S(2)}, u32[]{:S(2)}) collective-permute-start(f32[32,4096]{1,0:T(8,128)S(1)} %get-tuple-element.255), channel_id=1, source_target_pairs={{0,1},{1,0},{2,3},{3,2},{4,5},{5,4},{6,7},{7,6},{8,9},{9,8},{10,11... | collective-permute-start | bytes 1572872 | tf_op jit(solution)/shard_map/ppermute | solution.py:35
  169.5 8.0 %collective-permute-start.35 = (f32[32,2048]{1,0:T(8,128)S(1)}, f32[32,2048]{1,0:T(8,128)S(1)}, u32[]{:S(2)}, u32[]{:S(2)}) collective-permute-start(f32[32,2048]{1,0:T(8,128)S(1)} %get-tuple-element.264), channel_id=1, source_target_pairs={{0,64},{1,65},{2,66},{3,67},{4,68},{5,69},{6,70},{7,71},{8,72},{9,... | collective-permute-start | bytes 786440 | tf_op jit(solution)/shard_map/ppermute | solution.py:35

commit v7 on v6

--- a/solution.py
+++ b/solution.py
@@ -336,9 +336,9 @@
     cross_b = move(psi[:, :, 256:768], y_hi=1)
     near_2 = for_peer(after(near_left[2], mine), right, scale)
     near_own = dot_rows(after(near_left[0], near_2), right)
+    cross_b, near_2, near_own = fence((cross_b, near_2, near_own))
     hpsi, cross_a, mine, up, down, near_got, near_2, near_own, right = fence(
         (hpsi, cross_a, mine, up, down, near_got, near_2, near_own, right))
-    cross_b, near_2, up, down = fence((cross_b, near_2, up, down))
 
     mate_a, mate_b = move(cross_a, core=1), move(cross_b, core=1)
     near_got.append(move(near_2, dx=2))

time: 179 us -> 182 us (1.017)
  transfers between devices with their start and end apart: 36 -> 36, of which waited for: 16 -> 14; matrix products, arithmetic and copies ran while one was open for 12% -> 12% of each run, Pallas kernels for 20% -> 20%
where the time goes in v7:
time: 182 us; the launch traced here: 181 us
  waiting for transfers between devices  61.8 us (34%)
  starting transfers between devices  51.1 us (28%)
  Pallas kernels  40.2 us (22%)
  matrix products  18.4 us (10%)
  other arithmetic  4.8 us (3%)
  local copies, waits for them, and re-layouts  4.14 us (2%)
    ppermute x36, waiting for transfers between devices, move(): return lax.ppermute(value, ('band', 'ga'), pairs)  61.8 us
    ppermute x36, starting transfers between devices, move(): return lax.ppermute(value, ('band', 'ga'), pairs)  51.1 us
    pallas_call x17, Pallas kernels, call(): pl.pallas_call(kernel, out_shape=outs, compiler_params=pltpu.CompilerPara...  40.2 us
    dot_general x10, matrix products, dot_rows(): lax.dot_general(left, right, (((1,), (1,)), ((), ())), preferred_element_...  18.4 us
    unnamed x14, local copies, waits for them, and re-layouts  3.73 us
  transfers between devices with their start and end apart: 36, of which 14 were waited for; matrix products, arithmetic and copies ran while one was open for 12% of the time, Pallas kernels for 20%

profile of v7, /device:TPU:0, one launch (start us, length us, event | category | flops | bytes accessed | tf_op | source)
XLA Modules:
  0.0 181.4 jit_solution(2544643100966897301)
XLA Ops:
  1.2 1.7 collective-permute-start.2
  2.9 1.4 copy-done
  4.3 1.4 copy-done.2
  5.7 0.9 shard_map.66.largest
  6.9 0.9 copy-done.4
  8.5 3.4 %collective-permute-start.4 = (bf16[2,2,80,128]{3,2,1,0:T(8,128)(2,1)S(1)}, bf16[2,2,80,128]{3,2,1,0:T(8,128)(2,1)S(1)}, u32[]{:S(2)}, u32[]{:S(2)}) collective-permute-start(bf16[2,2,80,128]{3,2,1,0:T(8,128)(2,1)S(1)} %get-tuple-element.143), channel_id=1, source_target_pairs={{0,64},{1,65},{2,66},{3,67},{4,68},{5,69},{6,70},{7,71},{8,72},{9,... | collective-permute-start | bytes 245768 | tf_op jit(solution)/shard_map/ppermute | solution.py:35
  12.0 2.3 %shard_map.68.right = bf16[2048,1536]{1,0:T(8,128)(2,1)S(1)} custom-call(s32[5]{0:T(128)S(1)} %stack.23.at, bf16[2,512,768]{2,1,0:T(8,128)(2,1)S(1)} %copy-done.3, bf16[2,512,768]{2,1,0:T(8,128)(2,1)} %collective-permute-done.psi_mate.refs_1_.refs_2_.refs_3_.refs_4_.refs_5_, bf16[2,512,768]{2,1,0:T(8,128)(2,1)S(1)} %copy-done.1, ...), custom_call_target="tpu_custom_call" | custom-call | flops 1024 | bytes 1024 | tf_op jit(solution)/shard_map/pallas_call | solution.py:47
  14.3 1.8 shard_map.69
  16.0 1.8 collective-permute-done.5.fourth
  18.5 2.8 %collective-permute-start.7 = (bf16[528,256]{1,0:T(8,128)(2,1)S(1)}, bf16[528,256]{1,0:T(8,128)(2,1)S(1)}, u32[]{:S(2)}, u32[]{:S(2)}) collective-permute-start(bf16[528,256]{1,0:T(8,128)(2,1)S(1)} %get-tuple-element.169.first), channel_id=1, source_target_pairs={{0,6},{1,7},{2,0},{3,1},{4,2},{5,3},{6,4},{7,5},{8,14},{9,15},{10,... | collective-permute-start | bytes 811016 | tf_op jit(solution)/shard_map/ppermute | solution.py:35
  21.3 0.8 collective-permute-start.8
  22.1 0.9 collective-permute-start.9
  23.0 1.8 %fusion = f16[256,2048]{1,0:T(8,128)(2,1)S(1)} fusion(bf16[256,1536]{1,0:T(8,128)(2,1)S(1)} %get-tuple-element.161, bf16[2048,1536]{1,0:T(8,128)(2,1)S(1)} %shard_map.68.right, f32[2048]{0:T(1024)S(1)} %bitcast.48), kind=kOutput, calls=%fused_computation.9 | convolution fusion | flops 1611661312 | bytes 8134656 | tf_op jit(solution)/shard_map/dot_general | solution.py:39
  24.9 1.7 collective-permute-start.6
  26.6 1.8 %fusion.1 = f16[256,2048]{1,0:T(8,128)(2,1)S(1)} fusion(bf16[256,1536]{1,0:T(8,128)(2,1)S(1)} %get-tuple-element.165, bf16[2048,1536]{1,0:T(8,128)(2,1)S(1)} %shard_map.68.right, f32[2048]{0:T(1024)S(1)} %bitcast.49), kind=kOutput, calls=%fused_computation.10 | convolution fusion | flops 1611661312 | bytes 8134656 | tf_op jit(solution)/shard_map/dot_general | solution.py:39
  28.4 11.2 %collective-permute-done.6.refs_0_.refs_6_ = bf16[2,512,256]{2,1,0:T(8,128)(2,1)S(1)} collective-permute-done((bf16[2,512,256]{2,1,0:T(8,128)(2,1)S(1)}, bf16[2,512,256]{2,1,0:T(8,128)(2,1)S(1)}, u32[]{:S(2)}, u32[]{:S(2)}) %collective-permute-start.6) | collective-permute-done | bytes 524320 | tf_op jit(solution)/shard_map/ppermute | solution.py:35
  39.6 1.0 shard_map.71.z0.mine
  40.7 4.1 %collective-permute-start.10 = (bf16[528,1024]{1,0:T(8,128)(2,1)S(1)}, bf16[528,1024]{1,0:T(8,128)(2,1)S(1)}, u32[]{:S(2)}, u32[]{:S(2)}) collective-permute-start(bf16[528,1024]{1,0:T(8,128)(2,1)S(1)} %shard_map.71.z0.mine), channel_id=1, source_target_pairs={{0,24},{1,25},{2,26},{3,27},{4,28},{5,29},{6,30},{7,31},{8,0},{9,1... | collective-permute-start | bytes 3244040 | tf_op jit(solution)/shard_map/ppermute | solution.py:35
  44.8 1.9 %collective-permute-start.14 = (bf16[2,512,512]{2,1,0:T(8,128)(2,1)S(1)}, bf16[2,512,512]{2,1,0:T(8,128)(2,1)S(1)}, u32[]{:S(2)}, u32[]{:S(2)}) collective-permute-start(bf16[2,512,512]{2,1,0:T(8,128)(2,1)S(1)} %slice.119), channel_id=1, source_target_pairs={{0,64},{1,65},{2,66},{3,67},{4,68},{5,69},{6,70},{7,71},{8,72},{9,... | collective-permute-start | bytes 3145736 | tf_op jit(solution)/shard_map/ppermute | solution.py:35
  46.7 2.8 %fusion.2 = f16[256,2048]{1,0:T(8,128)(2,1)} fusion(bf16[256,1536]{1,0:T(8,128)(2,1)S(1)} %get-tuple-element.177, bf16[2048,1536]{1,0:T(8,128)(2,1)S(1)} %shard_map.68.right, f32[2048]{0:T(1024)S(1)} %bitcast.50), kind=kOutput, calls=%fused_computation.11 | convolution fusion | flops 1611661312 | bytes 8134656 | tf_op jit(solution)/shard_map/dot_general | solution.py:39
  49.5 1.8 collective-permute-start.12
  51.3 1.4 collective-permute-start.13
  52.7 1.8 %fusion.66 = f32[256,2048]{1,0:T(8,128)S(1)} fusion(bf16[256,1536]{1,0:T(8,128)(2,1)S(1)} %get-tuple-element.180, bf16[2048,1536]{1,0:T(8,128)(2,1)S(1)} %shard_map.68.right), kind=kOutput, calls=%fused_computation.61 | convolution fusion | flops 1610612736 | bytes 9175040 | tf_op jit(solution)/shard_map/dot_general | solution.py:39
  54.6 15.0 %collective-permute-done.14.refs_1_.refs_7_ = bf16[2,512,512]{2,1,0:T(8,128)(2,1)S(1)} collective-permute-done((bf16[2,512,512]{2,1,0:T(8,128)(2,1)S(1)}, bf16[2,512,512]{2,1,0:T(8,128)(2,1)S(1)}, u32[]{:S(2)}, u32[]{:S(2)}) %collective-permute-start.14) | collective-permute-done | bytes 1048608 | tf_op jit(solution)/shard_map/ppermute | solution.py:35
  69.6 4.1 %collective-permute-done.12 = f16[256,2048]{1,0:T(8,128)(2,1)S(1)} collective-permute-done((f16[256,2048]{1,0:T(8,128)(2,1)S(1)}, f16[256,2048]{1,0:T(8,128)(2,1)S(1)}, u32[]{:S(2)}, u32[]{:S(2)}) %collective-permute-start.12) | collective-permute-done | bytes 1048608 | tf_op jit(solution)/shard_map/ppermute | solution.py:35
  74.3 3.3 %collective-permute-start.18 = (bf16[528,512]{1,0:T(8,128)(2,1)S(1)}, bf16[528,512]{1,0:T(8,128)(2,1)S(1)}, u32[]{:S(2)}, u32[]{:S(2)}) collective-permute-start(bf16[528,512]{1,0:T(8,128)(2,1)S(1)} %slice.121), channel_id=1, source_target_pairs={{0,24},{1,25},{2,26},{3,27},{4,28},{5,29},{6,30},{7,31},{8,0},{9,1... | collective-permute-start | bytes 1622024 | tf_op jit(solution)/shard_map/ppermute | solution.py:35
  77.6 2.0 %collective-permute-start.16 = (f16[256,2048]{1,0:T(8,128)(2,1)}, f16[256,2048]{1,0:T(8,128)(2,1)S(1)}, u32[]{:S(2)}, u32[]{:S(2)}) collective-permute-start(f16[256,2048]{1,0:T(8,128)(2,1)} %fusion.2), channel_id=1, source_target_pairs={{0,4},{1,5},{2,6},{3,7},{4,0},{5,1},{6,2},{7,3},{8,12},{9,13},{10,... | collective-permute-start | bytes 3145736 | tf_op jit(solution)/shard_map/ppermute | solution.py:35
  79.6 1.6 collective-permute-start.15
  81.2 1.0 shard_map.72
  82.1 1.0 fusion.48
  83.2 1.4 collective-permute-start.21
  84.5 1.9 %fusion.45 = f16[256,1024]{1,0:T(8,128)(2,1)} fusion(bf16[256,1536]{1,0:T(8,128)(2,1)S(1)} %get-tuple-element.195, bf16[2048,1536]{1,0:T(8,128)(2,1)S(1)} %shard_map.68.right, f32[1024]{0:T(1024)S(1)} %bitcast.55), kind=kOutput, calls=%fused_computation.35 | convolution fusion | flops 805830656 | bytes 4460544 | tf_op jit(solution)/shard_map/dot_general | solution.py:39
  86.4 1.8 fusion.42
  88.2 1.8 %fusion.39 = f16[256,1024]{1,0:T(8,128)(2,1)} fusion(bf16[256,1536]{1,0:T(8,128)(2,1)S(1)} %get-tuple-element.199, bf16[2048,1536]{1,0:T(8,128)(2,1)S(1)} %shard_map.68.right, f32[1024]{0:T(1024)S(1)} %bitcast.51), kind=kOutput, calls=%fused_computation.33 | convolution fusion | flops 805830656 | bytes 4460544 | tf_op jit(solution)/shard_map/dot_general | solution.py:39
  90.0 1.8 %fusion.36 = f16[256,1024]{1,0:T(8,128)(2,1)} fusion(bf16[256,1536]{1,0:T(8,128)(2,1)S(1)} %get-tuple-element.201, bf16[2048,1536]{1,0:T(8,128)(2,1)S(1)} %shard_map.68.right, f32[1024]{0:T(1024)S(1)} %bitcast.52), kind=kOutput, calls=%fused_computation.32 | convolution fusion | flops 805830656 | bytes 4460544 | tf_op jit(solution)/shard_map/dot_general | solution.py:39
  91.9 1.8 fusion.33
  93.6 4.5 %shard_map.73.refs_10_ = f32[2,512,768]{2,1,0:T(8,128)S(1)} custom-call(s32[5]{0:T(128)S(1)} %stack.23.at, bf16[528,1024]{1,0:T(8,128)(2,1)S(1)} %shard_map.71.z0.mine, bf16[528,1024]{1,0:T(8,128)(2,1)S(1)} %collective-permute-done.10.z1.up, bf16[528,1024]{1,0:T(8,128)(2,1)S(1)} %collective-permute-done.11.z3.down, bf16[2,512,768]{2,1,0:T(8,128)(2,1)S(1)} %copy-done.3, ...), custom_call_target="tpu_custom_call" | custom-call | flops 1024 | bytes 1024 | tf_op jit(solution)/shard_map/pallas_call | solution.py:47
  98.1 5.4 %shard_map.74.refs_10_ = f32[2,512,768]{2,1,0:T(8,128)} custom-call(s32[5]{0:T(128)S(1)} %stack.23.at, bf16[528,1024]{1,0:T(8,128)(2,1)S(1)} %shard_map.71.z0.mine, bf16[528,1024]{1,0:T(8,128)(2,1)S(1)} %collective-permute-done.10.z1.up, bf16[528,1024]{1,0:T(8,128)(2,1)S(1)} %collective-permute-done.11.z3.down, bf16[2,512,768]{2,1,0:T(8,128)(2,1)S(1)} %copy-done.1, ...), custom_call_target="tpu_custom_call" | custom-call | flops 1024 | bytes 1024 | tf_op jit(solution)/shard_map/pallas_call | solution.py:47
  103.6 0.7 collective-permute-done.16
  104.3 0.7 collective-permute-start.22
  105.0 2.6 %collective-permute-start.23 = (f16[256,1024]{1,0:T(8,128)(2,1)}, f16[256,1024]{1,0:T(8,128)(2,1)}, u32[]{:S(2)}, u32[]{:S(2)}) collective-permute-start(f16[256,1024]{1,0:T(8,128)(2,1)} %fusion.42), channel_id=1, source_target_pairs={{0,24},{1,25},{2,26},{3,27},{4,28},{5,29},{6,30},{7,31},{8,0},{9,1... | collective-permute-start | bytes 1572872 | tf_op jit(solution)/shard_map/ppermute | solution.py:35
  107.5 0.8 collective-permute-start.24
  108.4 2.4 %collective-permute-start.25 = (f16[256,1024]{1,0:T(8,128)(2,1)}, f16[256,1024]{1,0:T(8,128)(2,1)}, u32[]{:S(2)}, u32[]{:S(2)}) collective-permute-start(f16[256,1024]{1,0:T(8,128)(2,1)} %fusion.36), channel_id=1, source_target_pairs={{0,6},{1,7},{2,0},{3,1},{4,2},{5,3},{6,4},{7,5},{8,14},{9,15},{10,... | collective-permute-start | bytes 1572872 | tf_op jit(solution)/shard_map/ppermute | solution.py:35
  110.8 6.3 %collective-permute-done.15.refs_6_.refs_7_ = bf16[2,512,768]{2,1,0:T(8,128)(2,1)S(1)} collective-permute-done((bf16[2,512,768]{2,1,0:T(8,128)(2,1)S(1)}, bf16[2,512,768]{2,1,0:T(8,128)(2,1)S(1)}, u32[]{:S(2)}, u32[]{:S(2)}) %collective-permute-start.15) | collective-permute-done | bytes 1572896 | tf_op jit(solution)/shard_map/ppermute | solution.py:35
  117.1 1.5 collective-permute-start.26
  118.6 7.3 %shard_map.75 = f32[2,512,768]{2,1,0:T(8,128)} custom-call(s32[5]{0:T(128)S(1)} %stack.23.at, bf16[528,1024]{1,0:T(8,128)(2,1)S(1)} %shard_map.71.z0.mine, bf16[528,1024]{1,0:T(8,128)(2,1)S(1)} %collective-permute-done.10.z1.up, bf16[528,1024]{1,0:T(8,128)(2,1)S(1)} %collective-permute-done.11.z3.down, ...), custom_call_target="tpu_custom_call" | custom-call | flops 1024 | bytes 1024 | tf_op jit(solution)/shard_map/pallas_call | solution.py:47
  126.6 1.8 %shard_map.77 = (f32[256,1024]{1,0:T(8,128)S(1)}, f32[256,1024]{1,0:T(8,128)S(1)}) custom-call(bf16[256,1536]{1,0:T(8,128)(2,1)S(1)} %get-tuple-element.230.left_h, bf16[256,1536]{1,0:T(8,128)(2,1)S(1)} %get-tuple-element.231.left_s, bf16[2048,1536]{1,0:T(8,128)(2,1)S(1)} %shard_map.68.right), custom_call_target="tpu_custom_call" | custom-call | flops 1024 | bytes 1024 | tf_op jit(solution)/shard_map/pallas_call | solution.py:47
  128.5 3.5 %collective-permute-done.25 = f16[256,1024]{1,0:T(8,128)(2,1)} collective-permute-done((f16[256,1024]{1,0:T(8,128)(2,1)}, f16[256,1024]{1,0:T(8,128)(2,1)}, u32[]{:S(2)}, u32[]{:S(2)}) %collective-permute-start.25) | collective-permute-done | bytes 524320 | tf_op jit(solution)/shard_map/ppermute | solution.py:35
  131.9 1.6 collective-permute-done.26
  133.6 1.6 multiply_add_fusion.2
  135.3 1.2 collective-permute-start.27
  136.5 2.1 %collective-permute-start.28 = (f32[64,1024]{1,0:T(8,128)S(1)}, f32[64,1024]{1,0:T(8,128)S(1)}, u32[]{:S(2)}, u32[]{:S(2)}) collective-permute-start(f32[64,1024]{1,0:T(8,128)S(1)} %get-tuple-element.278), channel_id=1, source_target_pairs={{0,6},{1,7},{2,0},{3,1},{4,2},{5,3},{6,4},{7,5},{8,14},{9,15},{10,... | collective-permute-start | bytes 786440 | tf_op jit(solution)/shard_map/ppermute | solution.py:35
  138.9 0.8 multiply_add_fusion
  139.7 1.8 multiply_add_fusion.1
  141.8 3.2 %collective-permute-start.31 = (f16[64,3072]{1,0:T(8,128)(2,1)S(1)}, f16[64,3072]{1,0:T(8,128)(2,1)S(1)}, u32[]{:S(2)}, u32[]{:S(2)}) collective-permute-start(f16[64,3072]{1,0:T(8,128)(2,1)S(1)} %get-tuple-element.274), channel_id=1, source_target_pairs={{0,24},{1,25},{2,26},{3,27},{4,28},{5,29},{6,30},{7,31},{8,0},{9,1... | collective-permute-start | bytes 1179656 | tf_op jit(solution)/shard_map/ppermute | solution.py:35
  145.7 4.3 %collective-permute-start.32 = (f16[64,3072]{1,0:T(8,128)(2,1)S(1)}, f16[64,3072]{1,0:T(8,128)(2,1)S(1)}, u32[]{:S(2)}, u32[]{:S(2)}) collective-permute-start(f16[64,3072]{1,0:T(8,128)(2,1)S(1)} %get-tuple-element.273), channel_id=1, source_target_pairs={{0,16},{1,17},{2,18},{3,19},{4,20},{5,21},{6,22},{7,23},{8,24},{9,... | collective-permute-start | bytes 1179656 | tf_op jit(solution)/shard_map/ppermute | solution.py:35
  150.1 10.0 %collective-permute-done.30 = f16[64,3072]{1,0:T(8,128)(2,1)S(1)} collective-permute-done((f16[64,3072]{1,0:T(8,128)(2,1)S(1)}, f16[64,3072]{1,0:T(8,128)(2,1)S(1)}, u32[]{:S(2)}, u32[]{:S(2)}) %collective-permute-start.30) | collective-permute-done | bytes 393248 | tf_op jit(solution)/shard_map/ppermute | solution.py:35
  160.5 0.9 collective-permute-start.34
  161.4 5.4 %shard_map.79.refs_10_ = f32[2,512,768]{2,1,0:T(8,128)} custom-call(s32[5]{0:T(128)S(1)} %stack.23.at, bf16[528,1024]{1,0:T(8,128)(2,1)S(1)} %shard_map.71.z0.mine, bf16[528,1024]{1,0:T(8,128)(2,1)S(1)} %collective-permute-done.10.z1.up, bf16[528,1024]{1,0:T(8,128)(2,1)S(1)} %collective-permute-done.11.z3.down, ...), custom_call_target="tpu_custom_call", output_to_operand_aliasing={{}: (14, {})} | custom-call | flops 1024 | bytes 1024 | tf_op jit(solution)/shard_map/pallas_call | solution.py:47
  166.7 5.2 %collective-permute-done.34.got = f32[32,4096]{1,0:T(8,128)S(1)} collective-permute-done((f32[32,4096]{1,0:T(8,128)S(1)}, f32[32,4096]{1,0:T(8,128)S(1)}, u32[]{:S(2)}, u32[]{:S(2)}) %collective-permute-start.34) | collective-permute-done | bytes 524320 | tf_op jit(solution)/shard_map/ppermute | solution.py:35
  172.0 1.5 collective-permute-start.35
  173.5 5.4 %shard_map.81 = f32[2,512,768]{2,1,0:T(8,128)} custom-call(s32[5]{0:T(128)S(1)} %stack.23.at, bf16[528,1024]{1,0:T(8,128)(2,1)S(1)} %shard_map.71.z0.mine, bf16[528,1024]{1,0:T(8,128)(2,1)S(1)} %collective-permute-done.10.z1.up, bf16[528,1024]{1,0:T(8,128)(2,1)S(1)} %collective-permute-done.11.z3.down, ...), custom_call_target="tpu_custom_call", output_to_operand_aliasing={{}: (14, {})} | custom-call | flops 1024 | bytes 1024 | tf_op jit(solution)/shard_map/pallas_call | solution.py:47
  178.9 1.1 collective-permute-done.35.got
  180.0 1.4 shard_map.82
  (68 shorter events, 5.6 us)
Async XLA Ops:
  0.6 6.3 %collective-permute-start = (bf16[2,512,768]{2,1,0:T(8,128)(2,1)}, bf16[2,512,768]{2,1,0:T(8,128)(2,1)}, u32[]{:S(2)}, u32[]{:S(2)}) collective-permute-start(bf16[2,512,768]{2,1,0:T(8,128)(2,1)} %refs_3_), channel_id=1, source_target_pairs={{0,32},{1,33},{2,34},{3,35},{4,36},{5,37},{6,38},{7,39},{8,40},{9,... | collective-permute-start | bytes 4718600 | tf_op jit(solution)/shard_map/ppermute | solution.py:35
  0.7 6.2 %collective-permute-start.1 = (bf16[2,512,768]{2,1,0:T(8,128)(2,1)}, bf16[2,512,768]{2,1,0:T(8,128)(2,1)}, u32[]{:S(2)}, u32[]{:S(2)}) collective-permute-start(bf16[2,512,768]{2,1,0:T(8,128)(2,1)} %refs_3_.2), channel_id=1, source_target_pairs={{0,32},{1,33},{2,34},{3,35},{4,36},{5,37},{6,38},{7,39},{8,40},{9,... | collective-permute-start | bytes 4718600 | tf_op jit(solution)/shard_map/ppermute | solution.py:35
  1.2 5.7 %collective-permute-start.2 = (bf16[2,64,512]{2,1,0:T(8,128)(2,1)}, bf16[2,64,512]{2,1,0:T(8,128)(2,1)S(1)}, u32[]{:S(2)}, u32[]{:S(2)}) collective-permute-start(bf16[2,64,512]{2,1,0:T(8,128)(2,1)} %own.1), channel_id=1, source_target_pairs={{0,1},{1,0},{2,3},{3,2},{4,5},{5,4},{6,7},{7,6},{8,9},{9,8},{10,11... | collective-permute-start | bytes 393224 | tf_op jit(solution)/shard_map/ppermute | solution.py:35
  2.9 1.4 copy-start
  4.3 1.4 copy-start.2
  5.7 6.3 %copy-start.1 = (bf16[2,512,768]{2,1,0:T(8,128)(2,1)S(1)}, bf16[2,512,768]{2,1,0:T(8,128)(2,1)}, u32[]{:S(2)}) copy-start(bf16[2,512,768]{2,1,0:T(8,128)(2,1)} %refs_3_.2) | copy-start | bytes 4718596
  5.7 6.3 %copy-start.3 = (bf16[2,512,768]{2,1,0:T(8,128)(2,1)S(1)}, bf16[2,512,768]{2,1,0:T(8,128)(2,1)}, u32[]{:S(2)}) copy-start(bf16[2,512,768]{2,1,0:T(8,128)(2,1)} %refs_3_) | copy-start | bytes 4718596
  6.9 0.9 copy-start.4
  8.4 7.6 %collective-permute-start.3 = (bf16[2,2,80,128]{3,2,1,0:T(8,128)(2,1)S(1)}, bf16[2,2,80,128]{3,2,1,0:T(8,128)(2,1)S(1)}, u32[]{:S(2)}, u32[]{:S(2)}) collective-permute-start(bf16[2,2,80,128]{3,2,1,0:T(8,128)(2,1)S(1)} %get-tuple-element.142), channel_id=1, source_target_pairs={{0,32},{1,33},{2,34},{3,35},{4,36},{5,37},{6,38},{7,39},{8,40},{9,... | collective-permute-start | bytes 245768 | tf_op jit(solution)/shard_map/ppermute | solution.py:35
  8.5 7.5 %collective-permute-start.4 = (bf16[2,2,80,128]{3,2,1,0:T(8,128)(2,1)S(1)}, bf16[2,2,80,128]{3,2,1,0:T(8,128)(2,1)S(1)}, u32[]{:S(2)}, u32[]{:S(2)}) collective-permute-start(bf16[2,2,80,128]{3,2,1,0:T(8,128)(2,1)S(1)} %get-tuple-element.143), channel_id=1, source_target_pairs={{0,64},{1,65},{2,66},{3,67},{4,68},{5,69},{6,70},{7,71},{8,72},{9,... | collective-permute-start | bytes 245768 | tf_op jit(solution)/shard_map/ppermute | solution.py:35
  11.9 5.9 %collective-permute-start.5 = (bf16[2,2,80,128]{3,2,1,0:T(8,128)(2,1)S(1)}, bf16[2,2,80,128]{3,2,1,0:T(8,128)(2,1)S(1)}, u32[]{:S(2)}, u32[]{:S(2)}) collective-permute-start(bf16[2,2,80,128]{3,2,1,0:T(8,128)(2,1)S(1)} %get-tuple-element.144), channel_id=1, source_target_pairs={{0,96},{1,97},{2,98},{3,99},{4,100},{5,101},{6,102},{7,103},{8,104... | collective-permute-start | bytes 245768 | tf_op jit(solution)/shard_map/ppermute | solution.py:35
  18.5 21.1 %collective-permute-start.7 = (bf16[528,256]{1,0:T(8,128)(2,1)S(1)}, bf16[528,256]{1,0:T(8,128)(2,1)S(1)}, u32[]{:S(2)}, u32[]{:S(2)}) collective-permute-start(bf16[528,256]{1,0:T(8,128)(2,1)S(1)} %get-tuple-element.169.first), channel_id=1, source_target_pairs={{0,6},{1,7},{2,0},{3,1},{4,2},{5,3},{6,4},{7,5},{8,14},{9,15},{10,... | collective-permute-start | bytes 811016 | tf_op jit(solution)/shard_map/ppermute | solution.py:35
  21.3 18.3 %collective-permute-start.8 = (bf16[528,256]{1,0:T(8,128)(2,1)S(1)}, bf16[528,256]{1,0:T(8,128)(2,1)S(1)}, u32[]{:S(2)}, u32[]{:S(2)}) collective-permute-start(bf16[528,256]{1,0:T(8,128)(2,1)S(1)} %get-tuple-element.169.first), channel_id=1, source_target_pairs={{0,4},{1,5},{2,6},{3,7},{4,0},{5,1},{6,2},{7,3},{8,12},{9,13},{10,... | collective-permute-start | bytes 811016 | tf_op jit(solution)/shard_map/ppermute | solution.py:35
  22.1 17.5 %collective-permute-start.9 = (bf16[528,256]{1,0:T(8,128)(2,1)S(1)}, bf16[528,256]{1,0:T(8,128)(2,1)S(1)}, u32[]{:S(2)}, u32[]{:S(2)}) collective-permute-start(bf16[528,256]{1,0:T(8,128)(2,1)S(1)} %get-tuple-element.169.first), channel_id=1, source_target_pairs={{0,2},{1,3},{2,4},{3,5},{4,6},{5,7},{6,0},{7,1},{8,10},{9,11},{10,... | collective-permute-start | bytes 811016 | tf_op jit(solution)/shard_map/ppermute | solution.py:35
  24.9 14.7 %collective-permute-start.6 = (bf16[2,512,256]{2,1,0:T(8,128)(2,1)S(1)}, bf16[2,512,256]{2,1,0:T(8,128)(2,1)S(1)}, u32[]{:S(2)}, u32[]{:S(2)}) collective-permute-start(bf16[2,512,256]{2,1,0:T(8,128)(2,1)S(1)} %slice.117), channel_id=1, source_target_pairs={{0,64},{1,65},{2,66},{3,67},{4,68},{5,69},{6,70},{7,71},{8,72},{9,... | collective-permute-start | bytes 1572872 | tf_op jit(solution)/shard_map/ppermute | solution.py:35
  40.7 33.4 %collective-permute-start.10 = (bf16[528,1024]{1,0:T(8,128)(2,1)S(1)}, bf16[528,1024]{1,0:T(8,128)(2,1)S(1)}, u32[]{:S(2)}, u32[]{:S(2)}) collective-permute-start(bf16[528,1024]{1,0:T(8,128)(2,1)S(1)} %shard_map.71.z0.mine), channel_id=1, source_target_pairs={{0,24},{1,25},{2,26},{3,27},{4,28},{5,29},{6,30},{7,31},{8,0},{9,1... | collective-permute-start | bytes 3244040 | tf_op jit(solution)/shard_map/ppermute | solution.py:35
  44.8 29.3 %collective-permute-start.11 = (bf16[528,1024]{1,0:T(8,128)(2,1)S(1)}, bf16[528,1024]{1,0:T(8,128)(2,1)S(1)}, u32[]{:S(2)}, u32[]{:S(2)}) collective-permute-start(bf16[528,1024]{1,0:T(8,128)(2,1)S(1)} %shard_map.71.z0.mine), channel_id=1, source_target_pairs={{0,8},{1,9},{2,10},{3,11},{4,12},{5,13},{6,14},{7,15},{8,16},{9,17... | collective-permute-start | bytes 3244040 | tf_op jit(solution)/shard_map/ppermute | solution.py:35
  44.8 24.8 %collective-permute-start.14 = (bf16[2,512,512]{2,1,0:T(8,128)(2,1)S(1)}, bf16[2,512,512]{2,1,0:T(8,128)(2,1)S(1)}, u32[]{:S(2)}, u32[]{:S(2)}) collective-permute-start(bf16[2,512,512]{2,1,0:T(8,128)(2,1)S(1)} %slice.119), channel_id=1, source_target_pairs={{0,64},{1,65},{2,66},{3,67},{4,68},{5,69},{6,70},{7,71},{8,72},{9,... | collective-permute-start | bytes 3145736 | tf_op jit(solution)/shard_map/ppermute | solution.py:35
  49.5 24.2 %collective-permute-start.12 = (f16[256,2048]{1,0:T(8,128)(2,1)S(1)}, f16[256,2048]{1,0:T(8,128)(2,1)S(1)}, u32[]{:S(2)}, u32[]{:S(2)}) collective-permute-start(f16[256,2048]{1,0:T(8,128)(2,1)S(1)} %fusion), channel_id=1, source_target_pairs={{0,2},{1,3},{2,4},{3,5},{4,6},{5,7},{6,0},{7,1},{8,10},{9,11},{10,... | collective-permute-start | bytes 3145736 | tf_op jit(solution)/shard_map/ppermute | solution.py:35
  51.3 22.8 %collective-permute-start.13 = (f16[256,2048]{1,0:T(8,128)(2,1)S(1)}, f16[256,2048]{1,0:T(8,128)(2,1)S(1)}, u32[]{:S(2)}, u32[]{:S(2)}) collective-permute-start(f16[256,2048]{1,0:T(8,128)(2,1)S(1)} %fusion.1), channel_id=1, source_target_pairs={{0,6},{1,7},{2,0},{3,1},{4,2},{5,3},{6,4},{7,5},{8,14},{9,15},{10,... | collective-permute-start | bytes 3145736 | tf_op jit(solution)/shard_map/ppermute | solution.py:35
  69.6 11.6 %collective-permute-start.20 = (bf16[2,512,512]{2,1,0:T(8,128)(2,1)S(1)}, bf16[2,512,512]{2,1,0:T(8,128)(2,1)S(1)}, u32[]{:S(2)}, u32[]{:S(2)}) collective-permute-start(bf16[2,512,512]{2,1,0:T(8,128)(2,1)S(1)} %collective-permute-done.14.refs_1_.refs_7_), channel_id=1, source_target_pairs={{0,32},{1,33},{2,34},{3,35},{4,36},{5,37},{6,38},{7,39},{8,40},{9,... | collective-permute-start | bytes 3145736 | tf_op jit(solution)/shard_map/ppermute | solution.py:35
  74.1 5.5 %collective-permute-start.19 = (bf16[2,512,256]{2,1,0:T(8,128)(2,1)S(1)}, bf16[2,512,256]{2,1,0:T(8,128)(2,1)S(1)}, u32[]{:S(2)}, u32[]{:S(2)}) collective-permute-start(bf16[2,512,256]{2,1,0:T(8,128)(2,1)S(1)} %collective-permute-done.6.refs_0_.refs_6_), channel_id=1, source_target_pairs={{0,32},{1,33},{2,34},{3,35},{4,36},{5,37},{6,38},{7,39},{8,40},{9,... | collective-permute-start | bytes 1572872 | tf_op jit(solution)/shard_map/ppermute | solution.py:35
  74.2 29.4 %collective-permute-start.17 = (bf16[528,512]{1,0:T(8,128)(2,1)S(1)}, bf16[528,512]{1,0:T(8,128)(2,1)S(1)}, u32[]{:S(2)}, u32[]{:S(2)}) collective-permute-start(bf16[528,512]{1,0:T(8,128)(2,1)S(1)} %slice.120), channel_id=1, source_target_pairs={{0,8},{1,9},{2,10},{3,11},{4,12},{5,13},{6,14},{7,15},{8,16},{9,17... | collective-permute-start | bytes 1622024 | tf_op jit(solution)/shard_map/ppermute | solution.py:35
  74.3 29.3 %collective-permute-start.18 = (bf16[528,512]{1,0:T(8,128)(2,1)S(1)}, bf16[528,512]{1,0:T(8,128)(2,1)S(1)}, u32[]{:S(2)}, u32[]{:S(2)}) collective-permute-start(bf16[528,512]{1,0:T(8,128)(2,1)S(1)} %slice.121), channel_id=1, source_target_pairs={{0,24},{1,25},{2,26},{3,27},{4,28},{5,29},{6,30},{7,31},{8,0},{9,1... | collective-permute-start | bytes 1622024 | tf_op jit(solution)/shard_map/ppermute | solution.py:35
  77.6 26.7 %collective-permute-start.16 = (f16[256,2048]{1,0:T(8,128)(2,1)}, f16[256,2048]{1,0:T(8,128)(2,1)S(1)}, u32[]{:S(2)}, u32[]{:S(2)}) collective-permute-start(f16[256,2048]{1,0:T(8,128)(2,1)} %fusion.2), channel_id=1, source_target_pairs={{0,4},{1,5},{2,6},{3,7},{4,0},{5,1},{6,2},{7,3},{8,12},{9,13},{10,... | collective-permute-start | bytes 3145736 | tf_op jit(solution)/shard_map/ppermute | solution.py:35
  79.6 37.5 %collective-permute-start.15 = (bf16[2,512,768]{2,1,0:T(8,128)(2,1)S(1)}, bf16[2,512,768]{2,1,0:T(8,128)(2,1)S(1)}, u32[]{:S(2)}, u32[]{:S(2)}) collective-permute-start(bf16[2,512,768]{2,1,0:T(8,128)(2,1)S(1)} %copy-done.1), channel_id=1, source_target_pairs={{0,64},{1,65},{2,66},{3,67},{4,68},{5,69},{6,70},{7,71},{8,72},{9,... | collective-permute-start | bytes 4718600 | tf_op jit(solution)/shard_map/ppermute | solution.py:35
  83.2 21.1 %collective-permute-start.21 = (f16[256,1024]{1,0:T(8,128)(2,1)S(1)}, f16[256,1024]{1,0:T(8,128)(2,1)S(1)}, u32[]{:S(2)}, u32[]{:S(2)}) collective-permute-start(f16[256,1024]{1,0:T(8,128)(2,1)S(1)} %fusion.48), channel_id=1, source_target_pairs={{0,16},{1,17},{2,18},{3,19},{4,20},{5,21},{6,22},{7,23},{8,24},{9,... | collective-permute-start | bytes 1572872 | tf_op jit(solution)/shard_map/ppermute | solution.py:35
  104.3 12.8 %copy-start.5 = (f16[256,1024]{1,0:T(8,128)(2,1)}, f16[256,1024]{1,0:T(8,128)(2,1)S(1)}, u32[]{:S(2)}) copy-start(f16[256,1024]{1,0:T(8,128)(2,1)S(1)} %collective-permute-done.21) | copy-start | bytes 1572868
  104.3 24.1 %collective-permute-start.22 = (f16[256,1024]{1,0:T(8,128)(2,1)}, f16[256,1024]{1,0:T(8,128)(2,1)}, u32[]{:S(2)}, u32[]{:S(2)}) collective-permute-start(f16[256,1024]{1,0:T(8,128)(2,1)} %fusion.45), channel_id=1, source_target_pairs={{0,8},{1,9},{2,10},{3,11},{4,12},{5,13},{6,14},{7,15},{8,16},{9,17... | collective-permute-start | bytes 1572872 | tf_op jit(solution)/shard_map/ppermute | solution.py:35
  105.0 23.4 %collective-permute-start.23 = (f16[256,1024]{1,0:T(8,128)(2,1)}, f16[256,1024]{1,0:T(8,128)(2,1)}, u32[]{:S(2)}, u32[]{:S(2)}) collective-permute-start(f16[256,1024]{1,0:T(8,128)(2,1)} %fusion.42), channel_id=1, source_target_pairs={{0,24},{1,25},{2,26},{3,27},{4,28},{5,29},{6,30},{7,31},{8,0},{9,1... | collective-permute-start | bytes 1572872 | tf_op jit(solution)/shard_map/ppermute | solution.py:35
  107.5 20.9 %collective-permute-start.24 = (f16[256,1024]{1,0:T(8,128)(2,1)}, f16[256,1024]{1,0:T(8,128)(2,1)}, u32[]{:S(2)}, u32[]{:S(2)}) collective-permute-start(f16[256,1024]{1,0:T(8,128)(2,1)} %fusion.39), channel_id=1, source_target_pairs={{0,2},{1,3},{2,4},{3,5},{4,6},{5,7},{6,0},{7,1},{8,10},{9,11},{10,... | collective-permute-start | bytes 1572872 | tf_op jit(solution)/shard_map/ppermute | solution.py:35
  108.4 23.6 %collective-permute-start.25 = (f16[256,1024]{1,0:T(8,128)(2,1)}, f16[256,1024]{1,0:T(8,128)(2,1)}, u32[]{:S(2)}, u32[]{:S(2)}) collective-permute-start(f16[256,1024]{1,0:T(8,128)(2,1)} %fusion.36), channel_id=1, source_target_pairs={{0,6},{1,7},{2,0},{3,1},{4,2},{5,3},{6,4},{7,5},{8,14},{9,15},{10,... | collective-permute-start | bytes 1572872 | tf_op jit(solution)/shard_map/ppermute | solution.py:35
  117.1 16.5 %collective-permute-start.26 = (f16[256,1024]{1,0:T(8,128)(2,1)}, f16[256,1024]{1,0:T(8,128)(2,1)}, u32[]{:S(2)}, u32[]{:S(2)}) collective-permute-start(f16[256,1024]{1,0:T(8,128)(2,1)} %fusion.33), channel_id=1, source_target_pairs={{0,4},{1,5},{2,6},{3,7},{4,0},{5,1},{6,2},{7,3},{8,12},{9,13},{10,... | collective-permute-start | bytes 1572872 | tf_op jit(solution)/shard_map/ppermute | solution.py:35
  126.6 7.0 %copy-start.6 = (f16[256,1024]{1,0:T(8,128)(2,1)S(1)}, f16[256,1024]{1,0:T(8,128)(2,1)}, u32[]{:S(2)}) copy-start(f16[256,1024]{1,0:T(8,128)(2,1)} %copy-done.5) | copy-start | bytes 1572868
  135.3 10.5 %collective-permute-start.27 = (f32[64,1024]{1,0:T(8,128)S(1)}, f32[64,1024]{1,0:T(8,128)S(1)}, u32[]{:S(2)}, u32[]{:S(2)}) collective-permute-start(f32[64,1024]{1,0:T(8,128)S(1)} %get-tuple-element.276), channel_id=1, source_target_pairs={{0,2},{1,3},{2,4},{3,5},{4,6},{5,7},{6,0},{7,1},{8,10},{9,11},{10,... | collective-permute-start | bytes 786440 | tf_op jit(solution)/shard_map/ppermute | solution.py:35
  136.5 13.5 %collective-permute-start.28 = (f32[64,1024]{1,0:T(8,128)S(1)}, f32[64,1024]{1,0:T(8,128)S(1)}, u32[]{:S(2)}, u32[]{:S(2)}) collective-permute-start(f32[64,1024]{1,0:T(8,128)S(1)} %get-tuple-element.278), channel_id=1, source_target_pairs={{0,6},{1,7},{2,0},{3,1},{4,2},{5,3},{6,4},{7,5},{8,14},{9,15},{10,... | collective-permute-start | bytes 786440 | tf_op jit(solution)/shard_map/ppermute | solution.py:35
  138.6 11.4 %collective-permute-start.29 = (f32[64,1024]{1,0:T(8,128)S(1)}, f32[64,1024]{1,0:T(8,128)S(1)}, u32[]{:S(2)}, u32[]{:S(2)}) collective-permute-start(f32[64,1024]{1,0:T(8,128)S(1)} %get-tuple-element.277), channel_id=1, source_target_pairs={{0,4},{1,5},{2,6},{3,7},{4,0},{5,1},{6,2},{7,3},{8,12},{9,13},{10,... | collective-permute-start | bytes 786440 | tf_op jit(solution)/shard_map/ppermute | solution.py:35
  141.7 18.4 %collective-permute-start.30 = (f16[64,3072]{1,0:T(8,128)(2,1)S(1)}, f16[64,3072]{1,0:T(8,128)(2,1)S(1)}, u32[]{:S(2)}, u32[]{:S(2)}) collective-permute-start(f16[64,3072]{1,0:T(8,128)(2,1)S(1)} %get-tuple-element.272), channel_id=1, source_target_pairs={{0,8},{1,9},{2,10},{3,11},{4,12},{5,13},{6,14},{7,15},{8,16},{9,17... | collective-permute-start | bytes 1179656 | tf_op jit(solution)/shard_map/ppermute | solution.py:35
  141.8 18.3 %collective-permute-start.31 = (f16[64,3072]{1,0:T(8,128)(2,1)S(1)}, f16[64,3072]{1,0:T(8,128)(2,1)S(1)}, u32[]{:S(2)}, u32[]{:S(2)}) collective-permute-start(f16[64,3072]{1,0:T(8,128)(2,1)S(1)} %get-tuple-element.274), channel_id=1, source_target_pairs={{0,24},{1,25},{2,26},{3,27},{4,28},{5,29},{6,30},{7,31},{8,0},{9,1... | collective-permute-start | bytes 1179656 | tf_op jit(solution)/shard_map/ppermute | solution.py:35
  145.7 14.4 %collective-permute-start.32 = (f16[64,3072]{1,0:T(8,128)(2,1)S(1)}, f16[64,3072]{1,0:T(8,128)(2,1)S(1)}, u32[]{:S(2)}, u32[]{:S(2)}) collective-permute-start(f16[64,3072]{1,0:T(8,128)(2,1)S(1)} %get-tuple-element.273), channel_id=1, source_target_pairs={{0,16},{1,17},{2,18},{3,19},{4,20},{5,21},{6,22},{7,23},{8,24},{9,... | collective-permute-start | bytes 1179656 | tf_op jit(solution)/shard_map/ppermute | solution.py:35
  150.0 11.3 %collective-permute-start.33 = (bf16[2,512,768]{2,1,0:T(8,128)(2,1)S(1)}, bf16[2,512,768]{2,1,0:T(8,128)(2,1)S(1)}, u32[]{:S(2)}, u32[]{:S(2)}) collective-permute-start(bf16[2,512,768]{2,1,0:T(8,128)(2,1)S(1)} %collective-permute-done.15.refs_6_.refs_7_), channel_id=1, source_target_pairs={{0,32},{1,33},{2,34},{3,35},{4,36},{5,37},{6,38},{7,39},{8,40},{9,... | collective-permute-start | bytes 4718600 | tf_op jit(solution)/shard_map/ppermute | solution.py:35
  160.5 11.5 %collective-permute-start.34 = (f32[32,4096]{1,0:T(8,128)S(1)}, f32[32,4096]{1,0:T(8,128)S(1)}, u32[]{:S(2)}, u32[]{:S(2)}) collective-permute-start(f32[32,4096]{1,0:T(8,128)S(1)} %get-tuple-element.253), channel_id=1, source_target_pairs={{0,1},{1,0},{2,3},{3,2},{4,5},{5,4},{6,7},{7,6},{8,9},{9,8},{10,11... | collective-permute-start | bytes 1572872 | tf_op jit(solution)/shard_map/ppermute | solution.py:35
  172.0 8.0 %collective-permute-start.35 = (f32[32,2048]{1,0:T(8,128)S(1)}, f32[32,2048]{1,0:T(8,128)S(1)}, u32[]{:S(2)}, u32[]{:S(2)}) collective-permute-start(f32[32,2048]{1,0:T(8,128)S(1)} %get-tuple-element.262), channel_id=1, source_target_pairs={{0,64},{1,65},{2,66},{3,67},{4,68},{5,69},{6,70},{7,71},{8,72},{9,... | collective-permute-start | bytes 786440 | tf_op jit(solution)/shard_map/ppermute | solution.py:35
